TPU v7x, 32 devices: a whole 2x2x4 slice. The times are simulated.
32 devices in a mesh: ctx: 8 (over z, y), tp: 4 (over x, core).
Axes of the slice: x: 2, y: 2, z: 4, core: 2. Of those that a mesh axis runs over, the one named last changes fastest.
Arguments:
- values_in: bfloat16 [2048, 8192], P('ctx', 'tp'), may hold values from -6 to 6
- gate_in: bfloat16 [2048, 8192], P('ctx', 'tp'), may hold values from -6 to 6
- keys_in: bfloat16 [2048, 1024], P('ctx', 'tp'), may hold values from -3 to 3
- queries_in: bfloat16 [2048, 1024], P('ctx', 'tp'), may hold values from -3 to 3
- step_in: bfloat16 [2048, 128], P('ctx', 'tp'), may hold values from -4 to 4
- block_order: int32 [32], replicated, may hold values from 0 to 31, as said below
- doc_lengths: int32 [16], replicated, may hold values from 1 to 1024, 2048 in all
- conv_values: float32 [4, 8192], P(None, 'tp'), may hold values from -3 to 3
- conv_keys: float32 [4, 1024], P(None, 'tp'), may hold values from -3 to 3
- conv_queries: float32 [4, 1024], P(None, 'tp'), may hold values from -3 to 3
- decay_log: float32 [128], P('tp'), may hold values from -7 to 0, as said below
- step_bias: float32 [128], P('tp'), may hold values from -9 to -2, as said below
- skip_gain: float32 [128], P('tp'), may hold values from 0.5 to 2
- norm_gain: float32 [8192], P('tp'), may hold values from 0.25 to 1.75
- out_weight: bfloat16 [8192, 4096], P('tp'), may hold values from -0.0625 to 0.0625
Outputs:
- layer_out: bfloat16 [2048, 4096], P(('ctx', 'tp'))
Inputs may be any that keep to these rules, and one draw needn't show every extreme that they name: `block_order`: loaded block j sits on loader j // 4; sequence block q belongs to owner q // 4; every block appears once; the 4 blocks of each loader belong to 4 different owners. `doc_lengths`: document lengths in sequence order; they sum to 2048 and the longest is exactly 1024. `decay_log`: logarithm of each head's decay coefficient. `step_bias`: bias added to each head's time-step pre-activation.
All inputs are finite; a program needn't handle non-finite values.
Results may differ from a plain program's by a relative error of at most 0.02.
Values may be sent and summed in bfloat16 or wider, within the bound.
No kernel may reach another device: no remote copies, remote signals or barrier semaphores. Data moves between devices by JAX's collectives and lax.ppermute only.
A program may use at most 128 MiB of HBM per device.

v0:
```python
import jax
import jax.numpy as jnp
from jax import lax
from jax.sharding import PartitionSpec as P

HEAD_DIM = 64
STATE = 128
CONV = 4
SPAN = 256
BLK = 64


def shifted_2(value, axis, steps):
    count = lax.axis_size(axis)
    leading, last = (max(0, -steps), min(count, count - steps))
    return lax.ppermute(value, axis, [(source, source + steps) for source in range(leading, last)])


def carried_in(shard, axis, join, neutral):
    place = lax.axis_index(axis)
    gathered = jax.tree.map(
        lambda a, kind: lax.all_gather(a.astype(kind), axis),
        shard,
        jax.tree.map(lambda a: jnp.bfloat16 if a.dtype == jnp.float32 else a.dtype, shard),
    )
    state = jax.tree.map(lambda a, e: jnp.zeros_like(a) + jnp.asarray(e, a.dtype), shard, neutral)

    def one(turn, state):
        return join(
            state,
            jax.tree.map(
                lambda a, own: lax.dynamic_index_in_dim(a, turn, 0, False).astype(own.dtype),
                gathered,
                shard,
            ),
        )

    return lax.fori_loop(0, place, one, state)


def document_index(positions, doc_lengths):
    offsets = jnp.cumsum(doc_lengths) - doc_lengths
    below_start = offsets[None, :] <= positions[:, None]
    documents = jnp.sum(below_start.astype(jnp.int32), axis=1, dtype=jnp.int32) - 1
    openings = jnp.any(offsets[None, :] == positions[:, None], axis=1).astype(jnp.int32)
    return (documents, openings)


def causal_conv(extended, weight, doc_ext):
    tap_count = weight.shape[0]
    row_count = extended.shape[0] - tap_count + 1
    current = doc_ext[tap_count - 1 :]
    accumulated = jnp.zeros((row_count, extended.shape[1]), jnp.float32)
    for tap_index in range(tap_count):
        keep_rows = (doc_ext[tap_index : tap_index + row_count] == current)[:, None]
        shifted = (
            extended[tap_index : tap_index + row_count].astype(jnp.float32) * weight[tap_index]
        )
        accumulated = accumulated + jnp.where(keep_rows, shifted, 0.0)
    return lax.optimization_barrier(jax.nn.silu(accumulated).astype(jnp.bfloat16))


def span_outputs(value_rows, step_rows, key_rows, query_rows, decay_sums, documents):
    row_count = value_rows.shape[0]
    per_group = value_rows.shape[1] // key_rows.shape[1]
    row_ids = jnp.arange(row_count, dtype=jnp.int32)
    keep_mask = (documents[:, None] == documents[None, :]) & (row_ids[None, :] <= row_ids[:, None])
    differences = decay_sums[:, :, None] - decay_sums[:, None, :]
    decays = jnp.where(keep_mask[None], jnp.exp(jnp.minimum(differences, 0.0)), 0.0)
    inner_products = jnp.einsum(
        "ign,jgn->gij", query_rows, key_rows, preferred_element_type=jnp.float32
    )
    weighted = (
        decays * jnp.repeat(inner_products, per_group, axis=0) * step_rows.T[:, None, :]
    ).astype(jnp.bfloat16)
    return jnp.einsum("hij,jhp->ihp", weighted, value_rows, preferred_element_type=jnp.float32)


def span_states(value_rows, step_rows, key_rows, decay_sums, documents, openings):
    per_group = value_rows.shape[1] // key_rows.shape[1]
    tail_decay = jnp.where(
        (documents == documents[-1])[None, :], jnp.exp(decay_sums[:, -1:] - decay_sums), 0.0
    )
    tail_weight = tail_decay.T * step_rows
    head_keys = jnp.repeat(key_rows, per_group, axis=1)
    tail_keys = (tail_weight[:, :, None] * head_keys.astype(jnp.float32)).astype(jnp.bfloat16)
    local_state = jnp.einsum(
        "jhp,jhn->hpn", value_rows, tail_keys, preferred_element_type=jnp.float32
    )
    opened = jnp.cumsum(openings)
    span_gate = jnp.where(opened[-1] == 0, jnp.exp(decay_sums[:, -1]), 0.0)
    inflow = jnp.where((opened == 0)[None, :], jnp.exp(decay_sums), 0.0)
    return (local_state, span_gate, inflow)


def span_inflow(query_rows, entering, inflow):
    per_group = entering.shape[0] // query_rows.shape[1]
    head_queries = jnp.repeat(query_rows.astype(jnp.float32), per_group, axis=1)
    carried = jnp.einsum("ihn,hpn->ihp", head_queries, entering, precision=lax.Precision.HIGHEST)
    return carried * inflow.T[:, :, None]


def gated_norm(mixed_rows, gate_rows, norm_gain, groups_local):
    gated_rows = mixed_rows * jax.nn.silu(gate_rows.astype(jnp.float32))
    grouped = gated_rows.reshape(gated_rows.shape[0], groups_local, -1)
    inverse_rms = lax.rsqrt(jnp.mean(grouped * grouped, axis=2, keepdims=True) + 1e-05)
    return ((grouped * inverse_rms).reshape(gated_rows.shape) * norm_gain).astype(jnp.bfloat16)


def on_device(
    values_in,
    gate_in,
    keys_in,
    queries_in,
    step_in,
    block_order,
    doc_lengths,
    conv_values,
    conv_keys,
    conv_queries,
    decay_log,
    step_bias,
    skip_gain,
    norm_gain,
    out_weight,
):
    ctx_count = lax.axis_size("ctx")
    ctx_index = lax.axis_index("ctx")
    token_count = values_in.shape[0]
    per_dev = token_count // BLK
    capacity = (per_dev + ctx_count - 1) // ctx_count
    rim_rows = CONV - 1
    pos_table = block_order.reshape(ctx_count, per_dev)
    owner_of = pos_table // per_dev
    local_ids = jnp.arange(per_dev, dtype=jnp.int32)
    earlier = local_ids[None, :] < local_ids[:, None]
    same_owner = owner_of[:, :, None] == owner_of[:, None, :]
    slot_rank = jnp.sum((same_owner & earlier[None]).astype(jnp.int32), axis=2, dtype=jnp.int32)
    my_owner = lax.dynamic_index_in_dim(owner_of, ctx_index, 0, keepdims=False)
    my_rank = lax.dynamic_index_in_dim(slot_rank, ctx_index, 0, keepdims=False)
    slot_ids = jnp.arange(ctx_count * capacity, dtype=jnp.int32)
    slot_hit = (my_owner * capacity + my_rank)[None, :] == slot_ids[:, None]
    source = jnp.sum(jnp.where(slot_hit, local_ids[None, :], 0), axis=1, dtype=jnp.int32)
    filled = jnp.any(slot_hit, axis=1)

    def pack_slots(local_rows):
        blocks = local_rows.reshape(per_dev, BLK, local_rows.shape[1])
        picked = jnp.where(filled[:, None, None], blocks[source], jnp.zeros((), local_rows.dtype))
        return picked

    all_slots = (jnp.arange(ctx_count, dtype=jnp.int32)[:, None] * capacity + slot_rank).reshape(-1)
    wanted = ctx_index * per_dev + local_ids
    owner_hit = block_order[None, :] == wanted[:, None]
    pick_slot = jnp.sum(jnp.where(owner_hit, all_slots[None, :], 0), axis=1, dtype=jnp.int32)

    def unpack_slots(received):
        return received[pick_slot].reshape(token_count, received.shape[2])

    packed_values = pack_slots(values_in)
    packed_gates = pack_slots(gate_in)
    packed_keys = pack_slots(keys_in)
    packed_queries = pack_slots(queries_in)
    packed_steps = pack_slots(step_in)
    received = (
        lax.all_to_all(packed_values, "ctx", split_axis=0, concat_axis=0, tiled=True),
        lax.all_to_all(packed_gates, "ctx", split_axis=0, concat_axis=0, tiled=True),
        lax.all_to_all(packed_keys, "ctx", split_axis=0, concat_axis=0, tiled=True),
        lax.all_to_all(packed_queries, "ctx", split_axis=0, concat_axis=0, tiled=True),
        lax.all_to_all(packed_steps, "ctx", split_axis=0, concat_axis=0, tiled=True),
    )
    own_values = unpack_slots(received[0])
    own_gates = unpack_slots(received[1])
    own_keys = unpack_slots(received[2])
    own_queries = unpack_slots(received[3])
    own_steps = unpack_slots(received[4])
    rim_values, rim_keys, rim_queries = shifted_2(
        (
            own_values[token_count - rim_rows :],
            own_keys[token_count - rim_rows :],
            own_queries[token_count - rim_rows :],
        ),
        "ctx",
        1,
    )
    positions = (
        ctx_index * token_count - rim_rows + jnp.arange(token_count + rim_rows, dtype=jnp.int32)
    )
    doc_ext, open_ext = document_index(positions, doc_lengths)
    documents = doc_ext[rim_rows:]
    openings = open_ext[rim_rows:]
    conv_value = causal_conv(
        jnp.concatenate([rim_values, own_values], axis=0), conv_values, doc_ext
    )
    conv_key = causal_conv(jnp.concatenate([rim_keys, own_keys], axis=0), conv_keys, doc_ext)
    conv_query = causal_conv(
        jnp.concatenate([rim_queries, own_queries], axis=0), conv_queries, doc_ext
    )
    heads_local = own_steps.shape[1]
    groups_local = own_keys.shape[1] // STATE
    span_count = token_count // SPAN
    step_size = jax.nn.softplus(own_steps.astype(jnp.float32) + step_bias)
    rates = -jnp.exp(decay_log) * step_size
    value_rows = conv_value.reshape(span_count, SPAN, heads_local, HEAD_DIM)
    key_rows = conv_key.reshape(span_count, SPAN, groups_local, STATE)
    query_rows = conv_query.reshape(span_count, SPAN, groups_local, STATE)
    step_spans = step_size.reshape(span_count, SPAN, heads_local)
    decay_sums = jnp.cumsum(rates.reshape(span_count, SPAN, heads_local).transpose(0, 2, 1), axis=2)
    span_docs = documents.reshape(span_count, SPAN)
    span_openings = openings.reshape(span_count, SPAN)
    intra = jax.vmap(span_outputs)(
        value_rows, step_spans, key_rows, query_rows, decay_sums, span_docs
    )
    local_states, span_gates, inflows = jax.vmap(span_states)(
        value_rows, step_spans, key_rows, decay_sums, span_docs, span_openings
    )

    def advance(running, inputs):
        decay_product, accumulated = running
        span_state, span_gate = inputs
        advanced = (span_gate * decay_product, span_gate[:, None, None] * accumulated + span_state)
        return (advanced, running)

    start_carry = (
        jnp.ones((heads_local,), jnp.float32),
        jnp.zeros((heads_local, HEAD_DIM, STATE), jnp.float32),
    )
    summary, prefixes = lax.scan(advance, start_carry, (local_states, span_gates))

    def combine(earlier_part, later_part):
        return (
            earlier_part[0] * later_part[0],
            later_part[0][:, None, None] * earlier_part[1] + later_part[1],
        )

    incoming = carried_in(summary, "ctx", combine, start_carry)
    entering = prefixes[0][:, :, None, None] * incoming[1][None] + prefixes[1]
    entering, inflows = (entering, inflows)
    inter = jax.vmap(span_inflow)(query_rows, entering, inflows)
    mixed_rows = intra + inter + skip_gain[None, None, :, None] * value_rows.astype(jnp.float32)
    mixed_rows = mixed_rows.reshape(token_count, heads_local * HEAD_DIM)
    normed = gated_norm(mixed_rows, own_gates, norm_gain, groups_local)
    return lax.psum_scatter(
        jnp.dot(normed, out_weight, preferred_element_type=jnp.float32).astype(jnp.bfloat16),
        "tp",
        scatter_dimension=0,
        tiled=True,
    )


def solution(mesh):
    in_specs = (
        P("ctx", "tp"),
        P("ctx", "tp"),
        P("ctx", "tp"),
        P("ctx", "tp"),
        P("ctx", "tp"),
        P(),
        P(),
        P(None, "tp"),
        P(None, "tp"),
        P(None, "tp"),
        P("tp"),
        P("tp"),
        P("tp"),
        P("tp"),
        P("tp", None),
    )
    out_specs = P(("ctx", "tp"), None)
    return jax.shard_map(
        on_device, mesh=mesh, in_specs=in_specs, out_specs=out_specs, check_vma=False
    )
```

profile of v0, /device:TPU:16, one launch (start us, length us, event | category | flops | bytes accessed | tf_op | source)
XLA Modules:
  0.0 318.5 jit_solution(12213087876811859005)
XLA Ops:
  6.5 0.8 reshape.792
  7.9 0.8 reshape.796
  9.4 0.7 reshape.914
  10.1 6.2 %all-to-all-start.1 = ((bf16[8,2,1024]{2,1,0:T(2,128)(2,1)}), bf16[8,2,1024]{2,1,0:T(2,128)(2,1)S(1)}, u32[]{:S(2)}, u32[]{:S(2)}) async-start(bf16[8,2,1024]{2,1,0:T(2,128)(2,1)} %reshape.914), calls=%async_computation.1 | async-start | bytes 65536 | tf_op jit(solution)/shard_map/all_to_all | solution.py:169
  16.3 0.7 copy.105
  18.3 1.5 gather_fusion.6
  19.8 1.5 gather_fusion.4
  21.3 0.8 broadcast_select_fusion.2
  22.5 0.7 gather_fusion.8
  23.2 3.2 %gather_fusion = bf16[8,64,2048]{2,1,0:T(8,128)(2,1)} fusion(bf16[4,64,2048]{2,1,0:T(8,128)(2,1)} %bitcast.167, s32[1024]{0:T(1024)S(1)} %pad_clamp_fusion.1), kind=kCustom, calls=%fused_computation | custom fusion | bytes 4194336 | tf_op jit(solution)/shard_map/gather | solution.py:148
  26.4 6.0 %all-to-all-start.3 = ((bf16[8,64,256]{2,1,0:T(8,128)(2,1)}), bf16[8,64,256]{2,1,0:T(8,128)(2,1)S(1)}, u32[]{:S(2)}, u32[]{:S(2)}) async-start(bf16[8,64,256]{2,1,0:T(8,128)(2,1)} %get-tuple-element.108), calls=%async_computation.3 | async-start | bytes 524288 | tf_op jit(solution)/shard_map/all_to_all | solution.py:167
  32.4 3.9 %broadcast_select_fusion = (bf16[8,64,2048]{2,1,0:T(8,128)(2,1)}, bf16[8,64,2048]{2,1,0:T(8,128)(2,1)}) fusion(bf16[8,64,2048]{2,1,0:T(8,128)(2,1)S(1)} %gather_fusion.8, pred[8]{0:T(512)(128)(4,1)S(1)} %fusion.22, bf16[8,64,2048]{2,1,0:T(8,128)(2,1)} %gather_fusion), kind=kLoop, calls=%fused_computation.32 | loop fusion | flops 2097152 | bytes 8388616 | tf_op jit(solution)/shard_map/jit(_where)/select_n | solution.py:148
  36.3 2.6 all-to-all-done.3
  38.9 5.7 %all-to-all-start = ((bf16[8,64,2048]{2,1,0:T(8,128)(2,1)}), bf16[8,64,2048]{2,1,0:T(8,128)(2,1)S(1)}, u32[]{:S(2)}, u32[]{:S(2)}) async-start(bf16[8,64,2048]{2,1,0:T(8,128)(2,1)} %get-tuple-element.107), calls=%async_computation | async-start | bytes 4194304 | tf_op jit(solution)/shard_map/all_to_all | solution.py:165
  48.6 1.3 broadcast_compare_fusion
  53.9 0.7 fusion.20
  55.7 3.4 %collective-permute-start.2 = (bf16[3,256]{1,0:T(4,128)(2,1)}, bf16[3,256]{1,0:T(4,128)(2,1)}, u32[]{:S(2)}, u32[]{:S(2)}) collective-permute-start(bf16[3,256]{1,0:T(4,128)(2,1)} %slice.189), channel_id=1, source_target_pairs={{0,4},{4,8},{8,12},{12,16},{16,20},{20,24},{24,28},{1,5},{5,9},{9,... | collective-permute-start | bytes 4616 | tf_op jit(solution)/shard_map/ppermute | solution.py:16
  59.7 29.3 %all-to-all-done = bf16[8,64,2048]{2,1,0:T(8,128)(2,1)S(1)} async-done(((bf16[8,64,2048]{2,1,0:T(8,128)(2,1)}), bf16[8,64,2048]{2,1,0:T(8,128)(2,1)S(1)}, u32[]{:S(2)}, u32[]{:S(2)}) %all-to-all-start) | async-done | bytes 2097184 | tf_op jit(solution)/shard_map/all_to_all | solution.py:165
  89.0 0.7 gather_fusion.1
  89.8 3.5 %collective-permute-start = (bf16[3,2048]{1,0:T(4,128)(2,1)S(1)}, bf16[3,2048]{1,0:T(4,128)(2,1)S(1)}, u32[]{:S(2)}, u32[]{:S(2)}) collective-permute-start(bf16[3,2048]{1,0:T(4,128)(2,1)S(1)} %slice.178), channel_id=1, source_target_pairs={{0,4},{4,8},{8,12},{12,16},{16,20},{20,24},{24,28},{1,5},{5,9},{9,... | collective-permute-start | bytes 36872 | tf_op jit(solution)/shard_map/ppermute | solution.py:16
  93.3 1.0 multiply_convert_fusion.1
  94.6 3.0 fusion.2
  97.6 4.5 %multiply_convert_fusion = bf16[256,2048]{1,0:T(8,128)(2,1)S(1)} fusion(bf16[256,2048]{1,0:T(8,128)(2,1)} %bitcast.166, bf16[3,2048]{1,0:T(4,128)(2,1)S(1)} %collective-permute-done, f32[2048]{0:T(1024)S(1)} %bitcast.185, f32[2048]{0:T(1024)S(1)} %bitcast.186, f32[2048]{0:T(1024)S(1)} %bitcast.184, f32[2048]{0:T(1024)S(1)} %bitcast.183, ...), kind=kLoop, calls=%fused_computation.30 | loop fusion | flops 14680064 | bytes 2142976 | tf_op jit(solution)/shard_map/convert_element_type | solution.py:60
  102.7 2.9 fusion.12
  105.6 15.9 %all_to_all.25 = bf16[8,64,256]{2,1,0:T(8,128)(2,1)S(1)} all-to-all(bf16[8,64,256]{2,1,0:T(8,128)(2,1)S(1)} %get-tuple-element.109), channel_id=1, replica_groups=mesh['ctx'=8,'tp'=4] {'ctx'}, dimensions={0} | all-to-all | bytes 524288 | tf_op jit(solution)/shard_map/all_to_all | solution.py:168
  121.5 7.2 %all-to-all-start.4 = ((bf16[8,64,2048]{2,1,0:T(8,128)(2,1)}), bf16[8,64,2048]{2,1,0:T(8,128)(2,1)}, u32[]{:S(2)}, u32[]{:S(2)}) async-start(bf16[8,64,2048]{2,1,0:T(8,128)(2,1)} %get-tuple-element.106), calls=%async_computation.4 | async-start | bytes 4194304 | tf_op jit(solution)/shard_map/all_to_all | solution.py:166
  128.9 0.7 gather_fusion.5
  129.6 3.4 %collective-permute-start.1 = (bf16[3,256]{1,0:T(4,128)(2,1)S(1)}, bf16[3,256]{1,0:T(4,128)(2,1)S(1)}, u32[]{:S(2)}, u32[]{:S(2)}) collective-permute-start(bf16[3,256]{1,0:T(4,128)(2,1)S(1)} %slice.184), channel_id=1, source_target_pairs={{0,4},{4,8},{8,12},{12,16},{16,20},{20,24},{24,28},{1,5},{5,9},{9,... | collective-permute-start | bytes 4616 | tf_op jit(solution)/shard_map/ppermute | solution.py:16
  133.2 87.8 %all-gather = bf16[8,32,1]{1,2,0:T(2,128)(2,1)S(1)} all-gather(bf16[1,32,1]{1,2,0:T(2,128)(2,1)S(1)} %copy.123), channel_id=2, replica_groups=mesh['ctx'=8,'tp'=4] {'ctx'}, dimensions={0}, use_global_device_ids=true | all-gather | bytes 576 | tf_op jit(solution)/shard_map/all_gather | solution.py:22
  221.7 3.8 %fusion.1 = bf16[32,256,256]{2,1,0:T(8,128)(2,1)} fusion(f32[32,256]{1,0:T(8,128)S(1)} %copy-done.13, f32[2,256,256]{2,1,0:T(8,128)S(1)} %fusion.34, f32[32,256]{1,0:T(8,128)S(1)} %bitcast_add_fusion, pred[256,256]{1,0:T(8,128)(4,1)S(1)} %fusion.15), kind=kLoop, calls=%fused_computation.14 | loop fusion | flops 12582912 | bytes 4849664 | tf_op jit(solution)/shard_map/vmap()/convert_element_type | solution.py:75
  225.5 2.3 gather_fusion.9
  227.8 3.2 %reshape.826 = f32[1,256,32,64]{3,2,1,0:T(8,128)} reshape(bf16[4,64,2048]{2,1,0:T(8,128)(2,1)S(1)} %gather_fusion.9) | data formatting | bytes 3145728 | tf_op jit(solution)/shard_map/convert_element_type | solution.py:104
  231.0 4.6 %copy.129 = f32[1,256,32,64]{1,3,2,0:T(8,128)} copy(f32[1,256,32,64]{3,2,1,0:T(8,128)} %reshape.826) | data formatting | bytes 4194304 | tf_op jit(solution)/shard_map/convert_element_type | solution.py:104
  235.6 1.7 copy.126
  237.2 4.9 %fusion.35 = f32[32,64,256]{2,1,0:T(8,128)} fusion(bf16[256,32,64]{0,2,1:T(8,128)(2,1)S(1)} %bitcast.160, bf16[32,256,256]{2,1,0:T(8,128)(2,1)} %fusion.1), kind=kOutput, calls=%fused_computation.118 | convolution fusion | flops 268435456 | bytes 7340032 | tf_op jit(solution)/shard_map/vmap(hij,jhp->ihp)/dot_general | solution.py:76
  242.2 5.6 %while.3 = (s32[]{:T(128)}, f32[32,64,128]{2,1,0:T(8,128)S(1)}, s32[]{:T(128)}, bf16[8,32]{1,0:T(8,128)(2,1)S(1)}, bf16[8,32,64,128]{3,2,1,0:T(8,128)(2,1)}, /*index=5*/s32[]{:T(128)}, s32[]{:T(128)}, s32[]{:T(128)}) while((s32[]{:T(128)}, f32[32,64,128]{2,1,0:T(8,128)S(1)}, s32[]{:T(128)}, bf16[8,32]{1,0:T(8,128)(2,1)S(1)}, ...), condition=%wide.region_12.13_spmd, body=%wide.region_11.12_spmd.sunk | while | flops 786469 | bytes 2621895 | solution.py:38
  242.3 1.3 convert_add_fusion.2
  243.6 1.3 convert_add_fusion.2
  245.0 1.3 convert_add_fusion.2
  246.3 1.3 convert_add_fusion.2
  248.3 1.1 copy-done.2
  250.0 7.5 %multiply_reduce_fusion = (f32[256,32]{0,1:T(8,128)S(1)}, f32[1,256,32,64]{1,3,2,0:T(8,128)}) fusion(f32[1,256,32,64]{1,3,2,0:T(8,128)S(1)} %copy-done.2, f32[1,256,32,64]{1,3,2,0:T(8,128)} %bitcast.163, f32[32]{0:T(128)S(1)} %copy-done.28, f32[256,32]{0,1:T(8,128)S(1)} %copy-done.12, f32[32,64,128]{2,1,0:T(8,128)S(1)} %get-tuple-element.70, ...), kind=kOutput, calls=%fused_computation.29 | convolution fusion | flops 811065344 | bytes 13697152 | tf_op jit(solution)/shard_map/vmap(ihn,hpn->ihp)/dot_general | solution.py:99
  257.6 2.9 copy.127
  261.3 0.9 copy.137
  262.2 0.7 copy-done.4
  262.8 0.8 fusion.11
  263.7 11.6 %convolution_convert_fusion = bf16[256,4096]{1,0:T(8,128)(2,1)} fusion(bf16[256,2048]{1,0:T(8,128)(2,1)S(1)} %fusion.11, bf16[2048,4096]{1,0:T(8,128)(2,1)} %param.31), kind=kOutput, calls=%fused_computation.15 | convolution fusion | flops 4296015872 | bytes 19922944 | tf_op jit(solution)/shard_map/dot_general | solution.py:243
  275.3 36.4 %reduce-scatter.2.cloned.1.call-done = bf16[64,4096]{1,0:T(8,128)(2,1)} async-done(((bf16[256,4096]{1,0:T(8,128)(2,1)}), bf16[64,4096]{1,0:T(8,128)(2,1)}) %reduce-scatter.2.cloned.1.call-update) | async-done | bytes 524304 | tf_op jit(solution)/shard_map/reduce_scatter | solution.py:242
  (154 shorter events, 15.0 us)
Async XLA Ops:
  6.5 15.9 %copy-start = (bf16[256,2048]{1,0:T(8,128)(2,1)S(1)}, bf16[256,2048]{1,0:T(8,128)(2,1)}, u32[]{:S(2)}) copy-start(bf16[256,2048]{1,0:T(8,128)(2,1)} %param.18) | copy-start | bytes 3145732
  10.1 16.3 %all-to-all-start.1 = ((bf16[8,2,1024]{2,1,0:T(2,128)(2,1)}), bf16[8,2,1024]{2,1,0:T(2,128)(2,1)S(1)}, u32[]{:S(2)}, u32[]{:S(2)}) async-start(bf16[8,2,1024]{2,1,0:T(2,128)(2,1)} %reshape.914), calls=%async_computation.1 | async-start | bytes 65536 | tf_op jit(solution)/shard_map/all_to_all | solution.py:169
  26.4 12.5 %all-to-all-start.3 = ((bf16[8,64,256]{2,1,0:T(8,128)(2,1)}), bf16[8,64,256]{2,1,0:T(8,128)(2,1)S(1)}, u32[]{:S(2)}, u32[]{:S(2)}) async-start(bf16[8,64,256]{2,1,0:T(8,128)(2,1)} %get-tuple-element.108), calls=%async_computation.3 | async-start | bytes 524288 | tf_op jit(solution)/shard_map/all_to_all | solution.py:167
  38.9 9.4 %copy-start.27 = (s32[32]{0:T(128)S(1)}, s32[32]{0:T(128)}, u32[]{:S(2)}) copy-start(s32[32]{0:T(128)} %param.22) | copy-start | bytes 388
  38.9 9.6 %copy-start.30 = (f32[32]{0:T(128)S(1)}, f32[32]{0:T(128)}, u32[]{:S(2)}) copy-start(f32[32]{0:T(128)} %param.27) | copy-start | bytes 388
  38.9 10.9 %copy-start.24 = (f32[4,256]{1,0:T(4,128)S(1)}, f32[4,256]{1,0:T(4,128)}, u32[]{:S(2)}) copy-start(f32[4,256]{1,0:T(4,128)} %param.25) | copy-start | bytes 12292
  38.9 11.5 %copy-start.16 = (f32[4,2048]{1,0:T(4,128)S(1)}, f32[4,2048]{1,0:T(4,128)}, u32[]{:S(2)}) copy-start(f32[4,2048]{1,0:T(4,128)} %param.24) | copy-start | bytes 98308
  38.9 13.0 %copy-start.26 = (f32[32]{0:T(128)S(1)}, f32[32]{0:T(128)}, u32[]{:S(2)}) copy-start(f32[32]{0:T(128)} %param.28) | copy-start | bytes 388
  38.9 50.1 %all-to-all-start = ((bf16[8,64,2048]{2,1,0:T(8,128)(2,1)}), bf16[8,64,2048]{2,1,0:T(8,128)(2,1)S(1)}, u32[]{:S(2)}, u32[]{:S(2)}) async-start(bf16[8,64,2048]{2,1,0:T(8,128)(2,1)} %get-tuple-element.107), calls=%async_computation | async-start | bytes 4194304 | tf_op jit(solution)/shard_map/all_to_all | solution.py:165
  44.6 197.5 %all-gather.4.cloned.1.call-start = ((), (), s32[]{:S(2)}) async-start(), calls=%async_computation.7 | async-start | bytes 4718592 | tf_op jit(solution)/shard_map/all_gather | solution.py:22
  46.3 4.9 %copy-start.18 = (s32[256]{0:T(256)}, s32[256]{0:T(256)S(1)}, u32[]{:S(2)}) copy-start(s32[256]{0:T(256)S(1)} %slice.123) | copy-start | bytes 3076
  48.5 11.2 %copy-start.17 = (s32[1024]{0:T(1024)}, s32[1024]{0:T(1024)S(1)}, u32[]{:S(2)}) copy-start(s32[1024]{0:T(1024)S(1)} %pad_clamp_fusion) | copy-start | bytes 12292
  52.6 7.1 %copy-start.6 = (f32[1,32,2,128]{3,1,2,0:T(8,128)}, f32[1,32,2,128]{3,1,2,0:T(8,128)S(1)}, u32[]{:S(2)}) copy-start(f32[1,32,2,128]{3,1,2,0:T(8,128)S(1)} %reduce-window.30) | copy-start | bytes 98308
  53.0 6.7 %copy-start.8 = (f32[32,2,128]{2,1,0:T(2,128)}, f32[32,2,128]{2,1,0:T(2,128)S(1)}, u32[]{:S(2)}) copy-start(f32[32,2,128]{2,1,0:T(2,128)S(1)} %broadcast.490) | copy-start | bytes 98308
  53.7 6.0 %copy-start.10 = (f32[1,32,256]{2,1,0:T(8,128)}, f32[1,32,256]{2,1,0:T(8,128)S(1)}, u32[]{:S(2)}) copy-start(f32[1,32,256]{2,1,0:T(8,128)S(1)} %get-tuple-element.87) | copy-start | bytes 98308
  55.7 37.6 %collective-permute-start.2 = (bf16[3,256]{1,0:T(4,128)(2,1)}, bf16[3,256]{1,0:T(4,128)(2,1)}, u32[]{:S(2)}, u32[]{:S(2)}) collective-permute-start(bf16[3,256]{1,0:T(4,128)(2,1)} %slice.189), channel_id=1, source_target_pairs={{0,4},{4,8},{8,12},{12,16},{16,20},{20,24},{24,28},{1,5},{5,9},{9,... | collective-permute-start | bytes 4616 | tf_op jit(solution)/shard_map/ppermute | solution.py:16
  89.8 7.8 %copy-start.5 = (bf16[4,64,2048]{2,1,0:T(8,128)(2,1)}, bf16[4,64,2048]{2,1,0:T(8,128)(2,1)S(1)}, u32[]{:S(2)}) copy-start(bf16[4,64,2048]{2,1,0:T(8,128)(2,1)S(1)} %gather_fusion.1) | copy-start | bytes 3145732
  89.8 7.8 %copy-start.14 = (f32[1,2048]{1,0:T(1,128)S(1)}, f32[1,2048]{1,0:T(1,128)}, u32[]{:S(2)}) copy-start(f32[1,2048]{1,0:T(1,128)} %get-tuple-element.92) | copy-start | bytes 24580
  89.8 7.8 %copy-start.15 = (f32[1,2048]{1,0:T(1,128)S(1)}, f32[1,2048]{1,0:T(1,128)}, u32[]{:S(2)}) copy-start(f32[1,2048]{1,0:T(1,128)} %get-tuple-element.93) | copy-start | bytes 24580
  89.8 7.8 %copy-start.21 = (pred[256]{0:T(512)(128)(4,1)S(1)}, pred[256]{0:T(512)(128)(4,1)}, u32[]{:S(2)}) copy-start(pred[256]{0:T(512)(128)(4,1)} %get-tuple-element.103) | copy-start | bytes 772
  89.8 7.8 %copy-start.22 = (pred[256]{0:T(512)(128)(4,1)S(1)}, pred[256]{0:T(512)(128)(4,1)}, u32[]{:S(2)}) copy-start(pred[256]{0:T(512)(128)(4,1)} %get-tuple-element.104) | copy-start | bytes 772
  89.8 7.8 %copy-start.23 = (pred[256]{0:T(512)(128)(4,1)S(1)}, pred[256]{0:T(512)(128)(4,1)}, u32[]{:S(2)}) copy-start(pred[256]{0:T(512)(128)(4,1)} %get-tuple-element.105) | copy-start | bytes 772
  89.8 7.7 %collective-permute-start = (bf16[3,2048]{1,0:T(4,128)(2,1)S(1)}, bf16[3,2048]{1,0:T(4,128)(2,1)S(1)}, u32[]{:S(2)}, u32[]{:S(2)}) collective-permute-start(bf16[3,2048]{1,0:T(4,128)(2,1)S(1)} %slice.178), channel_id=1, source_target_pairs={{0,4},{4,8},{8,12},{12,16},{16,20},{20,24},{24,28},{1,5},{5,9},{9,... | collective-permute-start | bytes 36872 | tf_op jit(solution)/shard_map/ppermute | solution.py:16
  97.6 5.0 %copy-start.29 = (f32[32]{0:T(128)S(1)}, f32[32]{0:T(128)}, u32[]{:S(2)}) copy-start(f32[32]{0:T(128)} %fusion.26) | copy-start | bytes 388
  121.5 7.2 %copy-start.25 = (f32[4,256]{1,0:T(4,128)S(1)}, f32[4,256]{1,0:T(4,128)}, u32[]{:S(2)}) copy-start(f32[4,256]{1,0:T(4,128)} %param.26) | copy-start | bytes 12292
  121.5 7.3 %copy-start.19 = (s32[256]{0:T(256)S(1)}, s32[256]{0:T(256)}, u32[]{:S(2)}) copy-start(s32[256]{0:T(256)} %copy-done.18) | copy-start | bytes 3076
  121.5 7.4 %copy-start.7 = (f32[1,32,2,128]{3,1,2,0:T(8,128)S(1)}, f32[1,32,2,128]{3,1,2,0:T(8,128)}, u32[]{:S(2)}) copy-start(f32[1,32,2,128]{3,1,2,0:T(8,128)} %copy-done.6) | copy-start | bytes 98308
  121.5 7.4 %copy-start.9 = (f32[32,2,128]{2,1,0:T(2,128)S(1)}, f32[32,2,128]{2,1,0:T(2,128)}, u32[]{:S(2)}) copy-start(f32[32,2,128]{2,1,0:T(2,128)} %copy-done.8) | copy-start | bytes 98308
  121.5 11.5 %copy-start.11 = (f32[1,32,256]{2,1,0:T(8,128)S(1)}, f32[1,32,256]{2,1,0:T(8,128)}, u32[]{:S(2)}) copy-start(f32[1,32,256]{2,1,0:T(8,128)} %copy-done.10) | copy-start | bytes 98308
  121.5 104.0 %all-to-all-start.4 = ((bf16[8,64,2048]{2,1,0:T(8,128)(2,1)}), bf16[8,64,2048]{2,1,0:T(8,128)(2,1)}, u32[]{:S(2)}, u32[]{:S(2)}) async-start(bf16[8,64,2048]{2,1,0:T(8,128)(2,1)} %get-tuple-element.106), calls=%async_computation.4 | async-start | bytes 4194304 | tf_op jit(solution)/shard_map/all_to_all | solution.py:166
  128.7 93.0 %copy-start.13 = (f32[32,256]{1,0:T(8,128)S(1)}, f32[32,256]{1,0:T(8,128)}, u32[]{:S(2)}) copy-start(f32[32,256]{1,0:T(8,128)} %get-tuple-element.89) | copy-start | bytes 98308
  128.7 183.0 %reduce-scatter.2.cloned.1.call-start = ((), (), s32[]{:S(2)}) async-start(), calls=%async_computation.6 | async-start | bytes 2621440 | tf_op jit(solution)/shard_map/reduce_scatter | solution.py:242
  129.6 91.4 %collective-permute-start.1 = (bf16[3,256]{1,0:T(4,128)(2,1)S(1)}, bf16[3,256]{1,0:T(4,128)(2,1)S(1)}, u32[]{:S(2)}, u32[]{:S(2)}) collective-permute-start(bf16[3,256]{1,0:T(4,128)(2,1)S(1)} %slice.184), channel_id=1, source_target_pairs={{0,4},{4,8},{8,12},{12,16},{16,20},{20,24},{24,28},{1,5},{5,9},{9,... | collective-permute-start | bytes 4616 | tf_op jit(solution)/shard_map/ppermute | solution.py:16
  247.8 1.6 copy-start.2
  247.8 2.2 copy-start.3
  247.8 2.2 copy-start.12
  247.8 2.2 copy-start.28
  261.2 1.6 copy-start.4
  261.3 1.6 copy-start.20
  263.6 48.1 %copy-start.1 = (bf16[256,2048]{1,0:T(8,128)(2,1)S(1)}, bf16[256,2048]{1,0:T(8,128)(2,1)}, u32[]{:S(2)}) copy-start(bf16[256,2048]{1,0:T(8,128)(2,1)} %param.18) | copy-start | bytes 3145732
Sparse Core Ops, SparseCore 0:
  105.7 107.3 all-gather.3
  275.4 36.2 reduce-scatter.1
where the time goes:
time: 322 us; the launch traced here: 319 us
  blocking collectives  104 us (32%)
  waiting for transfers between devices  68.4 us (21%)
  local copies, waits for them, and re-layouts  38.5 us (12%)
  starting transfers between devices  35.3 us (11%)
  other arithmetic  29.8 us (9%)
  matrix products  27.2 us (8%)
  between operations  15.4 us (5%)
    all_gather x1, blocking collectives, carried_in(): lax.all_gather(a.astype(kind), axis)  87.8 us
    reduce_scatter x1, waiting for transfers between devices, on_device(): lax.psum_scatter(jnp.dot(normed, out_weight, preferred_element_type=jnp.f...  36.4 us
    all_to_all x1, waiting for transfers between devices, on_device(): lax.all_to_all(packed_values, 'ctx', split_axis=0, concat_axis=0, tiled=T...  29.3 us
    all_to_all x1, blocking collectives, on_device(): lax.all_to_all(packed_queries, 'ctx', split_axis=0, concat_axis=0, tiled=...  15.9 us
    dot_general x1, matrix products, on_device(): jnp.dot(normed, out_weight, preferred_element_type=jnp.float32)  11.6 us
    ppermute x3, starting transfers between devices, shifted_2(): lax.ppermute(value, axis, [(source, source + steps) for source in range(l...  10.2 us
    convert_element_type x2, local copies, waits for them, and re-layouts, gated_norm(): gated_rows = mixed_rows * jax.nn.silu(gate_rows.astype(jnp.float32))  7.76 us
    dot_general x1, matrix products, span_inflow(): jnp.einsum('ihn,hpn->ihp', head_queries, entering, precision=lax.Precisio...  7.53 us
  transfers between devices with their start and end apart: 9, of which 3 were waited for; matrix products, arithmetic and copies ran while one was open for 16% of the time, Pallas kernels for 0%

commit v1 on v0

--- a/solution.py
+++ b/solution.py
@@ -1,6 +1,10 @@
+import functools
+
 import jax
 import jax.numpy as jnp
 from jax import lax
+from jax.experimental import pallas as pl
+from jax.experimental.pallas import tpu as pltpu
 from jax.sharding import PartitionSpec as P
 
 HEAD_DIM = 64
@@ -247,6 +251,471 @@
     )
 
 
+CHUNK = 128
+LANES = 128
+
+
+def shift_rows(extended, steps, row_count):
+    return pltpu.roll(extended, steps, 0)[8 : 8 + row_count]
+
+
+def tapped(current, previous, taps, since):
+    row_count, width = current.shape
+    extended = jnp.concatenate([previous, current], axis=0)
+    total = None
+    for tap_index in range(CONV):
+        steps = CONV - 1 - tap_index
+        weight = taps[tap_index : tap_index + 1, :]
+        if steps == 0:
+            term = current * weight
+        else:
+            keep = since >= steps
+            term = jnp.where(keep, shift_rows(extended, steps, row_count) * weight, 0.0)
+        total = term if total is None else total + term
+    return total / (1.0 + jnp.exp(-total))
+
+
+def loaded_block(inverse, sequence_block, me, per_dev):
+    loaded = inverse[sequence_block]
+    slot = jnp.bitwise_xor(lax.div(loaded, per_dev), me)
+    return slot, pl.multiple_of(lax.rem(loaded, per_dev) * BLK, BLK)
+
+
+def invert_order(order, inverse, count):
+    def one(j, carry):
+        inverse[order[j]] = j
+        return carry
+
+    lax.fori_loop(0, count, one, 0)
+
+
+def mixing_kernel(
+    heads,
+    group_heads,
+    per_dev,
+    chunks_step,
+    me_ref,
+    order_ref,
+    lengths_ref,
+    rows_ref,
+    key_taps_ref,
+    query_taps_ref,
+    bias_ref,
+    log_ref,
+    mix_ref,
+    query_ref,
+    key_ref,
+    tail_ref,
+    inflow_ref,
+    gate_ref,
+    since_ref,
+    inverse,
+    previous,
+):
+    me = me_ref[0]
+    step_id = pl.program_id(0)
+    token_rows = per_dev * BLK
+
+    @pl.when(step_id == 0)
+    def _():
+        invert_order(order_ref, inverse, order_ref.shape[0])
+        previous[...] = jnp.zeros_like(previous)
+
+    lane = lax.broadcasted_iota(jnp.int32, (8, LANES), 1)
+    row8 = lax.broadcasted_iota(jnp.int32, (8, LANES), 0)
+    own = lax.rem(me * heads, group_heads)
+    bias = jnp.zeros((8, LANES), jnp.float32)
+    decay = jnp.zeros((8, LANES), jnp.float32)
+    for h in range(heads):
+        bias = jnp.where(row8 == h, bias_ref[me * heads + h], bias)
+        decay = jnp.where(row8 == h, log_ref[me * heads + h], decay)
+    decay = -jnp.exp(decay)
+    causal = lax.broadcasted_iota(jnp.int32, (CHUNK, CHUNK), 0) >= lax.broadcasted_iota(
+        jnp.int32, (CHUNK, CHUNK), 1
+    )
+    column = lax.broadcasted_iota(jnp.int32, (CHUNK, CHUNK), 1).astype(jnp.float32)
+    row_of = lax.broadcasted_iota(jnp.int32, (CHUNK, CHUNK), 0).astype(jnp.float32)
+    low_half = lax.broadcasted_iota(jnp.int32, (CHUNK, LANES), 1) < HEAD_DIM
+    taps = jnp.concatenate([key_taps_ref[...], query_taps_ref[...]], axis=1)
+
+    def one_chunk(local, carry):
+        chunk = step_id * chunks_step + local
+        first = chunk * CHUNK
+        pieces, raw = [], None
+        for half in range(CHUNK // BLK):
+            loaded = inverse[chunk * (CHUNK // BLK) + half]
+            slot = jnp.bitwise_xor(lax.div(loaded, per_dev), me)
+            inner = lax.rem(loaded, per_dev)
+            start = pl.multiple_of(inner * BLK, BLK)
+            pieces.append(rows_ref[slot, pl.ds(start, BLK), :].astype(jnp.float32))
+            lanes_at = pl.multiple_of(lax.div(inner, 2) * LANES, LANES)
+            steps_in = rows_ref[
+                slot, pl.ds(token_rows, group_heads), pl.ds(lanes_at, LANES)
+            ].astype(jnp.float32)
+            turn = BLK * jnp.bitwise_xor(lax.rem(inner, 2), half)
+            steps_in = pltpu.roll(steps_in, turn, 1)
+            raw = steps_in if raw is None else jnp.where(lane[:1] < BLK, raw, steps_in)
+        raw = pltpu.roll(raw, lax.rem(group_heads - own, group_heads), 0)[:8] + bias
+        step = jnp.maximum(raw, 0.0) + jnp.log(1.0 + jnp.exp(-jnp.abs(raw)))
+        sums = decay * step
+        width = 1
+        while width < CHUNK:
+            sums = sums + jnp.where(lane >= width, pltpu.roll(sums, width, 1), 0.0)
+            width *= 2
+        position = first + lane
+        begun = jnp.zeros_like(lane)
+        offset = jnp.int32(0)
+        for k in range(lengths_ref.shape[0]):
+            begun = jnp.where(position >= offset, offset, begun)
+            offset = offset + lengths_ref[k]
+        last_sum = jnp.sum(jnp.where(lane == CHUNK - 1, sums, 0.0), axis=1, keepdims=True)
+        last_begun = jnp.max(begun, axis=1, keepdims=True)
+        tail = jnp.where(position >= last_begun, jnp.exp(last_sum - sums) * step, 0.0)
+        inflow = jnp.where(begun < first, jnp.exp(sums), 0.0)
+        gate = jnp.where(last_begun < first, jnp.exp(last_sum), 0.0)
+        since = (position - begun).astype(jnp.float32)
+        stacked = jnp.concatenate(
+            [sums, tail, inflow, since, jnp.zeros((CHUNK - 32, LANES), jnp.float32)], axis=0
+        )
+        turned = stacked.T
+
+        def spread(at):
+            return jnp.broadcast_to(turned[:, at : at + 1], (CHUNK, LANES))
+
+        since_rows = spread(24)
+        since_ref[local] = since_rows
+        current = jnp.concatenate(pieces, axis=0)
+        wide_since = jnp.concatenate([since_rows, since_rows], axis=1)
+        conv = tapped(current, previous[...], taps, wide_since).astype(jnp.bfloat16)
+        previous[...] = current[CHUNK - 8 :]
+        keys, queries = conv[:, :STATE], conv[:, STATE:]
+        query_ref[local] = queries
+        key_ref[local] = keys.astype(jnp.float32).T.astype(jnp.bfloat16)
+        inner_products = lax.dot_general(
+            queries, keys, (((1,), (1,)), ((), ())), preferred_element_type=jnp.float32
+        )
+        allowed = jnp.where(causal & (column >= row_of - since_rows), 0.0, -1e30)
+        for h in range(heads):
+            exponent = (spread(h) + allowed) - sums[h : h + 1, :]
+            weights = jnp.exp(exponent) * (inner_products * step[h : h + 1, :])
+            mix_ref[local, :, h * CHUNK : (h + 1) * CHUNK] = weights.astype(jnp.bfloat16)
+        for pair in range(heads // 2):
+            at = slice(pair * LANES, (pair + 1) * LANES)
+            tail_ref[local, :, at] = jnp.where(
+                low_half, spread(8 + 2 * pair), spread(9 + 2 * pair)
+            )
+            inflow_ref[local, :, at] = jnp.where(
+                low_half, spread(16 + 2 * pair), spread(17 + 2 * pair)
+            )
+            gate_ref[local, :, at] = jnp.where(
+                low_half[:8],
+                jnp.broadcast_to(gate[2 * pair : 2 * pair + 1], (8, LANES)),
+                jnp.broadcast_to(gate[2 * pair + 1 : 2 * pair + 2], (8, LANES)),
+            )
+        return carry
+
+    lax.fori_loop(0, chunks_step, one_chunk, 0)
+
+
+def scan_kernel(
+    heads,
+    per_dev,
+    chunks_step,
+    me_ref,
+    order_ref,
+    skip_ref,
+    rows_ref,
+    taps_ref,
+    mix_ref,
+    query_ref,
+    key_ref,
+    tail_ref,
+    inflow_ref,
+    gate_ref,
+    since_ref,
+    out_ref,
+    inverse,
+    previous,
+    state,
+):
+    me = me_ref[0]
+    step_id = pl.program_id(0)
+
+    @pl.when(step_id == 0)
+    def _():
+        invert_order(order_ref, inverse, order_ref.shape[0])
+        previous[...] = jnp.zeros_like(previous)
+        state[...] = jnp.zeros_like(state)
+
+    width = heads * HEAD_DIM
+    lane = lax.broadcasted_iota(jnp.int32, (1, width), 1)
+    skip = jnp.zeros((1, width), jnp.float32)
+    for h in range(heads):
+        skip = jnp.where(lane >= h * HEAD_DIM, skip_ref[me * heads + h], skip)
+    low_half = lax.broadcasted_iota(jnp.int32, (CHUNK, LANES), 1) < HEAD_DIM
+    taps = taps_ref[...]
+
+    def one_chunk(local, carry):
+        chunk = step_id * chunks_step + local
+        pieces = []
+        for half in range(CHUNK // BLK):
+            slot, start = loaded_block(
+                inverse, chunk * (CHUNK // BLK) + half, me, per_dev
+            )
+            pieces.append(rows_ref[slot, pl.ds(start, BLK), :].astype(jnp.float32))
+        current = jnp.concatenate(pieces, axis=0)
+        since = since_ref[local]
+        wide_since = jnp.concatenate([since] * (width // LANES), axis=1)
+        values = tapped(current, previous[...], taps, wide_since).astype(jnp.bfloat16)
+        previous[...] = current[CHUNK - 8 :]
+        values_wide = values.astype(jnp.float32)
+        entering = state[...]
+        carried = jnp.dot(
+            query_ref[local], entering.astype(jnp.bfloat16), preferred_element_type=jnp.float32
+        )
+        total = carried * inflow_ref[local] + skip * values_wide
+        tail_values = (values_wide * tail_ref[local]).astype(jnp.bfloat16)
+        state[...] = gate_ref[local][:1] * entering + jnp.dot(
+            key_ref[local], tail_values, preferred_element_type=jnp.float32
+        )
+        zero = jnp.zeros((CHUNK, LANES), jnp.bfloat16)
+        for pair in range(heads // 2):
+            at = slice(pair * LANES, (pair + 1) * LANES)
+            both = values[:, at]
+            block = jnp.concatenate(
+                [jnp.where(low_half, both, zero), jnp.where(low_half, zero, both)], axis=0
+            )
+            intra = jnp.dot(
+                mix_ref[local, :, 2 * pair * CHUNK : 2 * (pair + 1) * CHUNK],
+                block,
+                preferred_element_type=jnp.float32,
+            )
+            out_ref[local, :, at] = total[:, at] + intra
+        return carry
+
+    lax.fori_loop(0, chunks_step, one_chunk, 0)
+
+
+def gating_kernel(per_dev, me_ref, order_ref, mixed_ref, rows_ref, *refs):
+    out_refs, inverse = refs[:-1], refs[-1]
+    me = me_ref[0]
+    invert_order(order_ref, inverse, order_ref.shape[0])
+    for turn, out_ref in enumerate(out_refs):
+        owner = jnp.bitwise_xor(me, turn)
+
+        def one_block(b, carry, owner=owner, out_ref=out_ref):
+            slot, start = loaded_block(inverse, owner * per_dev + b, me, per_dev)
+            gates = rows_ref[slot, pl.ds(start, BLK), :].astype(jnp.float32)
+            at = pl.multiple_of((owner * per_dev + b) * BLK, BLK)
+            mixed = mixed_ref[pl.ds(at, BLK), :]
+            gated = mixed * (gates / (1.0 + jnp.exp(-gates)))
+            out_ref[pl.ds(pl.multiple_of(b * BLK, BLK), BLK), :] = gated.astype(jnp.bfloat16)
+            return carry
+
+        lax.fori_loop(0, per_dev, one_block, 0)
+
+
+def projection_kernel(
+    groups, place_ref, gated_ref, gain_ref, weight_ref, away_ref, stay_ref, normed
+):
+    turns, rows, width = gated_ref.shape
+    per_group = turns // groups
+    me, mine = place_ref[0], place_ref[1]
+    piece = rows // 4
+
+    @pl.when(pl.program_id(0) == 0)
+    def _():
+        for group in range(groups):
+            members = range(group * per_group, (group + 1) * per_group)
+            squares = jnp.zeros((rows, 1), jnp.float32)
+            for turn in members:
+                gated = gated_ref[turn].astype(jnp.float32)
+                squares = squares + jnp.sum(gated * gated, axis=1, keepdims=True)
+            inverse_rms = lax.rsqrt(squares * (1.0 / (per_group * width)) + 1e-05)
+            for turn in members:
+                source = jnp.bitwise_xor(me, turn)
+                gain = gain_ref[pl.ds(source, 1), :]
+                result = (gated_ref[turn].astype(jnp.float32) * inverse_rms * gain).astype(
+                    jnp.bfloat16
+                )
+                at = pl.multiple_of(source * width, width)
+                for block in range(4):
+                    away = jnp.bitwise_xor(block, mine)
+                    kept = 1 - lax.rem(away, 2)
+                    slot = 2 * kept + (1 - lax.div(away, 2))
+                    target = pl.multiple_of(slot * piece, piece)
+                    normed[pl.ds(target, piece), pl.ds(at, width)] = result[
+                        block * piece : (block + 1) * piece
+                    ]
+
+    partial = jnp.dot(normed[...], weight_ref[...], preferred_element_type=jnp.float32)
+    partial = partial.astype(jnp.bfloat16)
+    away_ref[...] = partial[: 2 * piece]
+    stay_ref[...] = partial[2 * piece :]
+
+
+def head_split(
+    values_in,
+    gate_in,
+    keys_in,
+    queries_in,
+    step_in,
+    block_order,
+    doc_lengths,
+    conv_values,
+    conv_keys,
+    conv_queries,
+    decay_log,
+    step_bias,
+    skip_gain,
+    norm_gain,
+    out_weight,
+):
+    ctx_count = lax.axis_size("ctx")
+    me = lax.axis_index("ctx")
+    tp_index = lax.axis_index("tp")
+    token_count, channels = values_in.shape
+    per_dev = token_count // BLK
+    blocks = block_order.shape[0]
+    total_tokens = token_count * ctx_count
+    heads_local = step_in.shape[1]
+    heads = heads_local // ctx_count
+    width = heads * HEAD_DIM
+    groups = keys_in.shape[1] // STATE
+    group_heads = heads_local // groups
+    lanes_count = ctx_count // groups
+    chunks = total_tokens // CHUNK
+    my_group = me // lanes_count
+    place = jnp.stack([me, tp_index]).astype(jnp.int32)
+    me_only = place[:1]
+
+    def turned(value, turn):
+        return lax.ppermute(value, "ctx", [(i, i ^ turn) for i in range(ctx_count)])
+
+    def for_group(group):
+        keys = lax.dynamic_slice_in_dim(keys_in, group * STATE, STATE, 1)
+        queries = lax.dynamic_slice_in_dim(queries_in, group * STATE, STATE, 1)
+        steps = lax.dynamic_slice_in_dim(step_in, group * group_heads, group_heads, 1)
+        return jnp.concatenate([jnp.concatenate([keys, queries], axis=1), steps.T], axis=0)
+
+    held = [for_group(my_group)]
+    for g in range(1, groups):
+        held.append(turned(for_group(my_group ^ g), g * lanes_count))
+    held = jnp.stack(held)
+    gathered = [held]
+    for turn in range(1, lanes_count):
+        gathered.append(turned(held, turn))
+    group_rows = jnp.stack(gathered, axis=1).reshape((ctx_count,) + held.shape[1:])
+
+    def spread_heads(rows):
+        own = lax.dynamic_slice_in_dim(rows, me * width, width, 1)
+        result = [own]
+        for turn in range(1, ctx_count):
+            block = lax.dynamic_slice_in_dim(rows, (me ^ turn) * width, width, 1)
+            result.append(turned(block, turn))
+        return jnp.stack(result)
+
+    value_rows = spread_heads(values_in)
+    gate_rows = spread_heads(gate_in)
+
+    key_taps = lax.dynamic_slice_in_dim(conv_keys, my_group * STATE, STATE, 1)
+    query_taps = lax.dynamic_slice_in_dim(conv_queries, my_group * STATE, STATE, 1)
+    value_taps = lax.dynamic_slice_in_dim(conv_values, me * width, width, 1)
+
+    smem = pl.BlockSpec(memory_space=pltpu.SMEM)
+
+    def whole(array):
+        return pl.BlockSpec(array.shape, lambda *ids: (0,) * array.ndim)
+
+    grid_steps = 4
+    chunks_step = chunks // grid_steps
+
+    def per_step(rows, columns):
+        return pl.BlockSpec((chunks_step, rows, columns), lambda i: (i, 0, 0))
+
+    mix_shapes = [
+        ((CHUNK, heads * CHUNK), jnp.bfloat16),
+        ((CHUNK, STATE), jnp.bfloat16),
+        ((STATE, CHUNK), jnp.bfloat16),
+        ((CHUNK, width), jnp.float32),
+        ((CHUNK, width), jnp.float32),
+        ((8, width), jnp.float32),
+        ((CHUNK, LANES), jnp.float32),
+    ]
+    mixing = pl.pallas_call(
+        functools.partial(mixing_kernel, heads, group_heads, per_dev, chunks_step),
+        grid=(grid_steps,),
+        in_specs=[smem, smem, smem, whole(group_rows), whole(key_taps), whole(query_taps), smem, smem],
+        out_specs=[per_step(*shape) for shape, _ in mix_shapes],
+        out_shape=[jax.ShapeDtypeStruct((chunks,) + shape, kind) for shape, kind in mix_shapes],
+        scratch_shapes=[pltpu.SMEM((blocks,), jnp.int32), pltpu.VMEM((8, 2 * STATE), jnp.float32)],
+        compiler_params=pltpu.CompilerParams(vmem_limit_bytes=24 * 1024 * 1024),
+        cost_estimate=pl.CostEstimate(flops=20_000_000, bytes_accessed=12_000_000, transcendentals=2_000_000),
+        name="mixing",
+    )(me_only, block_order, doc_lengths, group_rows, key_taps, query_taps, step_bias, decay_log)
+
+    mixed = pl.pallas_call(
+        functools.partial(scan_kernel, heads, per_dev, chunks_step),
+        grid=(grid_steps,),
+        in_specs=[smem, smem, smem, whole(value_rows), whole(value_taps)]
+        + [per_step(*shape) for shape, _ in mix_shapes],
+        out_specs=per_step(CHUNK, width),
+        out_shape=jax.ShapeDtypeStruct((chunks, CHUNK, width), jnp.float32),
+        scratch_shapes=[
+            pltpu.SMEM((blocks,), jnp.int32),
+            pltpu.VMEM((8, width), jnp.float32),
+            pltpu.VMEM((STATE, width), jnp.float32),
+        ],
+        compiler_params=pltpu.CompilerParams(vmem_limit_bytes=24 * 1024 * 1024),
+        cost_estimate=pl.CostEstimate(flops=600_000_000, bytes_accessed=14_000_000, transcendentals=600_000),
+        name="scan",
+    )(me_only, block_order, skip_gain, value_rows, value_taps, *mixing)
+
+    gated = pl.pallas_call(
+        functools.partial(gating_kernel, per_dev),
+        in_specs=[smem, smem, pl.BlockSpec(memory_space=pltpu.VMEM), pl.BlockSpec(memory_space=pltpu.VMEM)],
+        out_specs=[pl.BlockSpec(memory_space=pltpu.VMEM)] * ctx_count,
+        out_shape=[jax.ShapeDtypeStruct((token_count, width), jnp.bfloat16)] * ctx_count,
+        scratch_shapes=[pltpu.SMEM((blocks,), jnp.int32)],
+        compiler_params=pltpu.CompilerParams(vmem_limit_bytes=24 * 1024 * 1024),
+        cost_estimate=pl.CostEstimate(flops=5_000_000, bytes_accessed=4_000_000, transcendentals=600_000),
+        name="gating",
+    )(me_only, block_order, mixed.reshape(total_tokens, width), gate_rows)
+
+    received = jnp.stack([gated[0]] + [turned(gated[turn], turn) for turn in range(1, ctx_count)])
+
+    columns = out_weight.shape[1]
+    tile = 512
+    half_shape = jax.ShapeDtypeStruct((token_count // 2, columns), jnp.bfloat16)
+    gain = norm_gain.reshape(ctx_count, width)
+    away, stay = pl.pallas_call(
+        functools.partial(projection_kernel, groups),
+        grid=(columns // tile,),
+        in_specs=[
+            smem,
+            whole(received),
+            whole(gain),
+            pl.BlockSpec((channels, tile), lambda i: (0, i)),
+        ],
+        out_specs=[pl.BlockSpec((token_count // 2, tile), lambda i: (0, i))] * 2,
+        out_shape=[half_shape] * 2,
+        scratch_shapes=[pltpu.VMEM((token_count, channels), jnp.bfloat16)],
+        compiler_params=pltpu.CompilerParams(vmem_limit_bytes=24 * 1024 * 1024),
+        cost_estimate=pl.CostEstimate(
+            flops=2 * token_count * channels * columns, bytes_accessed=20_000_000, transcendentals=0
+        ),
+        name="projection",
+    )(place, received, gain, out_weight)
+
+    def joined(kept, sent, turn):
+        came = lax.ppermute(sent, "tp", [(i, i ^ turn) for i in range(4)])
+        return (kept.astype(jnp.float32) + came.astype(jnp.float32)).astype(jnp.bfloat16)
+
+    across = joined(stay, away, 1)
+    piece = token_count // 4
+    return joined(across[piece:], across[:piece], 2)
+
+
 def solution(mesh):
     in_specs = (
         P("ctx", "tp"),
@@ -266,6 +735,8 @@
         P("tp", None),
     )
     out_specs = P(("ctx", "tp"), None)
+    ctx_count, tp_count = mesh.shape["ctx"], mesh.shape["tp"]
+    plan = head_split if tp_count == 4 and ctx_count == 8 else on_device
     return jax.shard_map(
-        on_device, mesh=mesh, in_specs=in_specs, out_specs=out_specs, check_vma=False
-    )
+        plan, mesh=mesh, in_specs=in_specs, out_specs=out_specs, check_vma=False
+    )

time: 322 us -> 151 us (0.47)
  blocking collectives: 104 us -> 0 us
  Pallas kernels: 0 us -> 36.7 us
  local copies, waits for them, and re-layouts: 38.5 us -> 10.4 us
  other arithmetic: 29.8 us -> 2.12 us
  matrix products: 27.2 us -> 0 us
  between operations: 15.4 us -> 0.46 us
  waiting for transfers between devices: 68.4 us -> 64.5 us
    all_gather x1 -> x0, blocking collectives: 87.8 us -> none  [carried_in(): lax.all_gather(a.astype(kind), axis)]
    ppermute x3 -> x27, waiting for transfers between devices: 0.01 us -> 64.5 us  [the longest x25 49.4 us: turned(): return lax.ppermute(value, 'ctx', [(i, i ^ turn) for i in range(ctx_count)])]
    pallas_call x0 -> x4, Pallas kernels: none -> 36.7 us  [the longest x1 19.6 us: head_split(): pl.pallas_call(functools.partial(mixing_kernel, heads, group_heads, per_d...]
    reduce_scatter x1 -> x0, waiting for transfers between devices: 36.4 us -> none  [on_device(): lax.psum_scatter(jnp.dot(normed, out_weight, preferred_element_type=jnp.f...]
    all_to_all x4 -> x0, waiting for transfers between devices: 31.9 us -> none  [the longest x1 29.3 us: on_device(): lax.all_to_all(packed_values, 'ctx', split_axis=0, concat_axis=0, tiled=T...]
    dot_general x5 -> x0, matrix products: 27.2 us -> none  [the longest x1 11.6 us: on_device(): jnp.dot(normed, out_weight, preferred_element_type=jnp.float32)]
    ppermute x3 -> x27, starting transfers between devices: 10.2 us -> 35.7 us  [the longest x25 34 us: turned(): return lax.ppermute(value, 'ctx', [(i, i ^ turn) for i in range(ctx_count)])]
    all_to_all x4 -> x0, starting transfers between devices: 25.1 us -> none  [the longest x1 7.22 us: on_device(): lax.all_to_all(packed_gates, 'ctx', split_axis=0, concat_axis=0, tiled=True)]
  transfers between devices with their start and end apart: 9 -> 27, of which waited for: 3 -> 17; matrix products, arithmetic and copies ran while one was open for 16% -> 5% of each run, Pallas kernels for 0% -> 0%
where the time goes in v1:
time: 151 us; the launch traced here: 150 us
  waiting for transfers between devices  64.5 us (43%)
  Pallas kernels  36.7 us (24%)
  starting transfers between devices  35.7 us (24%)
  local copies, waits for them, and re-layouts  10.4 us (7%)
  other arithmetic  2.12 us (1%)
    ppermute x25, waiting for transfers between devices, turned(): return lax.ppermute(value, 'ctx', [(i, i ^ turn) for i in range(ctx_count)])  49.4 us
    ppermute x25, starting transfers between devices, turned(): return lax.ppermute(value, 'ctx', [(i, i ^ turn) for i in range(ctx_count)])  34 us
    pallas_call x1, Pallas kernels, head_split(): pl.pallas_call(functools.partial(mixing_kernel, heads, group_heads, per_d...  19.6 us
    ppermute x2, waiting for transfers between devices, joined(): came = lax.ppermute(sent, 'tp', [(i, i ^ turn) for i in range(4)])  15.1 us
    pallas_call x1, Pallas kernels, head_split(): pl.pallas_call(functools.partial(projection_kernel, groups), grid=(column...  8.36 us
    pallas_call x1, Pallas kernels, head_split(): pl.pallas_call(functools.partial(scan_kernel, heads, per_dev, chunks_step...  6.61 us
    unnamed x55, local copies, waits for them, and re-layouts  6.13 us
  transfers between devices with their start and end apart: 27, of which 17 were waited for; matrix products, arithmetic and copies ran while one was open for 5% of the time, Pallas kernels for 0%

profile of v1, /device:TPU:16, one launch (start us, length us, event | category | flops | bytes accessed | tf_op | source)
XLA Modules:
  0.0 149.9 jit_solution(4750733708347605861)
XLA Ops:
  0.0 0.7 dynamic-slice_bitcast_fusion.1
  0.7 1.0 constant_dynamic-slice_fusion.11
  2.4 2.3 %constant_dynamic-slice_fusion.14 = (bf16[256,256]{1,0:T(8,128)(2,1)}, bf16[256,256]{1,0:T(8,128)(2,1)}, bf16[256,256]{1,0:T(8,128)(2,1)}, bf16[256,256]{1,0:T(8...) fusion(bf16[256,2048]{1,0:T(8,128)(2,1)} %param.15, s32[]{:T(128)S(6)} %select_n.61, ...), kind=kLoop, calls=%fused_computation.46 | loop fusion | bytes 1835036 | tf_op jit(solution)/shard_map/dynamic_slice | solution.py:614
  4.7 1.8 %collective-permute-start = (bf16[256,256]{1,0:T(8,128)(2,1)}, bf16[256,256]{1,0:T(8,128)(2,1)}, u32[]{:S(2)}, u32[]{:S(2)}) collective-permute-start(bf16[256,256]{1,0:T(8,128)(2,1)} %get-tuple-element.51), channel_id=1, source_target_pairs={{0,4},{4,0},{8,12},{12,8},{16,20},{20,16},{24,28},{28,24},{1,5},{5... | collective-permute-start | bytes 393224 | tf_op jit(solution)/shard_map/ppermute | solution.py:593
  6.5 1.6 %collective-permute-start.1 = (bf16[256,256]{1,0:T(8,128)(2,1)}, bf16[256,256]{1,0:T(8,128)(2,1)}, u32[]{:S(2)}, u32[]{:S(2)}) collective-permute-start(bf16[256,256]{1,0:T(8,128)(2,1)} %get-tuple-element.50), channel_id=1, source_target_pairs={{0,8},{4,12},{8,0},{12,4},{16,24},{20,28},{24,16},{28,20},{1,9},{5... | collective-permute-start | bytes 393224 | tf_op jit(solution)/shard_map/ppermute | solution.py:593
  8.2 2.8 %collective-permute-start.3 = (bf16[256,256]{1,0:T(8,128)(2,1)}, bf16[256,256]{1,0:T(8,128)(2,1)}, u32[]{:S(2)}, u32[]{:S(2)}) collective-permute-start(bf16[256,256]{1,0:T(8,128)(2,1)} %get-tuple-element.48), channel_id=1, source_target_pairs={{0,16},{4,20},{8,24},{12,28},{16,0},{20,4},{24,8},{28,12},{1,17},{... | collective-permute-start | bytes 393224 | tf_op jit(solution)/shard_map/ppermute | solution.py:593
  11.0 0.9 bitcast_dynamic-update-slice_fusion.23
  13.0 1.3 collective-permute-start.4
  14.3 0.9 bitcast_dynamic-update-slice_fusion.22
  15.2 2.5 %collective-permute-done.1 = bf16[256,256]{1,0:T(8,128)(2,1)} collective-permute-done((bf16[256,256]{1,0:T(8,128)(2,1)}, bf16[256,256]{1,0:T(8,128)(2,1)}, u32[]{:S(2)}, u32[]{:S(2)}) %collective-permute-start.1) | collective-permute-done | bytes 131104 | tf_op jit(solution)/shard_map/ppermute | solution.py:593
  18.0 0.9 bitcast_dynamic-update-slice_fusion.21
  18.9 1.4 collective-permute-done.2
  20.3 1.1 collective-permute-start.6
  21.4 0.9 bitcast_dynamic-update-slice_fusion.20
  22.3 2.0 %collective-permute-done.3 = bf16[256,256]{1,0:T(8,128)(2,1)} collective-permute-done((bf16[256,256]{1,0:T(8,128)(2,1)}, bf16[256,256]{1,0:T(8,128)(2,1)}, u32[]{:S(2)}, u32[]{:S(2)}) %collective-permute-start.3) | collective-permute-done | bytes 131104 | tf_op jit(solution)/shard_map/ppermute | solution.py:593
  24.7 0.9 bitcast_dynamic-update-slice_fusion.19
  25.6 2.9 %collective-permute-done.4 = bf16[256,256]{1,0:T(8,128)(2,1)S(1)} collective-permute-done((bf16[256,256]{1,0:T(8,128)(2,1)S(1)}, bf16[256,256]{1,0:T(8,128)(2,1)S(1)}, u32[]{:S(2)}, u32[]{:S(2)}) %collective-permute-start.4) | collective-permute-done | bytes 131104 | tf_op jit(solution)/shard_map/ppermute | solution.py:593
  28.5 3.4 %collective-permute-start.12 = (bf16[256,256]{1,0:T(8,128)(2,1)S(1)}, bf16[256,256]{1,0:T(8,128)(2,1)S(1)}, u32[]{:S(2)}, u32[]{:S(2)}) collective-permute-start(bf16[256,256]{1,0:T(8,128)(2,1)S(1)} %get-tuple-element.43), channel_id=1, source_target_pairs={{0,8},{4,12},{8,0},{12,4},{16,24},{20,28},{24,16},{28,20},{1,9},{5... | collective-permute-start | bytes 393224 | tf_op jit(solution)/shard_map/ppermute | solution.py:593
  32.0 1.4 collective-permute-done.5
  33.4 2.4 %collective-permute-done.6 = bf16[256,256]{1,0:T(8,128)(2,1)S(1)} collective-permute-done((bf16[256,256]{1,0:T(8,128)(2,1)S(1)}, bf16[256,256]{1,0:T(8,128)(2,1)S(1)}, u32[]{:S(2)}, u32[]{:S(2)}) %collective-permute-start.6) | collective-permute-done | bytes 131104 | tf_op jit(solution)/shard_map/ppermute | solution.py:593
  36.3 2.8 %collective-permute-start.15 = (bf16[256,256]{1,0:T(8,128)(2,1)S(1)}, bf16[256,256]{1,0:T(8,128)(2,1)S(1)}, u32[]{:S(2)}, u32[]{:S(2)}) collective-permute-start(bf16[256,256]{1,0:T(8,128)(2,1)S(1)} %get-tuple-element.40), channel_id=1, source_target_pairs={{0,20},{4,16},{8,28},{12,24},{16,4},{20,0},{24,12},{28,8},{1,21},{... | collective-permute-start | bytes 393224 | tf_op jit(solution)/shard_map/ppermute | solution.py:593
  39.1 1.8 %collective-permute-start.16 = (bf16[256,256]{1,0:T(8,128)(2,1)S(1)}, bf16[256,256]{1,0:T(8,128)(2,1)S(1)}, u32[]{:S(2)}, u32[]{:S(2)}) collective-permute-start(bf16[256,256]{1,0:T(8,128)(2,1)S(1)} %get-tuple-element.45), channel_id=1, source_target_pairs={{0,24},{4,28},{8,16},{12,20},{16,8},{20,12},{24,0},{28,4},{1,25},{... | collective-permute-start | bytes 393224 | tf_op jit(solution)/shard_map/ppermute | solution.py:593
  40.9 1.0 collective-permute-start.17
  41.9 8.3 %collective-permute-done.14 = bf16[256,256]{1,0:T(8,128)(2,1)S(1)} collective-permute-done((bf16[256,256]{1,0:T(8,128)(2,1)S(1)}, bf16[256,256]{1,0:T(8,128)(2,1)S(1)}, u32[]{:S(2)}, u32[]{:S(2)}) %collective-permute-start.14) | collective-permute-done | bytes 131104 | tf_op jit(solution)/shard_map/ppermute | solution.py:593
  50.2 2.8 %collective-permute-done.15 = bf16[256,256]{1,0:T(8,128)(2,1)S(1)} collective-permute-done((bf16[256,256]{1,0:T(8,128)(2,1)S(1)}, bf16[256,256]{1,0:T(8,128)(2,1)S(1)}, u32[]{:S(2)}, u32[]{:S(2)}) %collective-permute-start.15) | collective-permute-done | bytes 131104 | tf_op jit(solution)/shard_map/ppermute | solution.py:593
  53.6 4.4 %collective-permute-start.9 = (bf16[2,272,256]{2,1,0:T(8,128)(2,1)S(1)}, bf16[2,272,256]{2,1,0:T(8,128)(2,1)S(1)}, u32[]{:S(2)}, u32[]{:S(2)}) collective-permute-start(bf16[2,272,256]{2,1,0:T(8,128)(2,1)S(1)} %get-tuple-element.54), channel_id=1, source_target_pairs={{0,8},{4,12},{8,0},{12,4},{16,24},{20,28},{24,16},{28,20},{1,9},{5... | collective-permute-start | bytes 835592 | tf_op jit(solution)/shard_map/ppermute | solution.py:593
  58.7 1.3 collective-permute-done.17
  60.0 8.5 %collective-permute-done.8 = bf16[2,272,256]{2,1,0:T(8,128)(2,1)S(1)} collective-permute-done((bf16[2,272,256]{2,1,0:T(8,128)(2,1)S(1)}, bf16[2,272,256]{2,1,0:T(8,128)(2,1)S(1)}, u32[]{:S(2)}, u32[]{:S(2)}) %collective-permute-start.8) | collective-permute-done | bytes 278560 | tf_op jit(solution)/shard_map/ppermute | solution.py:593
  68.8 0.7 copy-done.1
  69.5 19.6 %mixing.1 = (bf16[16,128,512]{2,1,0:T(8,128)(2,1)S(1)}, bf16[16,128,128]{2,1,0:T(8,128)(2,1)S(1)}, bf16[16,128,128]{2,1,0:T(8,128)(2,1)S(1)}, f32[16,128,256]{2,...) custom-call(s32[1]{0:T(128)} %bitcast.me_ref, ...), custom_call_target="tpu_custom_call" | custom-call | flops 20000000 | bytes 12000000 | tf_op jit(solution)/shard_map/mixing/pallas_call | solution.py:645
  89.1 6.6 %scan.1 = f32[16,128,256]{2,1,0:T(8,128)S(1)} custom-call(s32[1]{0:T(128)} %bitcast.me_ref, s32[32]{0:T(128)S(1)} %copy-done.1, f32[32]{0:T(128)S(1)} %copy-done.2, bf16[8,256,256]{2,1,0:T(8,128)(2,1)S(1)} %bitcast_dynamic-update-slice_fusion.16.rows_ref, f32[4,256]{1,0:T(4,128)S(1)} %constant_dynamic-slice_fusion.13.taps_ref, ...), custom_call_target="tpu_custom_call" | custom-call | flops 600000000 | bytes 14000000 | tf_op jit(solution)/shard_map/scan/pallas_call | solution.py:657
  95.7 2.2 %gating.1 = (bf16[256,256]{1,0:T(8,128)(2,1)S(1)}, bf16[256,256]{1,0:T(8,128)(2,1)S(1)}, bf16[256,256]{1,0:T(8,128)(2,1)S(1)}, bf16[256,256]{1,0:T(8,128)(2,1)S(...) custom-call(s32[1]{0:T(128)} %bitcast.me_ref, ...), custom_call_target="tpu_custom_call" | custom-call | flops 5000000 | bytes 4000000 | tf_op jit(solution)/shard_map/gating/pallas_call | solution.py:674
  97.9 1.1 collective-permute-start.18
  99.0 1.7 %collective-permute-start.19 = (bf16[256,256]{1,0:T(8,128)(2,1)S(1)}, bf16[256,256]{1,0:T(8,128)(2,1)S(1)}, u32[]{:S(2)}, u32[]{:S(2)}) collective-permute-start(bf16[256,256]{1,0:T(8,128)(2,1)S(1)} %get-tuple-element.31), channel_id=1, source_target_pairs={{0,8},{4,12},{8,0},{12,4},{16,24},{20,28},{24,16},{28,20},{1,9},{5... | collective-permute-start | bytes 393224 | tf_op jit(solution)/shard_map/ppermute | solution.py:593
  101.4 2.1 %collective-permute-start.21 = (bf16[256,256]{1,0:T(8,128)(2,1)S(1)}, bf16[256,256]{1,0:T(8,128)(2,1)S(1)}, u32[]{:S(2)}, u32[]{:S(2)}) collective-permute-start(bf16[256,256]{1,0:T(8,128)(2,1)S(1)} %get-tuple-element.33), channel_id=1, source_target_pairs={{0,16},{4,20},{8,24},{12,28},{16,0},{20,4},{24,8},{28,12},{1,17},{... | collective-permute-start | bytes 393224 | tf_op jit(solution)/shard_map/ppermute | solution.py:593
  103.6 1.3 collective-permute-start.22
  104.9 1.0 collective-permute-start.23
  105.9 1.5 %collective-permute-start.24 = (bf16[256,256]{1,0:T(8,128)(2,1)S(1)}, bf16[256,256]{1,0:T(8,128)(2,1)S(1)}, u32[]{:S(2)}, u32[]{:S(2)}) collective-permute-start(bf16[256,256]{1,0:T(8,128)(2,1)S(1)} %get-tuple-element.36), channel_id=1, source_target_pairs={{0,28},{4,24},{8,20},{12,16},{16,12},{20,8},{24,4},{28,0},{1,29},{... | collective-permute-start | bytes 393224 | tf_op jit(solution)/shard_map/ppermute | solution.py:593
  107.5 0.7 collective-permute-done.20
  108.2 7.5 %collective-permute-done.21 = bf16[256,256]{1,0:T(8,128)(2,1)S(1)} collective-permute-done((bf16[256,256]{1,0:T(8,128)(2,1)S(1)}, bf16[256,256]{1,0:T(8,128)(2,1)S(1)}, u32[]{:S(2)}, u32[]{:S(2)}) %collective-permute-start.21) | collective-permute-done | bytes 131104 | tf_op jit(solution)/shard_map/ppermute | solution.py:593
  115.7 2.8 %collective-permute-done.22 = bf16[256,256]{1,0:T(8,128)(2,1)S(1)} collective-permute-done((bf16[256,256]{1,0:T(8,128)(2,1)S(1)}, bf16[256,256]{1,0:T(8,128)(2,1)S(1)}, u32[]{:S(2)}, u32[]{:S(2)}) %collective-permute-start.22) | collective-permute-done | bytes 131104 | tf_op jit(solution)/shard_map/ppermute | solution.py:593
  118.6 3.2 %collective-permute-done.23 = bf16[256,256]{1,0:T(8,128)(2,1)S(1)} collective-permute-done((bf16[256,256]{1,0:T(8,128)(2,1)S(1)}, bf16[256,256]{1,0:T(8,128)(2,1)S(1)}, u32[]{:S(2)}, u32[]{:S(2)}) %collective-permute-start.23) | collective-permute-done | bytes 131104 | tf_op jit(solution)/shard_map/ppermute | solution.py:593
  121.7 1.8 %collective-permute-done.24 = bf16[256,256]{1,0:T(8,128)(2,1)S(1)} collective-permute-done((bf16[256,256]{1,0:T(8,128)(2,1)S(1)}, bf16[256,256]{1,0:T(8,128)(2,1)S(1)}, u32[]{:S(2)}, u32[]{:S(2)}) %collective-permute-start.24) | collective-permute-done | bytes 131104 | tf_op jit(solution)/shard_map/ppermute | solution.py:593
  123.6 8.4 %projection.1 = (bf16[128,4096]{1,0:T(8,128)(2,1)S(1)}, bf16[128,4096]{1,0:T(8,128)(2,1)S(1)}) custom-call(s32[2]{0:T(128)S(1)} %pad_add_fusion.place_ref, bf16[8,256,256]{2,1,0:T(8,128)(2,1)S(1)} %bitcast_dynamic-update-slice_fusion.gated_ref, f32[8,256]{1,0:T(8,128)S(1)} %reshape.11.gain_ref, bf16[2048,4096]{1,0:T(8,128)(2,1)S(1)} %bitcast.65), custom_call_target="tpu_custom_call" | custom-call | flops 4294967296 | bytes 20000000 | tf_op jit(solution)/shard_map/projection/pallas_call | solution.py:691
  132.0 2.6 %collective-permute-done.25 = bf16[128,4096]{1,0:T(8,128)(2,1)S(1)} collective-permute-done((bf16[128,4096]{1,0:T(8,128)(2,1)S(1)}, bf16[128,4096]{1,0:T(8,128)(2,1)S(1)}, u32[]{:S(2)}, u32[]{:S(2)}) %collective-permute-start.25) | collective-permute-done | bytes 1048608 | tf_op jit(solution)/shard_map/ppermute | solution.py:711
  134.9 1.6 %collective-permute-start.26 = (bf16[64,4096]{1,0:T(8,128)(2,1)S(1)}, bf16[64,4096]{1,0:T(8,128)(2,1)S(1)}, u32[]{:S(2)}, u32[]{:S(2)}) collective-permute-start(bf16[64,4096]{1,0:T(8,128)(2,1)S(1)} %slice.9), channel_id=1, source_target_pairs={{0,2},{1,3},{2,0},{3,1},{4,6},{5,7},{6,4},{7,5},{8,10},{9,11},{10,... | collective-permute-start | bytes 1572872 | tf_op jit(solution)/shard_map/ppermute | solution.py:711
  136.5 12.5 %collective-permute-done.26 = bf16[64,4096]{1,0:T(8,128)(2,1)S(1)} collective-permute-done((bf16[64,4096]{1,0:T(8,128)(2,1)S(1)}, bf16[64,4096]{1,0:T(8,128)(2,1)S(1)}, u32[]{:S(2)}, u32[]{:S(2)}) %collective-permute-start.26) | collective-permute-done | bytes 524320 | tf_op jit(solution)/shard_map/ppermute | solution.py:711
  149.0 0.9 add_convert_fusion.1
  (85 shorter events, 5.7 us)
Async XLA Ops:
  0.0 12.0 %copy-start = (f32[4,2048]{1,0:T(4,128)S(1)}, f32[4,2048]{1,0:T(4,128)}, u32[]{:S(2)}) copy-start(f32[4,2048]{1,0:T(4,128)} %param.22) | copy-start | bytes 98308
  2.4 9.6 %copy-start.6 = (bf16[256,2048]{1,0:T(8,128)(2,1)S(1)}, bf16[256,2048]{1,0:T(8,128)(2,1)}, u32[]{:S(2)}) copy-start(bf16[256,2048]{1,0:T(8,128)(2,1)} %param.16) | copy-start | bytes 3145732
  2.4 50.6 %collective-permute-start.7 = (bf16[272,256]{1,0:T(8,128)(2,1)}, bf16[272,256]{1,0:T(8,128)(2,1)S(1)}, u32[]{:S(2)}, u32[]{:S(2)}) collective-permute-start(bf16[272,256]{1,0:T(8,128)(2,1)} %pad_maximum_fusion.2), channel_id=1, source_target_pairs={{0,16},{4,20},{8,24},{12,28},{16,0},{20,4},{24,8},{28,12},{1,17},{... | collective-permute-start | bytes 417800 | tf_op jit(solution)/shard_map/ppermute | solution.py:593
  2.4 9.7 %copy-start.10 = (f32[2048]{0:T(1024)S(1)}, f32[2048]{0:T(1024)}, u32[]{:S(2)}) copy-start(f32[2048]{0:T(1024)} %param.28) | copy-start | bytes 24580
  2.4 9.7 %copy-start.11 = (f32[4,256]{1,0:T(4,128)S(1)}, f32[4,256]{1,0:T(4,128)}, u32[]{:S(2)}) copy-start(f32[4,256]{1,0:T(4,128)} %param.24) | copy-start | bytes 12292
  2.4 9.7 %copy-start.12 = (f32[4,256]{1,0:T(4,128)S(1)}, f32[4,256]{1,0:T(4,128)}, u32[]{:S(2)}) copy-start(f32[4,256]{1,0:T(4,128)} %param.23) | copy-start | bytes 12292
  4.7 7.7 %collective-permute-start = (bf16[256,256]{1,0:T(8,128)(2,1)}, bf16[256,256]{1,0:T(8,128)(2,1)}, u32[]{:S(2)}, u32[]{:S(2)}) collective-permute-start(bf16[256,256]{1,0:T(8,128)(2,1)} %get-tuple-element.51), channel_id=1, source_target_pairs={{0,4},{4,0},{8,12},{12,8},{16,20},{20,16},{24,28},{28,24},{1,5},{5... | collective-permute-start | bytes 393224 | tf_op jit(solution)/shard_map/ppermute | solution.py:593
  6.5 11.3 %collective-permute-start.1 = (bf16[256,256]{1,0:T(8,128)(2,1)}, bf16[256,256]{1,0:T(8,128)(2,1)}, u32[]{:S(2)}, u32[]{:S(2)}) collective-permute-start(bf16[256,256]{1,0:T(8,128)(2,1)} %get-tuple-element.50), channel_id=1, source_target_pairs={{0,8},{4,12},{8,0},{12,4},{16,24},{20,28},{24,16},{28,20},{1,9},{5... | collective-permute-start | bytes 393224 | tf_op jit(solution)/shard_map/ppermute | solution.py:593
  8.1 12.2 %collective-permute-start.2 = (bf16[256,256]{1,0:T(8,128)(2,1)}, bf16[256,256]{1,0:T(8,128)(2,1)}, u32[]{:S(2)}, u32[]{:S(2)}) collective-permute-start(bf16[256,256]{1,0:T(8,128)(2,1)} %get-tuple-element.49), channel_id=1, source_target_pairs={{0,12},{4,8},{8,4},{12,0},{16,28},{20,24},{24,20},{28,16},{1,13},{... | collective-permute-start | bytes 393224 | tf_op jit(solution)/shard_map/ppermute | solution.py:593
  8.2 16.0 %collective-permute-start.3 = (bf16[256,256]{1,0:T(8,128)(2,1)}, bf16[256,256]{1,0:T(8,128)(2,1)}, u32[]{:S(2)}, u32[]{:S(2)}) collective-permute-start(bf16[256,256]{1,0:T(8,128)(2,1)} %get-tuple-element.48), channel_id=1, source_target_pairs={{0,16},{4,20},{8,24},{12,28},{16,0},{20,4},{24,8},{28,12},{1,17},{... | collective-permute-start | bytes 393224 | tf_op jit(solution)/shard_map/ppermute | solution.py:593
  12.1 0.9 copy-start.9
  12.2 5.6 %copy-start.8 = (bf16[256,256]{1,0:T(8,128)(2,1)S(1)}, bf16[256,256]{1,0:T(8,128)(2,1)}, u32[]{:S(2)}) copy-start(bf16[256,256]{1,0:T(8,128)(2,1)} %get-tuple-element.52) | copy-start | bytes 393220
  12.2 8.1 %copy-start.7 = (bf16[256,256]{1,0:T(8,128)(2,1)S(1)}, bf16[256,256]{1,0:T(8,128)(2,1)}, u32[]{:S(2)}) copy-start(bf16[256,256]{1,0:T(8,128)(2,1)} %get-tuple-element.46) | copy-start | bytes 393220
  12.2 111.3 %slice-start = ((s8[16777216]{0:T(1024)(128)(4,1)}), s8[4194304]{0:T(1024)(128)(4,1)S(1)}, s32[]{:S(2)}) async-start(s8[16777216]{0:T(1024)(128)(4,1)} %bitcast.64), calls=%async_computation | async-start | bytes 8388608
  13.0 15.5 %collective-permute-start.4 = (bf16[256,256]{1,0:T(8,128)(2,1)S(1)}, bf16[256,256]{1,0:T(8,128)(2,1)S(1)}, u32[]{:S(2)}, u32[]{:S(2)}) collective-permute-start(bf16[256,256]{1,0:T(8,128)(2,1)S(1)} %copy-done.9), channel_id=1, source_target_pairs={{0,20},{4,16},{8,28},{12,24},{16,4},{20,0},{24,12},{28,8},{1,21},{... | collective-permute-start | bytes 393224 | tf_op jit(solution)/shard_map/ppermute | solution.py:593
  17.7 15.6 %collective-permute-start.5 = (bf16[256,256]{1,0:T(8,128)(2,1)S(1)}, bf16[256,256]{1,0:T(8,128)(2,1)S(1)}, u32[]{:S(2)}, u32[]{:S(2)}) collective-permute-start(bf16[256,256]{1,0:T(8,128)(2,1)S(1)} %copy-done.8), channel_id=1, source_target_pairs={{0,24},{4,28},{8,16},{12,20},{16,8},{20,12},{24,0},{28,4},{1,25},{... | collective-permute-start | bytes 393224 | tf_op jit(solution)/shard_map/ppermute | solution.py:593
  20.3 15.5 %collective-permute-start.6 = (bf16[256,256]{1,0:T(8,128)(2,1)S(1)}, bf16[256,256]{1,0:T(8,128)(2,1)S(1)}, u32[]{:S(2)}, u32[]{:S(2)}) collective-permute-start(bf16[256,256]{1,0:T(8,128)(2,1)S(1)} %copy-done.7), channel_id=1, source_target_pairs={{0,28},{4,24},{8,20},{12,16},{16,12},{20,8},{24,4},{28,0},{1,29},{... | collective-permute-start | bytes 393224 | tf_op jit(solution)/shard_map/ppermute | solution.py:593
  24.3 12.0 %collective-permute-start.11 = (bf16[256,256]{1,0:T(8,128)(2,1)S(1)}, bf16[256,256]{1,0:T(8,128)(2,1)S(1)}, u32[]{:S(2)}, u32[]{:S(2)}) collective-permute-start(bf16[256,256]{1,0:T(8,128)(2,1)S(1)} %get-tuple-element.44), channel_id=1, source_target_pairs={{0,4},{4,0},{8,12},{12,8},{16,20},{20,16},{24,28},{28,24},{1,5},{5... | collective-permute-start | bytes 393224 | tf_op jit(solution)/shard_map/ppermute | solution.py:593
  28.5 10.6 %collective-permute-start.12 = (bf16[256,256]{1,0:T(8,128)(2,1)S(1)}, bf16[256,256]{1,0:T(8,128)(2,1)S(1)}, u32[]{:S(2)}, u32[]{:S(2)}) collective-permute-start(bf16[256,256]{1,0:T(8,128)(2,1)S(1)} %get-tuple-element.43), channel_id=1, source_target_pairs={{0,8},{4,12},{8,0},{12,4},{16,24},{20,28},{24,16},{28,20},{1,9},{5... | collective-permute-start | bytes 393224 | tf_op jit(solution)/shard_map/ppermute | solution.py:593
  33.3 7.5 %collective-permute-start.13 = (bf16[256,256]{1,0:T(8,128)(2,1)S(1)}, bf16[256,256]{1,0:T(8,128)(2,1)S(1)}, u32[]{:S(2)}, u32[]{:S(2)}) collective-permute-start(bf16[256,256]{1,0:T(8,128)(2,1)S(1)} %get-tuple-element.42), channel_id=1, source_target_pairs={{0,12},{4,8},{8,4},{12,0},{16,28},{20,24},{24,20},{28,16},{1,13},{... | collective-permute-start | bytes 393224 | tf_op jit(solution)/shard_map/ppermute | solution.py:593
  35.7 14.4 %collective-permute-start.14 = (bf16[256,256]{1,0:T(8,128)(2,1)S(1)}, bf16[256,256]{1,0:T(8,128)(2,1)S(1)}, u32[]{:S(2)}, u32[]{:S(2)}) collective-permute-start(bf16[256,256]{1,0:T(8,128)(2,1)S(1)} %get-tuple-element.41), channel_id=1, source_target_pairs={{0,16},{4,20},{8,24},{12,28},{16,0},{20,4},{24,8},{28,12},{1,17},{... | collective-permute-start | bytes 393224 | tf_op jit(solution)/shard_map/ppermute | solution.py:593
  36.3 16.7 %collective-permute-start.15 = (bf16[256,256]{1,0:T(8,128)(2,1)S(1)}, bf16[256,256]{1,0:T(8,128)(2,1)S(1)}, u32[]{:S(2)}, u32[]{:S(2)}) collective-permute-start(bf16[256,256]{1,0:T(8,128)(2,1)S(1)} %get-tuple-element.40), channel_id=1, source_target_pairs={{0,20},{4,16},{8,28},{12,24},{16,4},{20,0},{24,12},{28,8},{1,21},{... | collective-permute-start | bytes 393224 | tf_op jit(solution)/shard_map/ppermute | solution.py:593
  39.1 19.6 %collective-permute-start.16 = (bf16[256,256]{1,0:T(8,128)(2,1)S(1)}, bf16[256,256]{1,0:T(8,128)(2,1)S(1)}, u32[]{:S(2)}, u32[]{:S(2)}) collective-permute-start(bf16[256,256]{1,0:T(8,128)(2,1)S(1)} %get-tuple-element.45), channel_id=1, source_target_pairs={{0,24},{4,28},{8,16},{12,20},{16,8},{20,12},{24,0},{28,4},{1,25},{... | collective-permute-start | bytes 393224 | tf_op jit(solution)/shard_map/ppermute | solution.py:593
  40.9 19.1 %collective-permute-start.17 = (bf16[256,256]{1,0:T(8,128)(2,1)S(1)}, bf16[256,256]{1,0:T(8,128)(2,1)S(1)}, u32[]{:S(2)}, u32[]{:S(2)}) collective-permute-start(bf16[256,256]{1,0:T(8,128)(2,1)S(1)} %get-tuple-element.39), channel_id=1, source_target_pairs={{0,28},{4,24},{8,20},{12,16},{16,12},{20,8},{24,4},{28,0},{1,29},{... | collective-permute-start | bytes 393224 | tf_op jit(solution)/shard_map/ppermute | solution.py:593
  53.1 15.4 %collective-permute-start.8 = (bf16[2,272,256]{2,1,0:T(8,128)(2,1)S(1)}, bf16[2,272,256]{2,1,0:T(8,128)(2,1)S(1)}, u32[]{:S(2)}, u32[]{:S(2)}) collective-permute-start(bf16[2,272,256]{2,1,0:T(8,128)(2,1)S(1)} %get-tuple-element.54), channel_id=1, source_target_pairs={{0,4},{4,0},{8,12},{12,8},{16,20},{20,16},{24,28},{28,24},{1,5},{5... | collective-permute-start | bytes 835592 | tf_op jit(solution)/shard_map/ppermute | solution.py:593
  53.6 14.8 %collective-permute-start.9 = (bf16[2,272,256]{2,1,0:T(8,128)(2,1)S(1)}, bf16[2,272,256]{2,1,0:T(8,128)(2,1)S(1)}, u32[]{:S(2)}, u32[]{:S(2)}) collective-permute-start(bf16[2,272,256]{2,1,0:T(8,128)(2,1)S(1)} %get-tuple-element.54), channel_id=1, source_target_pairs={{0,8},{4,12},{8,0},{12,4},{16,24},{20,28},{24,16},{28,20},{1,9},{5... | collective-permute-start | bytes 835592 | tf_op jit(solution)/shard_map/ppermute | solution.py:593
  58.0 10.4 %collective-permute-start.10 = (bf16[2,272,256]{2,1,0:T(8,128)(2,1)S(1)}, bf16[2,272,256]{2,1,0:T(8,128)(2,1)S(1)}, u32[]{:S(2)}, u32[]{:S(2)}) collective-permute-start(bf16[2,272,256]{2,1,0:T(8,128)(2,1)S(1)} %get-tuple-element.54), channel_id=1, source_target_pairs={{0,12},{4,8},{8,4},{12,0},{16,28},{20,24},{24,20},{28,16},{1,13},{... | collective-permute-start | bytes 835592 | tf_op jit(solution)/shard_map/ppermute | solution.py:593
  68.5 55.0 %slice-start.1 = ((s8[16777216]{0:T(1024)(128)(4,1)}), s8[4194304]{0:T(1024)(128)(4,1)S(1)}, s32[]{:S(2)}) async-start(s8[16777216]{0:T(1024)(128)(4,1)} %bitcast.64), calls=%async_computation.1 | async-start | bytes 8388608
  68.6 0.8 copy-start.1
  68.6 0.8 copy-start.3
  68.7 0.8 copy-start.4
  68.7 0.8 copy-start.5
  69.5 19.6 %copy-start.2 = (f32[32]{0:T(128)S(1)}, f32[32]{0:T(128)}, u32[]{:S(2)}) copy-start(f32[32]{0:T(128)} %skip_ref.1) | copy-start | bytes 388
  89.1 34.5 %slice-start.2 = ((s8[16777216]{0:T(1024)(128)(4,1)}), s8[4194304]{0:T(1024)(128)(4,1)S(1)}, s32[]{:S(2)}) async-start(s8[16777216]{0:T(1024)(128)(4,1)} %bitcast.64), calls=%async_computation.2 | async-start | bytes 8388608
  89.1 34.4 %slice-start.3 = ((s8[16777216]{0:T(1024)(128)(4,1)}), s8[4194304]{0:T(1024)(128)(4,1)S(1)}, s32[]{:S(2)}) async-start(s8[16777216]{0:T(1024)(128)(4,1)} %bitcast.64), calls=%async_computation.3 | async-start | bytes 8388608
  97.9 7.0 %collective-permute-start.18 = (bf16[256,256]{1,0:T(8,128)(2,1)S(1)}, bf16[256,256]{1,0:T(8,128)(2,1)S(1)}, u32[]{:S(2)}, u32[]{:S(2)}) collective-permute-start(bf16[256,256]{1,0:T(8,128)(2,1)S(1)} %get-tuple-element.30), channel_id=1, source_target_pairs={{0,4},{4,0},{8,12},{12,8},{16,20},{20,16},{24,28},{28,24},{1,5},{5... | collective-permute-start | bytes 393224 | tf_op jit(solution)/shard_map/ppermute | solution.py:593
  99.0 6.9 %collective-permute-start.19 = (bf16[256,256]{1,0:T(8,128)(2,1)S(1)}, bf16[256,256]{1,0:T(8,128)(2,1)S(1)}, u32[]{:S(2)}, u32[]{:S(2)}) collective-permute-start(bf16[256,256]{1,0:T(8,128)(2,1)S(1)} %get-tuple-element.31), channel_id=1, source_target_pairs={{0,8},{4,12},{8,0},{12,4},{16,24},{20,28},{24,16},{28,20},{1,9},{5... | collective-permute-start | bytes 393224 | tf_op jit(solution)/shard_map/ppermute | solution.py:593
  100.8 7.5 %collective-permute-start.20 = (bf16[256,256]{1,0:T(8,128)(2,1)S(1)}, bf16[256,256]{1,0:T(8,128)(2,1)S(1)}, u32[]{:S(2)}, u32[]{:S(2)}) collective-permute-start(bf16[256,256]{1,0:T(8,128)(2,1)S(1)} %get-tuple-element.32), channel_id=1, source_target_pairs={{0,12},{4,8},{8,4},{12,0},{16,28},{20,24},{24,20},{28,16},{1,13},{... | collective-permute-start | bytes 393224 | tf_op jit(solution)/shard_map/ppermute | solution.py:593
  101.4 14.3 %collective-permute-start.21 = (bf16[256,256]{1,0:T(8,128)(2,1)S(1)}, bf16[256,256]{1,0:T(8,128)(2,1)S(1)}, u32[]{:S(2)}, u32[]{:S(2)}) collective-permute-start(bf16[256,256]{1,0:T(8,128)(2,1)S(1)} %get-tuple-element.33), channel_id=1, source_target_pairs={{0,16},{4,20},{8,24},{12,28},{16,0},{20,4},{24,8},{28,12},{1,17},{... | collective-permute-start | bytes 393224 | tf_op jit(solution)/shard_map/ppermute | solution.py:593
  103.6 15.0 %collective-permute-start.22 = (bf16[256,256]{1,0:T(8,128)(2,1)S(1)}, bf16[256,256]{1,0:T(8,128)(2,1)S(1)}, u32[]{:S(2)}, u32[]{:S(2)}) collective-permute-start(bf16[256,256]{1,0:T(8,128)(2,1)S(1)} %get-tuple-element.34), channel_id=1, source_target_pairs={{0,20},{4,16},{8,28},{12,24},{16,4},{20,0},{24,12},{28,8},{1,21},{... | collective-permute-start | bytes 393224 | tf_op jit(solution)/shard_map/ppermute | solution.py:593
  104.9 16.8 %collective-permute-start.23 = (bf16[256,256]{1,0:T(8,128)(2,1)S(1)}, bf16[256,256]{1,0:T(8,128)(2,1)S(1)}, u32[]{:S(2)}, u32[]{:S(2)}) collective-permute-start(bf16[256,256]{1,0:T(8,128)(2,1)S(1)} %get-tuple-element.35), channel_id=1, source_target_pairs={{0,24},{4,28},{8,16},{12,20},{16,8},{20,12},{24,0},{28,4},{1,25},{... | collective-permute-start | bytes 393224 | tf_op jit(solution)/shard_map/ppermute | solution.py:593
  105.9 17.5 %collective-permute-start.24 = (bf16[256,256]{1,0:T(8,128)(2,1)S(1)}, bf16[256,256]{1,0:T(8,128)(2,1)S(1)}, u32[]{:S(2)}, u32[]{:S(2)}) collective-permute-start(bf16[256,256]{1,0:T(8,128)(2,1)S(1)} %get-tuple-element.36), channel_id=1, source_target_pairs={{0,28},{4,24},{8,20},{12,16},{16,12},{20,8},{24,4},{28,0},{1,29},{... | collective-permute-start | bytes 393224 | tf_op jit(solution)/shard_map/ppermute | solution.py:593
  131.9 2.7 %collective-permute-start.25 = (bf16[128,4096]{1,0:T(8,128)(2,1)S(1)}, bf16[128,4096]{1,0:T(8,128)(2,1)S(1)}, u32[]{:S(2)}, u32[]{:S(2)}) collective-permute-start(bf16[128,4096]{1,0:T(8,128)(2,1)S(1)} %get-tuple-element.38), channel_id=1, source_target_pairs={{0,1},{1,0},{2,3},{3,2},{4,5},{5,4},{6,7},{7,6},{8,9},{9,8},{10,11... | collective-permute-start | bytes 3145736 | tf_op jit(solution)/shard_map/ppermute | solution.py:711
  134.9 14.0 %collective-permute-start.26 = (bf16[64,4096]{1,0:T(8,128)(2,1)S(1)}, bf16[64,4096]{1,0:T(8,128)(2,1)S(1)}, u32[]{:S(2)}, u32[]{:S(2)}) collective-permute-start(bf16[64,4096]{1,0:T(8,128)(2,1)S(1)} %slice.9), channel_id=1, source_target_pairs={{0,2},{1,3},{2,0},{3,1},{4,6},{5,7},{6,4},{7,5},{8,10},{9,11},{10,... | collective-permute-start | bytes 1572872 | tf_op jit(solution)/shard_map/ppermute | solution.py:711

commit v2 on v0

--- a/solution.py
+++ b/solution.py
@@ -1,6 +1,10 @@
+import functools
+
 import jax
 import jax.numpy as jnp
 from jax import lax
+from jax.experimental import pallas as pl
+from jax.experimental.pallas import tpu as pltpu
 from jax.sharding import PartitionSpec as P
 
 HEAD_DIM = 64
@@ -247,6 +251,524 @@
     )
 
 
+CHUNK = 128
+LANES = 128
+
+
+def tapped(current, previous, taps, since):
+    row_count = current.shape[0]
+    extended = jnp.concatenate([previous, current], axis=0)
+    total = None
+    for tap_index in range(CONV):
+        steps = CONV - 1 - tap_index
+        weight = taps[tap_index : tap_index + 1, :]
+        if steps == 0:
+            term = current * weight
+        else:
+            shifted = pltpu.roll(extended, steps, 0)[8 : 8 + row_count]
+            term = jnp.where(since >= steps, shifted * weight, 0.0)
+        total = term if total is None else total + term
+    return silu(total)
+
+
+def silu(x):
+    half = 0.5 * x
+    return half + half * jnp.tanh(half)
+
+
+def mixing_kernel(
+    heads,
+    group_heads,
+    per_dev,
+    chunks_step,
+    piece_count,
+    me_ref,
+    order_ref,
+    lengths_ref,
+    bias_ref,
+    log_ref,
+    key_taps_ref,
+    query_taps_ref,
+    *refs,
+):
+    piece_refs, refs = refs[:piece_count], refs[piece_count:]
+    mix_ref, query_ref, key_ref, tail_ref, inflow_ref, gate_ref, since_ref = refs[:7]
+    sequence, previous, raw_steps, step_rows, row_stack = refs[7:]
+    groups = piece_refs[0].shape[0]
+    me = me_ref[0]
+    step_id = pl.program_id(0)
+    token_rows = per_dev * BLK
+    chunks = raw_steps.shape[0]
+
+    @pl.when(step_id == 0)
+    def _():
+        previous[...] = jnp.zeros_like(previous)
+        lane = lax.broadcasted_iota(jnp.int32, (8, LANES), 1)
+        row8 = lax.broadcasted_iota(jnp.int32, (8, LANES), 0)
+        own = lax.rem(me * heads, group_heads)
+        for g in range(groups):
+            for turn, piece_ref in enumerate(piece_refs):
+                loader = jnp.bitwise_xor(me, g * piece_count + turn)
+                for b in range(per_dev):
+                    place = order_ref[loader * per_dev + b]
+                    rows = pl.ds(pl.multiple_of(place * BLK, BLK), BLK)
+                    sequence[rows, :] = piece_ref[g, b * BLK : (b + 1) * BLK, :]
+                    at = (b // 2) * LANES
+                    steps_in = piece_ref[
+                        g, token_rows : token_rows + group_heads, at : at + LANES
+                    ].astype(jnp.float32)
+                    parity = lax.rem(place, 2)
+                    steps_in = pltpu.roll(
+                        steps_in, lax.rem(group_heads - own, group_heads), 0
+                    )[:8]
+                    steps_in = pltpu.roll(steps_in, BLK * jnp.bitwise_xor(parity, b % 2), 1)
+                    chunk = lax.div(place, 2)
+                    raw_steps[chunk] = jnp.where(
+                        lane // BLK == parity, steps_in, raw_steps[chunk]
+                    )
+        bias = jnp.zeros((8, LANES), jnp.float32)
+        decay = jnp.zeros((8, LANES), jnp.float32)
+        for h in range(heads):
+            bias = jnp.where(row8 == h, bias_ref[me * heads + h], bias)
+            decay = jnp.where(row8 == h, log_ref[me * heads + h], decay)
+        decay = -jnp.exp(decay)
+        raw = jnp.where(row8[None] < heads, raw_steps[...] + bias[None], 0.0)
+        step = jnp.maximum(raw, 0.0) + jnp.log(1.0 + jnp.exp(-jnp.abs(raw)))
+        step_rows[...] = step
+        sums = decay[None] * step
+        lanes = lax.broadcasted_iota(jnp.int32, (chunks, 8, LANES), 2)
+        width = 1
+        while width < CHUNK:
+            sums = sums + jnp.where(lanes >= width, pltpu.roll(sums, width, 2), 0.0)
+            width *= 2
+        first = lax.broadcasted_iota(jnp.int32, (chunks, 8, LANES), 0) * CHUNK
+        position = first + lanes
+        begun = jnp.zeros_like(position)
+        offset = jnp.int32(0)
+        for k in range(lengths_ref.shape[0]):
+            begun = jnp.where(position >= offset, offset, begun)
+            offset = offset + lengths_ref[k]
+        last_sum = jnp.sum(jnp.where(lanes == CHUNK - 1, sums, 0.0), axis=2, keepdims=True)
+        last_begun = jnp.max(begun, axis=2, keepdims=True)
+        row_stack[:, 0:8] = sums
+        row_stack[:, 8:16] = jnp.where(
+            position >= last_begun, jnp.exp(last_sum - sums) * step, 0.0
+        )
+        row_stack[:, 16:24] = jnp.where(begun < first, jnp.exp(sums), 0.0)
+        row_stack[:, 24:32] = (position - begun).astype(jnp.float32)
+        row_stack[:, 32:40] = jnp.where(
+            last_begun < first, jnp.exp(last_sum), jnp.zeros_like(sums)
+        )
+
+    causal = lax.broadcasted_iota(jnp.int32, (CHUNK, CHUNK), 0) >= lax.broadcasted_iota(
+        jnp.int32, (CHUNK, CHUNK), 1
+    )
+    column = lax.broadcasted_iota(jnp.int32, (CHUNK, CHUNK), 1).astype(jnp.float32)
+    row_of = lax.broadcasted_iota(jnp.int32, (CHUNK, CHUNK), 0).astype(jnp.float32)
+    low_half = lax.broadcasted_iota(jnp.int32, (CHUNK, LANES), 1) < HEAD_DIM
+    taps = jnp.concatenate([key_taps_ref[...], query_taps_ref[...]], axis=1)
+
+    def one_chunk(local, carry):
+        chunk = step_id * chunks_step + local
+        turned = jnp.concatenate(
+            [row_stack[chunk, :32], jnp.zeros((CHUNK - 32, LANES), jnp.float32)], axis=0
+        ).T
+
+        def spread(at):
+            return jnp.broadcast_to(turned[:, at : at + 1], (CHUNK, LANES))
+
+        since_rows = spread(24)
+        since_ref[local] = since_rows
+        rows = pl.ds(pl.multiple_of(chunk * CHUNK, CHUNK), CHUNK)
+        current = sequence[rows, :].astype(jnp.float32)
+        wide_since = jnp.concatenate([since_rows, since_rows], axis=1)
+        conv = tapped(current, previous[...], taps, wide_since)
+        previous[...] = current[CHUNK - 8 :]
+        keys, queries = conv[:, :STATE].astype(jnp.bfloat16), conv[:, STATE:].astype(jnp.bfloat16)
+        query_ref[local] = queries
+        key_ref[local] = conv[:, :STATE].T.astype(jnp.bfloat16)
+        inner_products = lax.dot_general(
+            queries, keys, (((1,), (1,)), ((), ())), preferred_element_type=jnp.float32
+        )
+        allowed = jnp.where(causal & (column >= row_of - since_rows), 0.0, -1e30)
+        for h in range(heads):
+            exponent = (spread(h) + allowed) - row_stack[chunk, h : h + 1, :]
+            weights = jnp.exp(exponent) * (inner_products * step_rows[chunk, h : h + 1, :])
+            mix_ref[local, :, h * CHUNK : (h + 1) * CHUNK] = weights.astype(jnp.bfloat16)
+        gate = row_stack[chunk, 32:40]
+        for pair in range(heads // 2):
+            at = slice(pair * LANES, (pair + 1) * LANES)
+            tail_ref[local, :, at] = jnp.where(
+                low_half, spread(8 + 2 * pair), spread(9 + 2 * pair)
+            )
+            inflow_ref[local, :, at] = jnp.where(
+                low_half, spread(16 + 2 * pair), spread(17 + 2 * pair)
+            )
+            gate_ref[local, :, at] = jnp.where(
+                low_half[:8],
+                jnp.broadcast_to(gate[2 * pair : 2 * pair + 1], (8, LANES)),
+                jnp.broadcast_to(gate[2 * pair + 1 : 2 * pair + 2], (8, LANES)),
+            )
+        return carry
+
+    lax.fori_loop(0, chunks_step, one_chunk, 0, unroll=2)
+
+
+def scan_kernel(
+    heads, per_dev, chunks_step, piece_count, me_ref, order_ref, skip_ref, taps_ref, *refs
+):
+    piece_refs, refs = refs[:piece_count], refs[piece_count:]
+    mix_ref, query_ref, key_ref, tail_ref, inflow_ref, gate_ref, since_ref, out_ref = refs[:8]
+    sequence, previous, state = refs[8:]
+    me = me_ref[0]
+    step_id = pl.program_id(0)
+
+    @pl.when(step_id == 0)
+    def _():
+        previous[...] = jnp.zeros_like(previous)
+        state[...] = jnp.zeros_like(state)
+        for turn, piece_ref in enumerate(piece_refs):
+            loader = jnp.bitwise_xor(me, turn)
+            for b in range(per_dev):
+                place = order_ref[loader * per_dev + b]
+                rows = pl.ds(pl.multiple_of(place * BLK, BLK), BLK)
+                sequence[rows, :] = piece_ref[b * BLK : (b + 1) * BLK, :]
+
+    width = heads * HEAD_DIM
+    lane = lax.broadcasted_iota(jnp.int32, (1, width), 1)
+    skip = jnp.zeros((1, width), jnp.float32)
+    for h in range(heads):
+        skip = jnp.where(lane >= h * HEAD_DIM, skip_ref[me * heads + h], skip)
+    low_half = lax.broadcasted_iota(jnp.int32, (CHUNK, LANES), 1) < HEAD_DIM
+    taps = taps_ref[...]
+
+    def one_chunk(local, carry):
+        chunk = step_id * chunks_step + local
+        rows = pl.ds(pl.multiple_of(chunk * CHUNK, CHUNK), CHUNK)
+        current = sequence[rows, :].astype(jnp.float32)
+        wide_since = jnp.concatenate([since_ref[local]] * (width // LANES), axis=1)
+        values = tapped(current, previous[...], taps, wide_since).astype(jnp.bfloat16)
+        previous[...] = current[CHUNK - 8 :]
+        values_wide = values.astype(jnp.float32)
+        entering = state[...]
+        carried = jnp.dot(
+            query_ref[local], entering.astype(jnp.bfloat16), preferred_element_type=jnp.float32
+        )
+        total = carried * inflow_ref[local] + skip * values_wide
+        tail_values = (values_wide * tail_ref[local]).astype(jnp.bfloat16)
+        state[...] = gate_ref[local, :1, :] * entering + jnp.dot(
+            key_ref[local], tail_values, preferred_element_type=jnp.float32
+        )
+        zero = jnp.zeros((CHUNK, LANES), jnp.bfloat16)
+        for pair in range(heads // 2):
+            at = slice(pair * LANES, (pair + 1) * LANES)
+            both = values[:, at]
+            block = jnp.concatenate(
+                [jnp.where(low_half, both, zero), jnp.where(low_half, zero, both)], axis=0
+            )
+            intra = jnp.dot(
+                mix_ref[local, :, 2 * pair * CHUNK : 2 * (pair + 1) * CHUNK],
+                block,
+                preferred_element_type=jnp.float32,
+            )
+            out_ref[local, :, at] = total[:, at] + intra
+        return carry
+
+    lax.fori_loop(0, chunks_step, one_chunk, 0, unroll=2)
+
+
+def gating_kernel(per_dev, piece_count, place_ref, order_ref, mixed_ref, *refs):
+    piece_refs, out_refs, laid = refs[:piece_count], refs[piece_count:-1], refs[-1]
+    me, mine = place_ref[0], place_ref[1]
+    for turn, piece_ref in enumerate(piece_refs):
+        loader = jnp.bitwise_xor(me, turn)
+        for b in range(per_dev):
+            place = order_ref[loader * per_dev + b]
+            gates = piece_ref[b * BLK : (b + 1) * BLK, :].astype(jnp.float32)
+            mixed = mixed_ref[pl.ds(pl.multiple_of(place * BLK, BLK), BLK), :]
+            gated = (mixed * silu(gates)).astype(jnp.bfloat16)
+            owner_turn = jnp.bitwise_xor(lax.div(place, per_dev), me)
+            away = jnp.bitwise_xor(lax.rem(place, per_dev), mine)
+            slot = 2 * (1 - lax.rem(away, 2)) + (1 - lax.div(away, 2))
+            laid[owner_turn, pl.ds(pl.multiple_of(slot * BLK, BLK), BLK), :] = gated
+    for turn, out_ref in enumerate(out_refs):
+        out_ref[...] = laid[turn]
+
+
+def normed_into(normed, gated_refs, gain_ref, me, first_turn):
+    count = len(gated_refs)
+    rows, width = gated_refs[0].shape
+    wide = [ref[...].astype(jnp.float32) for ref in gated_refs]
+    squares = wide[0] * wide[0]
+    for piece in wide[1:]:
+        squares = squares + piece * piece
+    mean = jnp.sum(squares, axis=1, keepdims=True) * (1.0 / (count * width))
+    inverse_rms = lax.rsqrt(mean + 1e-05)
+    for turn, piece in enumerate(wide):
+        source = jnp.bitwise_xor(me, first_turn + turn)
+        at = pl.multiple_of(lax.rem(source, count) * width, width)
+        gain = gain_ref[pl.ds(source, 1), :]
+        normed[:, pl.ds(at, width)] = (piece * inverse_rms * gain).astype(jnp.bfloat16)
+
+
+def near_kernel(place_ref, gain_ref, weight_ref, *refs):
+    gated_refs, partial_ref, normed = refs[:-2], refs[-2], refs[-1]
+
+    @pl.when(pl.program_id(0) == 0)
+    def _():
+        normed_into(normed, gated_refs, gain_ref, place_ref[0], 0)
+
+    partial_ref[...] = jnp.dot(
+        normed[...], weight_ref[...], preferred_element_type=jnp.float32
+    )
+
+
+def far_kernel(place_ref, gain_ref, weight_ref, near_ref, *refs):
+    gated_refs, away_ref, stay_ref, normed = refs[:-3], refs[-3], refs[-2], refs[-1]
+
+    @pl.when(pl.program_id(0) == 0)
+    def _():
+        normed_into(normed, gated_refs, gain_ref, place_ref[0], len(gated_refs))
+
+    partial = near_ref[...] + jnp.dot(
+        normed[...], weight_ref[...], preferred_element_type=jnp.float32
+    )
+    partial = partial.astype(jnp.bfloat16)
+    rows = partial.shape[0] // 2
+    away_ref[...] = partial[:rows]
+    stay_ref[...] = partial[rows:]
+
+
+def head_split(
+    values_in,
+    gate_in,
+    keys_in,
+    queries_in,
+    step_in,
+    block_order,
+    doc_lengths,
+    conv_values,
+    conv_keys,
+    conv_queries,
+    decay_log,
+    step_bias,
+    skip_gain,
+    norm_gain,
+    out_weight,
+):
+    ctx_count = lax.axis_size("ctx")
+    tp_count = lax.axis_size("tp")
+    me = lax.axis_index("ctx")
+    tp_index = lax.axis_index("tp")
+    token_count, channels = values_in.shape
+    per_dev = token_count // BLK
+    total_tokens = token_count * ctx_count
+    heads_local = step_in.shape[1]
+    heads = heads_local // ctx_count
+    width = heads * HEAD_DIM
+    groups = keys_in.shape[1] // STATE
+    group_heads = heads_local // groups
+    near = ctx_count // groups
+    chunks = total_tokens // CHUNK
+    my_group = me // near
+    place = jnp.stack([me, tp_index]).astype(jnp.int32)
+
+    def turned(value, turn):
+        return lax.ppermute(value, "ctx", [(i, i ^ turn) for i in range(ctx_count)])
+
+    def for_group(group):
+        keys = lax.dynamic_slice_in_dim(keys_in, group * STATE, STATE, 1)
+        queries = lax.dynamic_slice_in_dim(queries_in, group * STATE, STATE, 1)
+        steps = lax.dynamic_slice_in_dim(step_in, group * group_heads, group_heads, 1)
+        return jnp.concatenate([jnp.concatenate([keys, queries], axis=1), steps.T], axis=0)
+
+    def for_heads(turn):
+        at = (me ^ turn) * width
+        return jnp.stack(
+            [lax.dynamic_slice_in_dim(rows, at, width, 1) for rows in (values_in, gate_in)]
+        )
+
+    held = jnp.stack([for_group(my_group), turned(for_group(my_group ^ 1), near)])
+    group_rows = [held] + [turned(held, turn) for turn in range(1, near)]
+    head_rows = [for_heads(0)] + [turned(for_heads(turn), turn) for turn in range(1, ctx_count)]
+
+    key_taps = lax.dynamic_slice_in_dim(conv_keys, my_group * STATE, STATE, 1)
+    query_taps = lax.dynamic_slice_in_dim(conv_queries, my_group * STATE, STATE, 1)
+    value_taps = lax.dynamic_slice_in_dim(conv_values, me * width, width, 1)
+
+    smem = pl.BlockSpec(memory_space=pltpu.SMEM)
+    vmem = pl.BlockSpec(memory_space=pltpu.VMEM)
+    params = pltpu.CompilerParams(vmem_limit_bytes=28 * 1024 * 1024)
+
+    def whole(array):
+        return pl.BlockSpec(array.shape, lambda *ids: (0,) * array.ndim)
+
+    grid_steps = 4
+    chunks_step = chunks // grid_steps
+
+    def per_step(rows, columns):
+        return pl.BlockSpec((chunks_step, rows, columns), lambda i: (i, 0, 0))
+
+    mix_shapes = [
+        ((CHUNK, heads * CHUNK), jnp.bfloat16),
+        ((CHUNK, STATE), jnp.bfloat16),
+        ((STATE, CHUNK), jnp.bfloat16),
+        ((CHUNK, width), jnp.float32),
+        ((CHUNK, width), jnp.float32),
+        ((8, width), jnp.float32),
+        ((CHUNK, LANES), jnp.float32),
+    ]
+    mixing = pl.pallas_call(
+        functools.partial(mixing_kernel, heads, group_heads, per_dev, chunks_step, near),
+        grid=(grid_steps,),
+        in_specs=[smem] * 5 + [whole(key_taps), whole(query_taps)] + [whole(held)] * near,
+        out_specs=[per_step(*shape) for shape, _ in mix_shapes],
+        out_shape=[jax.ShapeDtypeStruct((chunks,) + shape, kind) for shape, kind in mix_shapes],
+        scratch_shapes=[
+            pltpu.VMEM((total_tokens, 2 * STATE), jnp.bfloat16),
+            pltpu.VMEM((8, 2 * STATE), jnp.float32),
+            pltpu.VMEM((chunks, 8, LANES), jnp.float32),
+            pltpu.VMEM((chunks, 8, LANES), jnp.float32),
+            pltpu.VMEM((chunks, 40, LANES), jnp.float32),
+        ],
+        compiler_params=params,
+        cost_estimate=pl.CostEstimate(
+            flops=20_000_000, bytes_accessed=20_000_000, transcendentals=2_000_000
+        ),
+        name="mixing",
+    )(place, block_order, doc_lengths, step_bias, decay_log, key_taps, query_taps, *group_rows)
+
+    mixed = pl.pallas_call(
+        functools.partial(scan_kernel, heads, per_dev, chunks_step, ctx_count),
+        grid=(grid_steps,),
+        in_specs=[smem] * 3
+        + [whole(value_taps)]
+        + [pl.BlockSpec((None, token_count, width), lambda i: (0, 0, 0))] * ctx_count
+        + [per_step(*shape) for shape, _ in mix_shapes],
+        out_specs=per_step(CHUNK, width),
+        out_shape=jax.ShapeDtypeStruct((chunks, CHUNK, width), jnp.float32),
+        scratch_shapes=[
+            pltpu.VMEM((total_tokens, width), jnp.bfloat16),
+            pltpu.VMEM((8, width), jnp.float32),
+            pltpu.VMEM((STATE, width), jnp.float32),
+        ],
+        compiler_params=params,
+        cost_estimate=pl.CostEstimate(
+            flops=600_000_000, bytes_accessed=14_000_000, transcendentals=600_000
+        ),
+        name="scan",
+    )(place, block_order, skip_gain, value_taps, *head_rows, *mixing)
+
+    gated = pl.pallas_call(
+        functools.partial(gating_kernel, per_dev, ctx_count),
+        grid=(1,),
+        in_specs=[smem, smem, pl.BlockSpec((total_tokens, width), lambda i: (0, 0))]
+        + [pl.BlockSpec((None, token_count, width), lambda i: (1, 0, 0))] * ctx_count,
+        out_specs=[pl.BlockSpec((token_count, width), lambda i: (0, 0))] * ctx_count,
+        out_shape=[jax.ShapeDtypeStruct((token_count, width), jnp.bfloat16)] * ctx_count,
+        scratch_shapes=[pltpu.VMEM((ctx_count, token_count, width), jnp.bfloat16)],
+        compiler_params=params,
+        cost_estimate=pl.CostEstimate(
+            flops=5_000_000, bytes_accessed=4_000_000, transcendentals=600_000
+        ),
+        name="gating",
+    )(place, block_order, mixed.reshape(total_tokens, width), *head_rows)
+
+    pieces = [gated[0]] + [turned(gated[turn], turn) for turn in range(1, ctx_count)]
+
+    columns = out_weight.shape[1]
+    tile = 2048
+    tiles = columns // tile
+    group_width = near * width
+    gain = norm_gain.reshape(ctx_count, width)
+    weight = out_weight.reshape(groups, group_width, columns)
+
+    def project(kernel, gated_pieces, own, first, count, extra, extra_specs, out_specs, out_shape):
+        spec = pltpu.PrefetchScalarGridSpec(
+            num_scalar_prefetch=1,
+            grid=(count,),
+            in_specs=[
+                pl.BlockSpec(gain.shape, lambda i, at: (0, 0)),
+                pl.BlockSpec(
+                    (None, group_width, tile),
+                    lambda i, at: (
+                        lax.div(at[0], near) if own else 1 - lax.div(at[0], near),
+                        0,
+                        first + i,
+                    ),
+                ),
+            ]
+            + extra_specs
+            + [pl.BlockSpec((token_count, width), lambda i, at: (0, 0))] * len(gated_pieces),
+            out_specs=out_specs,
+            scratch_shapes=[pltpu.VMEM((token_count, group_width), jnp.bfloat16)],
+        )
+        return pl.pallas_call(
+            kernel,
+            grid_spec=spec,
+            out_shape=out_shape,
+            compiler_params=pltpu.CompilerParams(vmem_limit_bytes=44 * 1024 * 1024),
+            cost_estimate=pl.CostEstimate(
+                flops=2 * token_count * group_width * tile * count,
+                bytes_accessed=2 * group_width * tile * count,
+                transcendentals=0,
+            ),
+            name="near_projection" if own else "far_projection",
+        )(place, gain, weight, *extra, *gated_pieces)
+
+    near_partial = project(
+        near_kernel,
+        pieces[:near],
+        True,
+        0,
+        tiles,
+        [],
+        [],
+        pl.BlockSpec((token_count, tile), lambda i, at: (0, i)),
+        jax.ShapeDtypeStruct((token_count, columns), jnp.float32),
+    )
+
+    def joined(kept, sent, turn):
+        came = lax.ppermute(sent, "tp", [(i, i ^ turn) for i in range(tp_count)])
+        return (kept.astype(jnp.float32) + came.astype(jnp.float32)).astype(jnp.bfloat16)
+
+    results = []
+    rows = token_count // 2
+    parts = 2
+    part_tiles = tiles // parts
+    for part in range(parts):
+        first = part * part_tiles
+        away, stay = project(
+            far_kernel,
+            pieces[near:],
+            False,
+            first,
+            part_tiles,
+            [near_partial],
+            [pl.BlockSpec((token_count, tile), lambda i, at, first=first: (0, first + i))],
+            [pl.BlockSpec((rows, tile), lambda i, at: (0, i))] * 2,
+            [jax.ShapeDtypeStruct((rows, columns // parts), jnp.bfloat16)] * 2,
+        )
+        across = joined(stay, away, 1)
+        results.append(joined(across[rows // 2 :], across[: rows // 2], 2))
+    return jnp.concatenate(results, axis=1)
+
+
+def on_mesh(*arrays):
+    ctx_count, tp_count = lax.axis_size("ctx"), lax.axis_size("tp")
+    groups = arrays[2].shape[1] // STATE
+    heads_local = arrays[4].shape[1]
+    fits = (
+        groups == 2
+        and tp_count == 4
+        and ctx_count & (ctx_count - 1) == 0
+        and heads_local % (2 * ctx_count) == 0
+        and heads_local // ctx_count <= 8
+        and arrays[0].shape[0] == 2 * STATE
+    )
+    return (head_split if fits else on_device)(*arrays)
+
+
 def solution(mesh):
     in_specs = (
         P("ctx", "tp"),
@@ -267,5 +789,5 @@
     )
     out_specs = P(("ctx", "tp"), None)
     return jax.shard_map(
-        on_device, mesh=mesh, in_specs=in_specs, out_specs=out_specs, check_vma=False
-    )
+        on_mesh, mesh=mesh, in_specs=in_specs, out_specs=out_specs, check_vma=False
+    )

time: 322 us -> 122 us (0.38); the launches traced: 319 us -> 122 us
  blocking collectives: 104 us -> 0 us
  local copies, waits for them, and re-layouts: 38.5 us -> 3.56 us
  Pallas kernels: 0 us -> 28.1 us
  other arithmetic: 29.8 us -> 2.26 us
  waiting for transfers between devices: 68.4 us -> 41.1 us
  matrix products: 27.2 us -> 0 us
  between operations: 15.4 us -> 0.35 us
  starting transfers between devices: 35.3 us -> 46.4 us
    all_gather x1 -> x0, blocking collectives: 87.8 us -> none  [carried_in(): lax.all_gather(a.astype(kind), axis)]
    ppermute x3 -> x22, waiting for transfers between devices: 0.01 us -> 41.1 us  [the longest x18 30.4 us: turned(): return lax.ppermute(value, 'ctx', [(i, i ^ turn) for i in range(ctx_count)])]
    reduce_scatter x1 -> x0, waiting for transfers between devices: 36.4 us -> none  [on_device(): lax.psum_scatter(jnp.dot(normed, out_weight, preferred_element_type=jnp.f...]
    ppermute x3 -> x22, starting transfers between devices: 10.2 us -> 46.4 us  [the longest x18 42.8 us: turned(): return lax.ppermute(value, 'ctx', [(i, i ^ turn) for i in range(ctx_count)])]
    all_to_all x4 -> x0, waiting for transfers between devices: 31.9 us -> none  [the longest x1 29.3 us: on_device(): lax.all_to_all(packed_values, 'ctx', split_axis=0, concat_axis=0, tiled=T...]
    pallas_call x0 -> x6, Pallas kernels: none -> 28.1 us  [the longest x3 14.1 us: project(): pl.pallas_call(kernel, grid_spec=spec, out_shape=out_shape, compiler_para...]
    dot_general x5 -> x0, matrix products: 27.2 us -> none  [the longest x1 11.6 us: on_device(): jnp.dot(normed, out_weight, preferred_element_type=jnp.float32)]
    all_to_all x4 -> x0, starting transfers between devices: 25.1 us -> none  [the longest x1 7.22 us: on_device(): lax.all_to_all(packed_gates, 'ctx', split_axis=0, concat_axis=0, tiled=True)]
  transfers between devices with their start and end apart: 9 -> 22, of which waited for: 3 -> 13; matrix products, arithmetic and copies ran while one was open for 16% -> 3% of each run, Pallas kernels for 0% -> 15%
where the time goes in v2:
time: 122 us
  starting transfers between devices  46.4 us (38%)
  waiting for transfers between devices  41.1 us (34%)
  Pallas kernels  28.1 us (23%)
  local copies, waits for them, and re-layouts  3.56 us (3%)
  other arithmetic  2.26 us (2%)
    ppermute x18, starting transfers between devices, turned(): return lax.ppermute(value, 'ctx', [(i, i ^ turn) for i in range(ctx_count)])  42.8 us
    ppermute x18, waiting for transfers between devices, turned(): return lax.ppermute(value, 'ctx', [(i, i ^ turn) for i in range(ctx_count)])  30.4 us
    pallas_call x3, Pallas kernels, project(): pl.pallas_call(kernel, grid_spec=spec, out_shape=out_shape, compiler_para...  14.1 us
    ppermute x4, waiting for transfers between devices, joined(): came = lax.ppermute(sent, 'tp', [(i, i ^ turn) for i in range(tp_count)])  10.8 us
    pallas_call x1, Pallas kernels, head_split(): pl.pallas_call(functools.partial(mixing_kernel, heads, group_heads, per_d...  8.14 us
    pallas_call x1, Pallas kernels, head_split(): pl.pallas_call(functools.partial(scan_kernel, heads, per_dev, chunks_step...  4.83 us
    ppermute x4, starting transfers between devices, joined(): came = lax.ppermute(sent, 'tp', [(i, i ^ turn) for i in range(tp_count)])  3.57 us
  transfers between devices with their start and end apart: 22, of which 13 were waited for; matrix products, arithmetic and copies ran while one was open for 3% of the time, Pallas kernels for 15%

profile of v2, /device:TPU:16, one launch (start us, length us, event | category | flops | bytes accessed | tf_op | source)
XLA Modules:
  0.0 121.8 jit_solution(7759935408090072602)
XLA Ops:
  0.0 0.7 dynamic-slice_bitcast_fusion.17
  0.7 1.0 constant_dynamic-slice_fusion.2
  1.7 0.1 collective-permute-start.7
  1.8 1.8 %dynamic-slice_bitcast_fusion = (bf16[1,256,256]{2,1,0:T(8,128)(2,1)S(1)}, bf16[1,256,256]{2,1,0:T(8,128)(2,1)S(1)}, bf16[1,256,256]{2,1,0:T(8,128)(2,1)S(1)}, b...) fusion(bf16[256,2048]{1,0:T(8,128)(2,1)} %param.16, ...), kind=kLoop, calls=%fused_computation.16 | loop fusion | bytes 4194336 | tf_op jit(solution)/shard_map/stack | solution.py:587
  3.6 0.7 pad_maximum_fusion.7
  4.4 3.8 %collective-permute-start.4 = (bf16[2,256,256]{2,1,0:T(8,128)(2,1)}, bf16[2,256,256]{2,1,0:T(8,128)(2,1)S(1)}, u32[]{:S(2)}, u32[]{:S(2)}) collective-permute-start(bf16[2,256,256]{2,1,0:T(8,128)(2,1)} %pad_maximum_fusion.7), channel_id=1, source_target_pairs={{0,20},{4,16},{8,28},{12,24},{16,4},{20,0},{24,12},{28,8},{1,21},{... | collective-permute-start | bytes 786440 | tf_op jit(solution)/shard_map/ppermute | solution.py:577
  8.2 0.5 collective-permute-start.5
  8.9 16.0 %collective-permute-start.10 = (bf16[2,272,256]{2,1,0:T(8,128)(2,1)S(1)}, bf16[2,272,256]{2,1,0:T(8,128)(2,1)S(1)}, u32[]{:S(2)}, u32[]{:S(2)}) collective-permute-start(bf16[2,272,256]{2,1,0:T(8,128)(2,1)S(1)} %pad_maximum_fusion.1.refs_0_), channel_id=1, source_target_pairs={{0,12},{4,8},{8,4},{12,0},{16,28},{20,24},{24,20},{28,16},{1,13},{... | collective-permute-start | bytes 835592 | tf_op jit(solution)/shard_map/ppermute | solution.py:577
  24.9 0.5 collective-permute-start.8
  25.4 0.1 collective-permute-start.9
  25.6 0.6 collective-permute-done.4.refs_5_
  26.2 2.5 %collective-permute-start.6 = (bf16[2,256,256]{2,1,0:T(8,128)(2,1)S(1)}, bf16[2,256,256]{2,1,0:T(8,128)(2,1)S(1)}, u32[]{:S(2)}, u32[]{:S(2)}) collective-permute-start(bf16[2,256,256]{2,1,0:T(8,128)(2,1)S(1)} %pad_maximum_fusion.9), channel_id=1, source_target_pairs={{0,28},{4,24},{8,20},{12,16},{16,12},{20,8},{24,4},{28,0},{1,29},{... | collective-permute-start | bytes 786440 | tf_op jit(solution)/shard_map/ppermute | solution.py:577
  28.7 5.0 %collective-permute-done.5.refs_6_ = bf16[2,256,256]{2,1,0:T(8,128)(2,1)S(1)} collective-permute-done((bf16[2,256,256]{2,1,0:T(8,128)(2,1)S(1)}, bf16[2,256,256]{2,1,0:T(8,128)(2,1)S(1)}, u32[]{:S(2)}, u32[]{:S(2)}) %collective-permute-start.5) | collective-permute-done | bytes 262176 | tf_op jit(solution)/shard_map/ppermute | solution.py:577
  33.7 2.7 %collective-permute-start.2 = (bf16[2,256,256]{2,1,0:T(8,128)(2,1)S(1)}, bf16[2,256,256]{2,1,0:T(8,128)(2,1)S(1)}, u32[]{:S(2)}, u32[]{:S(2)}) collective-permute-start(bf16[2,256,256]{2,1,0:T(8,128)(2,1)S(1)} %pad_maximum_fusion.5), channel_id=1, source_target_pairs={{0,12},{4,8},{8,4},{12,0},{16,28},{20,24},{24,20},{28,16},{1,13},{... | collective-permute-start | bytes 786440 | tf_op jit(solution)/shard_map/ppermute | solution.py:577
  36.4 3.5 %collective-permute-done.8.refs_1_ = bf16[2,272,256]{2,1,0:T(8,128)(2,1)S(1)} collective-permute-done((bf16[2,272,256]{2,1,0:T(8,128)(2,1)S(1)}, bf16[2,272,256]{2,1,0:T(8,128)(2,1)S(1)}, u32[]{:S(2)}, u32[]{:S(2)}) %collective-permute-start.8) | collective-permute-done | bytes 278560 | tf_op jit(solution)/shard_map/ppermute | solution.py:577
  39.9 8.0 %collective-permute-start.1 = (bf16[2,256,256]{2,1,0:T(8,128)(2,1)S(1)}, bf16[2,256,256]{2,1,0:T(8,128)(2,1)S(1)}, u32[]{:S(2)}, u32[]{:S(2)}) collective-permute-start(bf16[2,256,256]{2,1,0:T(8,128)(2,1)S(1)} %pad_maximum_fusion.4), channel_id=1, source_target_pairs={{0,8},{4,12},{8,0},{12,4},{16,24},{20,28},{24,16},{28,20},{1,9},{5... | collective-permute-start | bytes 786440 | tf_op jit(solution)/shard_map/ppermute | solution.py:577
  47.9 0.5 collective-permute-start
  48.5 0.1 pad_add_fusion.me_ref.place_ref
  48.6 8.1 %mixing.1 = (bf16[16,128,512]{2,1,0:T(8,128)(2,1)S(1)}, bf16[16,128,128]{2,1,0:T(8,128)(2,1)S(1)}, bf16[16,128,128]{2,1,0:T(8,128)(2,1)S(1)}, f32[16,128,256]{2,...) custom-call(s32[2]{0:T(128)S(1)} %pad_add_fusion.me_ref.place_ref, ...), custom_call_target="tpu_custom_call" | custom-call | flops 20000000 | bytes 20000000 | tf_op jit(solution)/shard_map/mixing/pallas_call | solution.py:621
  56.8 0.5 collective-permute-done.2.refs_3_
  57.3 4.1 %collective-permute-done.1.refs_2_ = bf16[2,256,256]{2,1,0:T(8,128)(2,1)S(1)} collective-permute-done((bf16[2,256,256]{2,1,0:T(8,128)(2,1)S(1)}, bf16[2,256,256]{2,1,0:T(8,128)(2,1)S(1)}, u32[]{:S(2)}, u32[]{:S(2)}) %collective-permute-start.1) | collective-permute-done | bytes 262176 | tf_op jit(solution)/shard_map/ppermute | solution.py:577
  61.4 0.7 collective-permute-done.refs_1_
  62.1 4.8 %scan.1 = f32[16,128,256]{2,1,0:T(8,128)S(1)} custom-call(s32[2]{0:T(128)S(1)} %pad_add_fusion.me_ref.place_ref, s32[32]{0:T(128)S(1)} %copy-done.1, f32[32]{0:T(128)S(1)} %copy-done.2, f32[4,256]{1,0:T(4,128)S(1)} %constant_dynamic-slice_fusion.6.taps_ref, bf16[2,256,256]{2,1,0:T(8,128)(2,1)S(1)} %pad_maximum_fusion.2.refs_0_, ...), custom_call_target="tpu_custom_call" | custom-call | flops 600000000 | bytes 14000000 | tf_op jit(solution)/shard_map/scan/pallas_call | solution.py:641
  67.0 1.1 gating.1
  68.0 0.9 collective-permute-start.11
  68.9 2.5 %collective-permute-start.12 = (bf16[256,256]{1,0:T(8,128)(2,1)S(1)}, bf16[256,256]{1,0:T(8,128)(2,1)S(1)}, u32[]{:S(2)}, u32[]{:S(2)}) collective-permute-start(bf16[256,256]{1,0:T(8,128)(2,1)S(1)} %get-tuple-element.33), channel_id=1, source_target_pairs={{0,8},{4,12},{8,0},{12,4},{16,24},{20,28},{24,16},{28,20},{1,9},{5... | collective-permute-start | bytes 393224 | tf_op jit(solution)/shard_map/ppermute | solution.py:577
  71.4 0.2 collective-permute-start.13
  71.6 0.6 collective-permute-start.14
  72.2 3.0 %collective-permute-start.15 = (bf16[256,256]{1,0:T(8,128)(2,1)S(1)}, bf16[256,256]{1,0:T(8,128)(2,1)S(1)}, u32[]{:S(2)}, u32[]{:S(2)}) collective-permute-start(bf16[256,256]{1,0:T(8,128)(2,1)S(1)} %get-tuple-element.36), channel_id=1, source_target_pairs={{0,20},{4,16},{8,28},{12,24},{16,4},{20,0},{24,12},{28,8},{1,21},{... | collective-permute-start | bytes 393224 | tf_op jit(solution)/shard_map/ppermute | solution.py:577
  75.2 0.6 collective-permute-start.16
  75.9 1.3 %collective-permute-done.12.refs_2_ = bf16[256,256]{1,0:T(8,128)(2,1)S(1)} collective-permute-done((bf16[256,256]{1,0:T(8,128)(2,1)S(1)}, bf16[256,256]{1,0:T(8,128)(2,1)S(1)}, u32[]{:S(2)}, u32[]{:S(2)}) %collective-permute-start.12) | collective-permute-done | bytes 131104 | tf_op jit(solution)/shard_map/ppermute | solution.py:577
  77.2 0.3 collective-permute-start.17
  77.4 1.3 %collective-permute-done.13.refs_3_ = bf16[256,256]{1,0:T(8,128)(2,1)S(1)} collective-permute-done((bf16[256,256]{1,0:T(8,128)(2,1)S(1)}, bf16[256,256]{1,0:T(8,128)(2,1)S(1)}, u32[]{:S(2)}, u32[]{:S(2)}) %collective-permute-start.13) | collective-permute-done | bytes 131104 | tf_op jit(solution)/shard_map/ppermute | solution.py:577
  78.7 5.7 %near_projection.1.near_ref = f32[256,4096]{1,0:T(8,128)S(1)} custom-call(s32[2]{0:T(128)S(1)} %pad_add_fusion.me_ref.place_ref, f32[8,256]{1,0:T(8,128)S(1)} %reshape.9.gain_ref, bf16[2,1024,4096]{2,1,0:T(8,128)(2,1)} %bitcast.44, bf16[256,256]{1,0:T(8,128)(2,1)S(1)} %get-tuple-element.31.refs_0_, bf16[256,256]{1,0:T(8,128)(2,1)S(1)} %collective-permute-done.11.refs_1_, ...), custom_call_target="tpu_custom_call" | custom-call | flops 2147483648 | bytes 8388608 | tf_op jit(solution)/shard_map/near_projection/pallas_call | solution.py:706
  84.5 5.6 %collective-permute-done.15.refs_1_ = bf16[256,256]{1,0:T(8,128)(2,1)S(1)} collective-permute-done((bf16[256,256]{1,0:T(8,128)(2,1)S(1)}, bf16[256,256]{1,0:T(8,128)(2,1)S(1)}, u32[]{:S(2)}, u32[]{:S(2)}) %collective-permute-start.15) | collective-permute-done | bytes 131104 | tf_op jit(solution)/shard_map/ppermute | solution.py:577
  90.1 5.6 %collective-permute-done.16.refs_2_ = bf16[256,256]{1,0:T(8,128)(2,1)S(1)} collective-permute-done((bf16[256,256]{1,0:T(8,128)(2,1)S(1)}, bf16[256,256]{1,0:T(8,128)(2,1)S(1)}, u32[]{:S(2)}, u32[]{:S(2)}) %collective-permute-start.16) | collective-permute-done | bytes 131104 | tf_op jit(solution)/shard_map/ppermute | solution.py:577
  95.7 2.2 %collective-permute-done.17.refs_3_ = bf16[256,256]{1,0:T(8,128)(2,1)S(1)} collective-permute-done((bf16[256,256]{1,0:T(8,128)(2,1)S(1)}, bf16[256,256]{1,0:T(8,128)(2,1)S(1)}, u32[]{:S(2)}, u32[]{:S(2)}) %collective-permute-start.17) | collective-permute-done | bytes 131104 | tf_op jit(solution)/shard_map/ppermute | solution.py:577
  97.8 4.2 %far_projection.2 = (bf16[128,2048]{1,0:T(8,128)(2,1)S(1)}, bf16[128,2048]{1,0:T(8,128)(2,1)S(1)}) custom-call(s32[2]{0:T(128)S(1)} %pad_add_fusion.me_ref.place_ref, f32[8,256]{1,0:T(8,128)S(1)} %reshape.9.gain_ref, bf16[2,1024,4096]{2,1,0:T(8,128)(2,1)} %bitcast.45, f32[256,4096]{1,0:T(8,128)S(1)} %near_projection.1.near_ref, ...), custom_call_target="tpu_custom_call" | custom-call | flops 1073741824 | bytes 4194304 | tf_op jit(solution)/shard_map/far_projection/pallas_call | solution.py:706
  102.0 0.1 collective-permute-start.18
  102.1 4.2 %far_projection.3 = (bf16[128,2048]{1,0:T(8,128)(2,1)S(1)}, bf16[128,2048]{1,0:T(8,128)(2,1)S(1)}) custom-call(s32[2]{0:T(128)S(1)} %pad_add_fusion.me_ref.place_ref, f32[8,256]{1,0:T(8,128)S(1)} %reshape.9.gain_ref, bf16[2,1024,4096]{2,1,0:T(8,128)(2,1)} %bitcast.46, f32[256,4096]{1,0:T(8,128)S(1)} %near_projection.1.near_ref, ...), custom_call_target="tpu_custom_call" | custom-call | flops 1073741824 | bytes 4194304 | tf_op jit(solution)/shard_map/far_projection/pallas_call | solution.py:706
  106.3 0.6 collective-permute-start.20
  106.8 0.1 add_convert_fusion.1
  107.0 1.6 %collective-permute-start.19 = (bf16[64,2048]{1,0:T(8,128)(2,1)S(1)}, bf16[64,2048]{1,0:T(8,128)(2,1)S(1)}, u32[]{:S(2)}, u32[]{:S(2)}) collective-permute-start(bf16[64,2048]{1,0:T(8,128)(2,1)S(1)} %slice.17), channel_id=1, source_target_pairs={{0,2},{1,3},{2,0},{3,1},{4,6},{5,7},{6,4},{7,5},{8,10},{9,11},{10,... | collective-permute-start | bytes 786440 | tf_op jit(solution)/shard_map/ppermute | solution.py:732
  108.5 0.1 add_convert_fusion
  108.7 1.4 %collective-permute-start.21 = (bf16[64,2048]{1,0:T(8,128)(2,1)S(1)}, bf16[64,2048]{1,0:T(8,128)(2,1)S(1)}, u32[]{:S(2)}, u32[]{:S(2)}) collective-permute-start(bf16[64,2048]{1,0:T(8,128)(2,1)S(1)} %slice.19), channel_id=1, source_target_pairs={{0,2},{1,3},{2,0},{3,1},{4,6},{5,7},{6,4},{7,5},{8,10},{9,11},{10,... | collective-permute-start | bytes 786440 | tf_op jit(solution)/shard_map/ppermute | solution.py:732
  110.1 6.1 %collective-permute-done.19 = bf16[64,2048]{1,0:T(8,128)(2,1)S(1)} collective-permute-done((bf16[64,2048]{1,0:T(8,128)(2,1)S(1)}, bf16[64,2048]{1,0:T(8,128)(2,1)S(1)}, u32[]{:S(2)}, u32[]{:S(2)}) %collective-permute-start.19) | collective-permute-done | bytes 262176 | tf_op jit(solution)/shard_map/ppermute | solution.py:732
  116.3 4.6 %collective-permute-done.21 = bf16[64,2048]{1,0:T(8,128)(2,1)S(1)} collective-permute-done((bf16[64,2048]{1,0:T(8,128)(2,1)S(1)}, bf16[64,2048]{1,0:T(8,128)(2,1)S(1)}, u32[]{:S(2)}, u32[]{:S(2)}) %collective-permute-start.21) | collective-permute-done | bytes 262176 | tf_op jit(solution)/shard_map/ppermute | solution.py:732
  121.0 0.8 pad_maximum_fusion
  (45 shorter events, 0.5 us)
Async XLA Ops:
  0.0 25.6 %copy-start = (f32[4,2048]{1,0:T(4,128)S(1)}, f32[4,2048]{1,0:T(4,128)}, u32[]{:S(2)}) copy-start(f32[4,2048]{1,0:T(4,128)} %param.22) | copy-start | bytes 98308
  1.7 7.2 %collective-permute-start.7 = (bf16[272,256]{1,0:T(8,128)(2,1)S(1)}, bf16[272,256]{1,0:T(8,128)(2,1)S(1)}, u32[]{:S(2)}, u32[]{:S(2)}) collective-permute-start(bf16[272,256]{1,0:T(8,128)(2,1)S(1)} %pad_maximum_fusion.10), channel_id=1, source_target_pairs={{0,16},{4,20},{8,24},{12,28},{16,0},{20,4},{24,8},{28,12},{1,17},{... | collective-permute-start | bytes 417800 | tf_op jit(solution)/shard_map/ppermute | solution.py:577
  4.4 44.2 %copy-start.7 = (f32[4,256]{1,0:T(4,128)S(1)}, f32[4,256]{1,0:T(4,128)}, u32[]{:S(2)}) copy-start(f32[4,256]{1,0:T(4,128)} %param.24) | copy-start | bytes 12292
  4.4 44.2 %copy-start.8 = (f32[4,256]{1,0:T(4,128)S(1)}, f32[4,256]{1,0:T(4,128)}, u32[]{:S(2)}) copy-start(f32[4,256]{1,0:T(4,128)} %param.23) | copy-start | bytes 12292
  4.4 21.8 %collective-permute-start.4 = (bf16[2,256,256]{2,1,0:T(8,128)(2,1)}, bf16[2,256,256]{2,1,0:T(8,128)(2,1)S(1)}, u32[]{:S(2)}, u32[]{:S(2)}) collective-permute-start(bf16[2,256,256]{2,1,0:T(8,128)(2,1)} %pad_maximum_fusion.7), channel_id=1, source_target_pairs={{0,20},{4,16},{8,28},{12,24},{16,4},{20,0},{24,12},{28,8},{1,21},{... | collective-permute-start | bytes 786440 | tf_op jit(solution)/shard_map/ppermute | solution.py:577
  8.2 40.4 %copy-start.1 = (s32[32]{0:T(128)S(1)}, s32[32]{0:T(128)}, u32[]{:S(2)}) copy-start(s32[32]{0:T(128)} %order_ref.5) | copy-start | bytes 388
  8.2 40.4 %copy-start.3 = (s32[16]{0:T(128)S(1)}, s32[16]{0:T(128)}, u32[]{:S(2)}) copy-start(s32[16]{0:T(128)} %lengths_ref.1) | copy-start | bytes 196
  8.2 40.4 %copy-start.4 = (f32[32]{0:T(128)S(1)}, f32[32]{0:T(128)}, u32[]{:S(2)}) copy-start(f32[32]{0:T(128)} %bias_ref.1) | copy-start | bytes 388
  8.2 40.4 %copy-start.5 = (f32[32]{0:T(128)S(1)}, f32[32]{0:T(128)}, u32[]{:S(2)}) copy-start(f32[32]{0:T(128)} %log_ref.1) | copy-start | bytes 388
  8.2 25.5 %collective-permute-start.5 = (bf16[2,256,256]{2,1,0:T(8,128)(2,1)S(1)}, bf16[2,256,256]{2,1,0:T(8,128)(2,1)S(1)}, u32[]{:S(2)}, u32[]{:S(2)}) collective-permute-start(bf16[2,256,256]{2,1,0:T(8,128)(2,1)S(1)} %pad_maximum_fusion.8), channel_id=1, source_target_pairs={{0,24},{4,28},{8,16},{12,20},{16,8},{20,12},{24,0},{28,4},{1,25},{... | collective-permute-start | bytes 786440 | tf_op jit(solution)/shard_map/ppermute | solution.py:577
  8.9 24.8 %collective-permute-start.10 = (bf16[2,272,256]{2,1,0:T(8,128)(2,1)S(1)}, bf16[2,272,256]{2,1,0:T(8,128)(2,1)S(1)}, u32[]{:S(2)}, u32[]{:S(2)}) collective-permute-start(bf16[2,272,256]{2,1,0:T(8,128)(2,1)S(1)} %pad_maximum_fusion.1.refs_0_), channel_id=1, source_target_pairs={{0,12},{4,8},{8,4},{12,0},{16,28},{20,24},{24,20},{28,16},{1,13},{... | collective-permute-start | bytes 835592 | tf_op jit(solution)/shard_map/ppermute | solution.py:577
  24.9 15.0 %collective-permute-start.8 = (bf16[2,272,256]{2,1,0:T(8,128)(2,1)S(1)}, bf16[2,272,256]{2,1,0:T(8,128)(2,1)S(1)}, u32[]{:S(2)}, u32[]{:S(2)}) collective-permute-start(bf16[2,272,256]{2,1,0:T(8,128)(2,1)S(1)} %pad_maximum_fusion.1.refs_0_), channel_id=1, source_target_pairs={{0,4},{4,0},{8,12},{12,8},{16,20},{20,16},{24,28},{28,24},{1,5},{5... | collective-permute-start | bytes 835592 | tf_op jit(solution)/shard_map/ppermute | solution.py:577
  25.4 22.5 %collective-permute-start.9 = (bf16[2,272,256]{2,1,0:T(8,128)(2,1)S(1)}, bf16[2,272,256]{2,1,0:T(8,128)(2,1)S(1)}, u32[]{:S(2)}, u32[]{:S(2)}) collective-permute-start(bf16[2,272,256]{2,1,0:T(8,128)(2,1)S(1)} %pad_maximum_fusion.1.refs_0_), channel_id=1, source_target_pairs={{0,8},{4,12},{8,0},{12,4},{16,24},{20,28},{24,16},{28,20},{1,9},{5... | collective-permute-start | bytes 835592 | tf_op jit(solution)/shard_map/ppermute | solution.py:577
  26.2 30.6 %collective-permute-start.6 = (bf16[2,256,256]{2,1,0:T(8,128)(2,1)S(1)}, bf16[2,256,256]{2,1,0:T(8,128)(2,1)S(1)}, u32[]{:S(2)}, u32[]{:S(2)}) collective-permute-start(bf16[2,256,256]{2,1,0:T(8,128)(2,1)S(1)} %pad_maximum_fusion.9), channel_id=1, source_target_pairs={{0,28},{4,24},{8,20},{12,16},{16,12},{20,8},{24,4},{28,0},{1,29},{... | collective-permute-start | bytes 786440 | tf_op jit(solution)/shard_map/ppermute | solution.py:577
  33.7 23.1 %collective-permute-start.3 = (bf16[2,256,256]{2,1,0:T(8,128)(2,1)S(1)}, bf16[2,256,256]{2,1,0:T(8,128)(2,1)S(1)}, u32[]{:S(2)}, u32[]{:S(2)}) collective-permute-start(bf16[2,256,256]{2,1,0:T(8,128)(2,1)S(1)} %pad_maximum_fusion.6), channel_id=1, source_target_pairs={{0,16},{4,20},{8,24},{12,28},{16,0},{20,4},{24,8},{28,12},{1,17},{... | collective-permute-start | bytes 786440 | tf_op jit(solution)/shard_map/ppermute | solution.py:577
  33.7 23.5 %collective-permute-start.2 = (bf16[2,256,256]{2,1,0:T(8,128)(2,1)S(1)}, bf16[2,256,256]{2,1,0:T(8,128)(2,1)S(1)}, u32[]{:S(2)}, u32[]{:S(2)}) collective-permute-start(bf16[2,256,256]{2,1,0:T(8,128)(2,1)S(1)} %pad_maximum_fusion.5), channel_id=1, source_target_pairs={{0,12},{4,8},{8,4},{12,0},{16,28},{20,24},{24,20},{28,16},{1,13},{... | collective-permute-start | bytes 786440 | tf_op jit(solution)/shard_map/ppermute | solution.py:577
  39.9 21.5 %collective-permute-start.1 = (bf16[2,256,256]{2,1,0:T(8,128)(2,1)S(1)}, bf16[2,256,256]{2,1,0:T(8,128)(2,1)S(1)}, u32[]{:S(2)}, u32[]{:S(2)}) collective-permute-start(bf16[2,256,256]{2,1,0:T(8,128)(2,1)S(1)} %pad_maximum_fusion.4), channel_id=1, source_target_pairs={{0,8},{4,12},{8,0},{12,4},{16,24},{20,28},{24,16},{28,20},{1,9},{5... | collective-permute-start | bytes 786440 | tf_op jit(solution)/shard_map/ppermute | solution.py:577
  47.9 14.2 %collective-permute-start = (bf16[2,256,256]{2,1,0:T(8,128)(2,1)S(1)}, bf16[2,256,256]{2,1,0:T(8,128)(2,1)S(1)}, u32[]{:S(2)}, u32[]{:S(2)}) collective-permute-start(bf16[2,256,256]{2,1,0:T(8,128)(2,1)S(1)} %pad_maximum_fusion.3), channel_id=1, source_target_pairs={{0,4},{4,0},{8,12},{12,8},{16,20},{20,16},{24,28},{28,24},{1,5},{5... | collective-permute-start | bytes 786440 | tf_op jit(solution)/shard_map/ppermute | solution.py:577
  48.5 13.6 %copy-start.2 = (f32[32]{0:T(128)S(1)}, f32[32]{0:T(128)}, u32[]{:S(2)}) copy-start(f32[32]{0:T(128)} %skip_ref.1) | copy-start | bytes 388
  66.9 4.6 %copy-start.6 = (f32[2048]{0:T(1024)S(1)}, f32[2048]{0:T(1024)}, u32[]{:S(2)}) copy-start(f32[2048]{0:T(1024)} %param.28) | copy-start | bytes 24580
  68.0 7.2 %collective-permute-start.11 = (bf16[256,256]{1,0:T(8,128)(2,1)S(1)}, bf16[256,256]{1,0:T(8,128)(2,1)S(1)}, u32[]{:S(2)}, u32[]{:S(2)}) collective-permute-start(bf16[256,256]{1,0:T(8,128)(2,1)S(1)} %get-tuple-element.32), channel_id=1, source_target_pairs={{0,4},{4,0},{8,12},{12,8},{16,20},{20,16},{24,28},{28,24},{1,5},{5... | collective-permute-start | bytes 393224 | tf_op jit(solution)/shard_map/ppermute | solution.py:577
  68.9 8.3 %collective-permute-start.12 = (bf16[256,256]{1,0:T(8,128)(2,1)S(1)}, bf16[256,256]{1,0:T(8,128)(2,1)S(1)}, u32[]{:S(2)}, u32[]{:S(2)}) collective-permute-start(bf16[256,256]{1,0:T(8,128)(2,1)S(1)} %get-tuple-element.33), channel_id=1, source_target_pairs={{0,8},{4,12},{8,0},{12,4},{16,24},{20,28},{24,16},{28,20},{1,9},{5... | collective-permute-start | bytes 393224 | tf_op jit(solution)/shard_map/ppermute | solution.py:577
  71.4 7.3 %collective-permute-start.13 = (bf16[256,256]{1,0:T(8,128)(2,1)S(1)}, bf16[256,256]{1,0:T(8,128)(2,1)S(1)}, u32[]{:S(2)}, u32[]{:S(2)}) collective-permute-start(bf16[256,256]{1,0:T(8,128)(2,1)S(1)} %get-tuple-element.34), channel_id=1, source_target_pairs={{0,12},{4,8},{8,4},{12,0},{16,28},{20,24},{24,20},{28,16},{1,13},{... | collective-permute-start | bytes 393224 | tf_op jit(solution)/shard_map/ppermute | solution.py:577
  71.6 12.9 %collective-permute-start.14 = (bf16[256,256]{1,0:T(8,128)(2,1)S(1)}, bf16[256,256]{1,0:T(8,128)(2,1)S(1)}, u32[]{:S(2)}, u32[]{:S(2)}) collective-permute-start(bf16[256,256]{1,0:T(8,128)(2,1)S(1)} %get-tuple-element.35), channel_id=1, source_target_pairs={{0,16},{4,20},{8,24},{12,28},{16,0},{20,4},{24,8},{28,12},{1,17},{... | collective-permute-start | bytes 393224 | tf_op jit(solution)/shard_map/ppermute | solution.py:577
  72.2 17.9 %collective-permute-start.15 = (bf16[256,256]{1,0:T(8,128)(2,1)S(1)}, bf16[256,256]{1,0:T(8,128)(2,1)S(1)}, u32[]{:S(2)}, u32[]{:S(2)}) collective-permute-start(bf16[256,256]{1,0:T(8,128)(2,1)S(1)} %get-tuple-element.36), channel_id=1, source_target_pairs={{0,20},{4,16},{8,28},{12,24},{16,4},{20,0},{24,12},{28,8},{1,21},{... | collective-permute-start | bytes 393224 | tf_op jit(solution)/shard_map/ppermute | solution.py:577
  75.2 20.4 %collective-permute-start.16 = (bf16[256,256]{1,0:T(8,128)(2,1)S(1)}, bf16[256,256]{1,0:T(8,128)(2,1)S(1)}, u32[]{:S(2)}, u32[]{:S(2)}) collective-permute-start(bf16[256,256]{1,0:T(8,128)(2,1)S(1)} %get-tuple-element.37), channel_id=1, source_target_pairs={{0,24},{4,28},{8,16},{12,20},{16,8},{20,12},{24,0},{28,4},{1,25},{... | collective-permute-start | bytes 393224 | tf_op jit(solution)/shard_map/ppermute | solution.py:577
  77.2 20.7 %collective-permute-start.17 = (bf16[256,256]{1,0:T(8,128)(2,1)S(1)}, bf16[256,256]{1,0:T(8,128)(2,1)S(1)}, u32[]{:S(2)}, u32[]{:S(2)}) collective-permute-start(bf16[256,256]{1,0:T(8,128)(2,1)S(1)} %get-tuple-element.38), channel_id=1, source_target_pairs={{0,28},{4,24},{8,20},{12,16},{16,12},{20,8},{24,4},{28,0},{1,29},{... | collective-permute-start | bytes 393224 | tf_op jit(solution)/shard_map/ppermute | solution.py:577
  102.0 4.8 %collective-permute-start.18 = (bf16[128,2048]{1,0:T(8,128)(2,1)S(1)}, bf16[128,2048]{1,0:T(8,128)(2,1)S(1)}, u32[]{:S(2)}, u32[]{:S(2)}) collective-permute-start(bf16[128,2048]{1,0:T(8,128)(2,1)S(1)} %get-tuple-element.40), channel_id=1, source_target_pairs={{0,1},{1,0},{2,3},{3,2},{4,5},{5,4},{6,7},{7,6},{8,9},{9,8},{10,11... | collective-permute-start | bytes 1572872 | tf_op jit(solution)/shard_map/ppermute | solution.py:732
  106.3 2.3 %collective-permute-start.20 = (bf16[128,2048]{1,0:T(8,128)(2,1)S(1)}, bf16[128,2048]{1,0:T(8,128)(2,1)S(1)}, u32[]{:S(2)}, u32[]{:S(2)}) collective-permute-start(bf16[128,2048]{1,0:T(8,128)(2,1)S(1)} %get-tuple-element.42), channel_id=1, source_target_pairs={{0,1},{1,0},{2,3},{3,2},{4,5},{5,4},{6,7},{7,6},{8,9},{9,8},{10,11... | collective-permute-start | bytes 1572872 | tf_op jit(solution)/shard_map/ppermute | solution.py:732
  107.0 9.2 %collective-permute-start.19 = (bf16[64,2048]{1,0:T(8,128)(2,1)S(1)}, bf16[64,2048]{1,0:T(8,128)(2,1)S(1)}, u32[]{:S(2)}, u32[]{:S(2)}) collective-permute-start(bf16[64,2048]{1,0:T(8,128)(2,1)S(1)} %slice.17), channel_id=1, source_target_pairs={{0,2},{1,3},{2,0},{3,1},{4,6},{5,7},{6,4},{7,5},{8,10},{9,11},{10,... | collective-permute-start | bytes 786440 | tf_op jit(solution)/shard_map/ppermute | solution.py:732
  108.7 12.2 %collective-permute-start.21 = (bf16[64,2048]{1,0:T(8,128)(2,1)S(1)}, bf16[64,2048]{1,0:T(8,128)(2,1)S(1)}, u32[]{:S(2)}, u32[]{:S(2)}) collective-permute-start(bf16[64,2048]{1,0:T(8,128)(2,1)S(1)} %slice.19), channel_id=1, source_target_pairs={{0,2},{1,3},{2,0},{3,1},{4,6},{5,7},{6,4},{7,5},{8,10},{9,11},{10,... | collective-permute-start | bytes 786440 | tf_op jit(solution)/shard_map/ppermute | solution.py:732

commit v3 on v2

--- a/solution.py
+++ b/solution.py
@@ -415,9 +415,9 @@
 
 
 def scan_kernel(
-    heads, per_dev, chunks_step, piece_count, me_ref, order_ref, skip_ref, taps_ref, *refs
+    heads, per_dev, chunks_step, turns, me_ref, order_ref, skip_ref, taps_ref, *refs
 ):
-    piece_refs, refs = refs[:piece_count], refs[piece_count:]
+    piece_refs, refs = refs[: len(turns)], refs[len(turns) :]
     mix_ref, query_ref, key_ref, tail_ref, inflow_ref, gate_ref, since_ref, out_ref = refs[:8]
     sequence, previous, state = refs[8:]
     me = me_ref[0]
@@ -427,7 +427,7 @@
     def _():
         previous[...] = jnp.zeros_like(previous)
         state[...] = jnp.zeros_like(state)
-        for turn, piece_ref in enumerate(piece_refs):
+        for turn, piece_ref in zip(turns, piece_refs):
             loader = jnp.bitwise_xor(me, turn)
             for b in range(per_dev):
                 place = order_ref[loader * per_dev + b]
@@ -477,10 +477,10 @@
     lax.fori_loop(0, chunks_step, one_chunk, 0, unroll=2)
 
 
-def gating_kernel(per_dev, piece_count, place_ref, order_ref, mixed_ref, *refs):
-    piece_refs, out_refs, laid = refs[:piece_count], refs[piece_count:-1], refs[-1]
+def gating_kernel(per_dev, turns, place_ref, order_ref, mixed_ref, *refs):
+    piece_refs, out_refs, laid = refs[: len(turns)], refs[len(turns) : -1], refs[-1]
     me, mine = place_ref[0], place_ref[1]
-    for turn, piece_ref in enumerate(piece_refs):
+    for turn, piece_ref in zip(turns, piece_refs):
         loader = jnp.bitwise_xor(me, turn)
         for b in range(per_dev):
             place = order_ref[loader * per_dev + b]
@@ -511,32 +511,47 @@
         normed[:, pl.ds(at, width)] = (piece * inverse_rms * gain).astype(jnp.bfloat16)
 
 
+def weight_tiles(weight_ref, group, buffer, sems, count):
+    tile = buffer.shape[1] // count
+    tiles = [slice(i * tile, (i + 1) * tile) for i in range(count)]
+    return tiles, [
+        pltpu.make_async_copy(weight_ref.at[group, :, at], buffer.at[:, at], sems.at[i])
+        for i, at in enumerate(tiles)
+    ]
+
+
 def near_kernel(place_ref, gain_ref, weight_ref, *refs):
-    gated_refs, partial_ref, normed = refs[:-2], refs[-2], refs[-1]
-
-    @pl.when(pl.program_id(0) == 0)
-    def _():
-        normed_into(normed, gated_refs, gain_ref, place_ref[0], 0)
-
-    partial_ref[...] = jnp.dot(
-        normed[...], weight_ref[...], preferred_element_type=jnp.float32
-    )
-
-
-def far_kernel(place_ref, gain_ref, weight_ref, near_ref, *refs):
-    gated_refs, away_ref, stay_ref, normed = refs[:-3], refs[-3], refs[-2], refs[-1]
-
-    @pl.when(pl.program_id(0) == 0)
-    def _():
-        normed_into(normed, gated_refs, gain_ref, place_ref[0], len(gated_refs))
-
-    partial = near_ref[...] + jnp.dot(
-        normed[...], weight_ref[...], preferred_element_type=jnp.float32
-    )
-    partial = partial.astype(jnp.bfloat16)
-    rows = partial.shape[0] // 2
-    away_ref[...] = partial[:rows]
-    stay_ref[...] = partial[rows:]
+    gated_refs, (partial_ref, next_ref, normed, buffer, sems) = refs[:-5], refs[-5:]
+    count = sems.shape[0] - 1
+    group = lax.div(place_ref[0], len(gated_refs))
+    tiles, copies = weight_tiles(weight_ref, group, buffer, sems, count)
+    onward = pltpu.make_async_copy(weight_ref.at[1 - group], next_ref, sems.at[count])
+    for copy in copies + [onward]:
+        copy.start()
+    normed_into(normed, gated_refs, gain_ref, place_ref[0], 0)
+    for at, copy in zip(tiles, copies):
+        copy.wait()
+        partial_ref[:, at] = jnp.dot(
+            normed[...], buffer[:, at], preferred_element_type=jnp.float32
+        )
+    onward.wait()
+
+
+def far_kernel(parts, place_ref, gain_ref, weight_ref, near_ref, *refs):
+    gated_refs, refs = refs[: -2 * parts - 1], refs[-2 * parts - 1 :]
+    away_refs, stay_refs, normed = refs[:parts], refs[parts:-1], refs[-1]
+    normed_into(normed, gated_refs, gain_ref, place_ref[0], len(gated_refs))
+    rows, columns = away_refs[0].shape
+    tile = 1024
+    for part in range(parts):
+        for first in range(0, columns, tile):
+            at = slice(part * columns + first, part * columns + first + tile)
+            partial = near_ref[:, at] + jnp.dot(
+                normed[...], weight_ref[:, at], preferred_element_type=jnp.float32
+            )
+            partial = partial.astype(jnp.bfloat16)
+            away_refs[part][:, first : first + tile] = partial[:rows]
+            stay_refs[part][:, first : first + tile] = partial[rows:]
 
 
 def head_split(
@@ -590,7 +605,8 @@
 
     held = jnp.stack([for_group(my_group), turned(for_group(my_group ^ 1), near)])
     group_rows = [held] + [turned(held, turn) for turn in range(1, near)]
-    head_rows = [for_heads(0)] + [turned(for_heads(turn), turn) for turn in range(1, ctx_count)]
+    turns = (0, 6, 7, 4, 3, 2, 5, 1)
+    head_rows = [turned(for_heads(turn), turn) if turn else for_heads(turn) for turn in turns]
 
     key_taps = lax.dynamic_slice_in_dim(conv_keys, my_group * STATE, STATE, 1)
     query_taps = lax.dynamic_slice_in_dim(conv_queries, my_group * STATE, STATE, 1)
@@ -639,7 +655,7 @@
     )(place, block_order, doc_lengths, step_bias, decay_log, key_taps, query_taps, *group_rows)
 
     mixed = pl.pallas_call(
-        functools.partial(scan_kernel, heads, per_dev, chunks_step, ctx_count),
+        functools.partial(scan_kernel, heads, per_dev, chunks_step, turns),
         grid=(grid_steps,),
         in_specs=[smem] * 3
         + [whole(value_taps)]
@@ -660,7 +676,7 @@
     )(place, block_order, skip_gain, value_taps, *head_rows, *mixing)
 
     gated = pl.pallas_call(
-        functools.partial(gating_kernel, per_dev, ctx_count),
+        functools.partial(gating_kernel, per_dev, turns),
         grid=(1,),
         in_specs=[smem, smem, pl.BlockSpec((total_tokens, width), lambda i: (0, 0))]
         + [pl.BlockSpec((None, token_count, width), lambda i: (1, 0, 0))] * ctx_count,
@@ -677,55 +693,51 @@
     pieces = [gated[0]] + [turned(gated[turn], turn) for turn in range(1, ctx_count)]
 
     columns = out_weight.shape[1]
-    tile = 2048
-    tiles = columns // tile
     group_width = near * width
     gain = norm_gain.reshape(ctx_count, width)
     weight = out_weight.reshape(groups, group_width, columns)
 
-    def project(kernel, gated_pieces, own, first, count, extra, extra_specs, out_specs, out_shape):
-        spec = pltpu.PrefetchScalarGridSpec(
-            num_scalar_prefetch=1,
-            grid=(count,),
-            in_specs=[
-                pl.BlockSpec(gain.shape, lambda i, at: (0, 0)),
-                pl.BlockSpec(
-                    (None, group_width, tile),
-                    lambda i, at: (
-                        lax.div(at[0], near) if own else 1 - lax.div(at[0], near),
-                        0,
-                        first + i,
-                    ),
-                ),
-            ]
-            + extra_specs
-            + [pl.BlockSpec((token_count, width), lambda i, at: (0, 0))] * len(gated_pieces),
-            out_specs=out_specs,
-            scratch_shapes=[pltpu.VMEM((token_count, group_width), jnp.bfloat16)],
-        )
+    def project(kernel, weight, weight_space, operands, out_shape, scratch, limit, name):
         return pl.pallas_call(
             kernel,
-            grid_spec=spec,
+            in_specs=[smem, vmem, pl.BlockSpec(memory_space=weight_space)] + [vmem] * len(operands),
+            out_specs=[vmem] * len(out_shape),
             out_shape=out_shape,
-            compiler_params=pltpu.CompilerParams(vmem_limit_bytes=44 * 1024 * 1024),
+            scratch_shapes=[pltpu.VMEM((token_count, group_width), jnp.bfloat16)] + scratch,
+            compiler_params=pltpu.CompilerParams(vmem_limit_bytes=limit * 1024 * 1024),
             cost_estimate=pl.CostEstimate(
-                flops=2 * token_count * group_width * tile * count,
-                bytes_accessed=2 * group_width * tile * count,
+                flops=2 * token_count * group_width * columns,
+                bytes_accessed=2 * group_width * columns,
                 transcendentals=0,
             ),
-            name="near_projection" if own else "far_projection",
-        )(place, gain, weight, *extra, *gated_pieces)
-
-    near_partial = project(
+            name=name,
+        )(place, gain, weight, *operands)
+
+    near_partial, far_weight = project(
         near_kernel,
+        weight,
+        pl.ANY,
         pieces[:near],
-        True,
-        0,
-        tiles,
+        [
+            jax.ShapeDtypeStruct((token_count, columns), jnp.float32),
+            jax.ShapeDtypeStruct((group_width, columns), jnp.bfloat16),
+        ],
+        [pltpu.VMEM((group_width, columns), jnp.bfloat16), pltpu.SemaphoreType.DMA((5,))],
+        28,
+        "near_projection",
+    )
+    parts = 2
+    rows = token_count // 2
+    part_shape = jax.ShapeDtypeStruct((rows, columns // parts), jnp.bfloat16)
+    split = project(
+        functools.partial(far_kernel, parts),
+        far_weight,
+        pltpu.VMEM,
+        [near_partial] + pieces[near:],
+        [part_shape] * (2 * parts),
         [],
-        [],
-        pl.BlockSpec((token_count, tile), lambda i, at: (0, i)),
-        jax.ShapeDtypeStruct((token_count, columns), jnp.float32),
+        8,
+        "far_projection",
     )
 
     def joined(kept, sent, turn):
@@ -733,22 +745,7 @@
         return (kept.astype(jnp.float32) + came.astype(jnp.float32)).astype(jnp.bfloat16)
 
     results = []
-    rows = token_count // 2
-    parts = 2
-    part_tiles = tiles // parts
-    for part in range(parts):
-        first = part * part_tiles
-        away, stay = project(
-            far_kernel,
-            pieces[near:],
-            False,
-            first,
-            part_tiles,
-            [near_partial],
-            [pl.BlockSpec((token_count, tile), lambda i, at, first=first: (0, first + i))],
-            [pl.BlockSpec((rows, tile), lambda i, at: (0, i))] * 2,
-            [jax.ShapeDtypeStruct((rows, columns // parts), jnp.bfloat16)] * 2,
-        )
+    for away, stay in zip(split[:parts], split[parts:]):
         across = joined(stay, away, 1)
         results.append(joined(across[rows // 2 :], across[: rows // 2], 2))
     return jnp.concatenate(results, axis=1)

time: 122 us -> 118 us (0.967)
  waiting for transfers between devices: 41.1 us -> 47.2 us
  starting transfers between devices: 46.4 us -> 41 us
  Pallas kernels: 28.1 us -> 23.6 us
    ppermute x18, starting transfers between devices: 42.8 us -> 38.3 us  [turned(): return lax.ppermute(value, 'ctx', [(i, i ^ turn) for i in range(ctx_count)])]
    pallas_call x4 -> x3, Pallas kernels: 15.1 us -> 10.7 us  [the longest x2 9.6 us: project(): pl.pallas_call(kernel, in_specs=[smem, vmem, pl.BlockSpec(memory_space=we...]
    ppermute x18, waiting for transfers between devices: 30.4 us -> 34.2 us  [turned(): return lax.ppermute(value, 'ctx', [(i, i ^ turn) for i in range(ctx_count)])]
    ppermute x4, waiting for transfers between devices: 10.8 us -> 13 us  [joined(): came = lax.ppermute(sent, 'tp', [(i, i ^ turn) for i in range(tp_count)])]
  transfers between devices with their start and end apart: 22 -> 22, of which waited for: 13 -> 14; matrix products, arithmetic and copies ran while one was open for 3% -> 3% of each run, Pallas kernels for 15% -> 12%
where the time goes in v3:
time: 118 us
  waiting for transfers between devices  47.2 us (40%)
  starting transfers between devices  41 us (35%)
  Pallas kernels  23.6 us (20%)
  local copies, waits for them, and re-layouts  3.57 us (3%)
  other arithmetic  2.27 us (2%)
    ppermute x18, starting transfers between devices, turned(): return lax.ppermute(value, 'ctx', [(i, i ^ turn) for i in range(ctx_count)])  38.3 us
    ppermute x18, waiting for transfers between devices, turned(): return lax.ppermute(value, 'ctx', [(i, i ^ turn) for i in range(ctx_count)])  34.2 us
    ppermute x4, waiting for transfers between devices, joined(): came = lax.ppermute(sent, 'tp', [(i, i ^ turn) for i in range(tp_count)])  13 us
    pallas_call x2, Pallas kernels, project(): pl.pallas_call(kernel, in_specs=[smem, vmem, pl.BlockSpec(memory_space=we...  9.6 us
    pallas_call x1, Pallas kernels, head_split(): pl.pallas_call(functools.partial(mixing_kernel, heads, group_heads, per_d...  8.14 us
    pallas_call x1, Pallas kernels, head_split(): pl.pallas_call(functools.partial(scan_kernel, heads, per_dev, chunks_step...  4.83 us
    ppermute x4, starting transfers between devices, joined(): came = lax.ppermute(sent, 'tp', [(i, i ^ turn) for i in range(tp_count)])  2.72 us
  transfers between devices with their start and end apart: 22, of which 14 were waited for; matrix products, arithmetic and copies ran while one was open for 3% of the time, Pallas kernels for 12%

profile of v3, /device:TPU:16, one launch (start us, length us, event | category | flops | bytes accessed | tf_op | source)
XLA Modules:
  0.0 118.0 jit_solution(4774753030250811137)
XLA Ops:
  0.0 0.7 dynamic-slice_bitcast_fusion.17
  0.7 1.0 constant_dynamic-slice_fusion.2
  1.7 0.1 collective-permute-start.7
  1.8 1.8 %dynamic-slice_bitcast_fusion = (bf16[1,256,256]{2,1,0:T(8,128)(2,1)S(1)}, bf16[1,256,256]{2,1,0:T(8,128)(2,1)S(1)}, bf16[1,256,256]{2,1,0:T(8,128)(2,1)S(1)}, b...) fusion(bf16[256,2048]{1,0:T(8,128)(2,1)} %param.16, ...), kind=kLoop, calls=%fused_computation.16 | loop fusion | bytes 4194336 | tf_op jit(solution)/shard_map/stack | solution.py:602
  3.6 0.7 pad_maximum_fusion.8
  4.4 3.8 %collective-permute-start.5 = (bf16[2,256,256]{2,1,0:T(8,128)(2,1)}, bf16[2,256,256]{2,1,0:T(8,128)(2,1)S(1)}, u32[]{:S(2)}, u32[]{:S(2)}) collective-permute-start(bf16[2,256,256]{2,1,0:T(8,128)(2,1)} %pad_maximum_fusion.8), channel_id=1, source_target_pairs={{0,20},{4,16},{8,28},{12,24},{16,4},{20,0},{24,12},{28,8},{1,21},{... | collective-permute-start | bytes 786440 | tf_op jit(solution)/shard_map/ppermute | solution.py:592
  8.2 0.5 collective-permute-start
  8.9 16.0 %collective-permute-start.10 = (bf16[2,272,256]{2,1,0:T(8,128)(2,1)S(1)}, bf16[2,272,256]{2,1,0:T(8,128)(2,1)S(1)}, u32[]{:S(2)}, u32[]{:S(2)}) collective-permute-start(bf16[2,272,256]{2,1,0:T(8,128)(2,1)S(1)} %pad_maximum_fusion.1.refs_0_), channel_id=1, source_target_pairs={{0,12},{4,8},{8,4},{12,0},{16,28},{20,24},{24,20},{28,16},{1,13},{... | collective-permute-start | bytes 835592 | tf_op jit(solution)/shard_map/ppermute | solution.py:592
  24.9 0.6 collective-permute-start.8
  25.6 0.6 collective-permute-done.5.refs_6_
  26.2 2.5 %collective-permute-start.1 = (bf16[2,256,256]{2,1,0:T(8,128)(2,1)S(1)}, bf16[2,256,256]{2,1,0:T(8,128)(2,1)S(1)}, u32[]{:S(2)}, u32[]{:S(2)}) collective-permute-start(bf16[2,256,256]{2,1,0:T(8,128)(2,1)S(1)} %pad_maximum_fusion.4), channel_id=1, source_target_pairs={{0,28},{4,24},{8,20},{12,16},{16,12},{20,8},{24,4},{28,0},{1,29},{... | collective-permute-start | bytes 786440 | tf_op jit(solution)/shard_map/ppermute | solution.py:592
  28.7 5.0 %collective-permute-done.refs_1_ = bf16[2,256,256]{2,1,0:T(8,128)(2,1)S(1)} collective-permute-done((bf16[2,256,256]{2,1,0:T(8,128)(2,1)S(1)}, bf16[2,256,256]{2,1,0:T(8,128)(2,1)S(1)}, u32[]{:S(2)}, u32[]{:S(2)}) %collective-permute-start) | collective-permute-done | bytes 262176 | tf_op jit(solution)/shard_map/ppermute | solution.py:592
  33.7 2.7 %collective-permute-start.3 = (bf16[2,256,256]{2,1,0:T(8,128)(2,1)S(1)}, bf16[2,256,256]{2,1,0:T(8,128)(2,1)S(1)}, u32[]{:S(2)}, u32[]{:S(2)}) collective-permute-start(bf16[2,256,256]{2,1,0:T(8,128)(2,1)S(1)} %pad_maximum_fusion.6), channel_id=1, source_target_pairs={{0,12},{4,8},{8,4},{12,0},{16,28},{20,24},{24,20},{28,16},{1,13},{... | collective-permute-start | bytes 786440 | tf_op jit(solution)/shard_map/ppermute | solution.py:592
  36.4 8.2 %collective-permute-done.9.refs_2_ = bf16[2,272,256]{2,1,0:T(8,128)(2,1)S(1)} collective-permute-done((bf16[2,272,256]{2,1,0:T(8,128)(2,1)S(1)}, bf16[2,272,256]{2,1,0:T(8,128)(2,1)S(1)}, u32[]{:S(2)}, u32[]{:S(2)}) %collective-permute-start.9) | collective-permute-done | bytes 278560 | tf_op jit(solution)/shard_map/ppermute | solution.py:592
  44.6 2.5 %collective-permute-start.4 = (bf16[2,256,256]{2,1,0:T(8,128)(2,1)S(1)}, bf16[2,256,256]{2,1,0:T(8,128)(2,1)S(1)}, u32[]{:S(2)}, u32[]{:S(2)}) collective-permute-start(bf16[2,256,256]{2,1,0:T(8,128)(2,1)S(1)} %pad_maximum_fusion.7), channel_id=1, source_target_pairs={{0,8},{4,12},{8,0},{12,4},{16,24},{20,28},{24,16},{28,20},{1,9},{5... | collective-permute-start | bytes 786440 | tf_op jit(solution)/shard_map/ppermute | solution.py:592
  47.1 1.5 %collective-permute-start.6 = (bf16[2,256,256]{2,1,0:T(8,128)(2,1)S(1)}, bf16[2,256,256]{2,1,0:T(8,128)(2,1)S(1)}, u32[]{:S(2)}, u32[]{:S(2)}) collective-permute-start(bf16[2,256,256]{2,1,0:T(8,128)(2,1)S(1)} %pad_maximum_fusion.9), channel_id=1, source_target_pairs={{0,4},{4,0},{8,12},{12,8},{16,20},{20,16},{24,28},{28,24},{1,5},{5... | collective-permute-start | bytes 786440 | tf_op jit(solution)/shard_map/ppermute | solution.py:592
  48.6 0.1 pad_add_fusion.me_ref.place_ref
  48.8 8.1 %mixing.1 = (bf16[16,128,512]{2,1,0:T(8,128)(2,1)S(1)}, bf16[16,128,128]{2,1,0:T(8,128)(2,1)S(1)}, bf16[16,128,128]{2,1,0:T(8,128)(2,1)S(1)}, f32[16,128,256]{2,...) custom-call(s32[2]{0:T(128)S(1)} %pad_add_fusion.me_ref.place_ref, ...), custom_call_target="tpu_custom_call" | custom-call | flops 20000000 | bytes 20000000 | tf_op jit(solution)/shard_map/mixing/pallas_call | solution.py:637
  56.9 0.3 collective-permute-done.3.refs_4_
  57.2 4.2 %collective-permute-done.4.refs_5_ = bf16[2,256,256]{2,1,0:T(8,128)(2,1)S(1)} collective-permute-done((bf16[2,256,256]{2,1,0:T(8,128)(2,1)S(1)}, bf16[2,256,256]{2,1,0:T(8,128)(2,1)S(1)}, u32[]{:S(2)}, u32[]{:S(2)}) %collective-permute-start.4) | collective-permute-done | bytes 262176 | tf_op jit(solution)/shard_map/ppermute | solution.py:592
  61.4 0.7 collective-permute-done.6.refs_7_
  62.1 4.8 %scan.1 = f32[16,128,256]{2,1,0:T(8,128)S(1)} custom-call(s32[2]{0:T(128)S(1)} %pad_add_fusion.me_ref.place_ref, s32[32]{0:T(128)S(1)} %copy-done.1, f32[32]{0:T(128)S(1)} %copy-done.2, f32[4,256]{1,0:T(4,128)S(1)} %constant_dynamic-slice_fusion.6.taps_ref, bf16[2,256,256]{2,1,0:T(8,128)(2,1)S(1)} %pad_maximum_fusion.2.refs_0_, ...), custom_call_target="tpu_custom_call" | custom-call | flops 600000000 | bytes 14000000 | tf_op jit(solution)/shard_map/scan/pallas_call | solution.py:657
  66.9 1.1 gating.1
  68.0 0.9 collective-permute-start.11
  68.9 2.5 %collective-permute-start.12 = (bf16[256,256]{1,0:T(8,128)(2,1)S(1)}, bf16[256,256]{1,0:T(8,128)(2,1)S(1)}, u32[]{:S(2)}, u32[]{:S(2)}) collective-permute-start(bf16[256,256]{1,0:T(8,128)(2,1)S(1)} %get-tuple-element.35), channel_id=1, source_target_pairs={{0,8},{4,12},{8,0},{12,4},{16,24},{20,28},{24,16},{28,20},{1,9},{5... | collective-permute-start | bytes 393224 | tf_op jit(solution)/shard_map/ppermute | solution.py:592
  71.4 0.1 collective-permute-start.13
  71.5 0.7 collective-permute-start.14
  72.2 3.0 %collective-permute-start.15 = (bf16[256,256]{1,0:T(8,128)(2,1)S(1)}, bf16[256,256]{1,0:T(8,128)(2,1)S(1)}, u32[]{:S(2)}, u32[]{:S(2)}) collective-permute-start(bf16[256,256]{1,0:T(8,128)(2,1)S(1)} %get-tuple-element.40), channel_id=1, source_target_pairs={{0,20},{4,16},{8,28},{12,24},{16,4},{20,0},{24,12},{28,8},{1,21},{... | collective-permute-start | bytes 393224 | tf_op jit(solution)/shard_map/ppermute | solution.py:592
  75.2 0.6 collective-permute-start.16
  75.9 1.3 %collective-permute-done.12.refs_2_ = bf16[256,256]{1,0:T(8,128)(2,1)S(1)} collective-permute-done((bf16[256,256]{1,0:T(8,128)(2,1)S(1)}, bf16[256,256]{1,0:T(8,128)(2,1)S(1)}, u32[]{:S(2)}, u32[]{:S(2)}) %collective-permute-start.12) | collective-permute-done | bytes 131104 | tf_op jit(solution)/shard_map/ppermute | solution.py:592
  77.2 0.2 collective-permute-start.17
  77.4 1.3 %collective-permute-done.13.refs_3_ = bf16[256,256]{1,0:T(8,128)(2,1)S(1)} collective-permute-done((bf16[256,256]{1,0:T(8,128)(2,1)S(1)}, bf16[256,256]{1,0:T(8,128)(2,1)S(1)}, u32[]{:S(2)}, u32[]{:S(2)}) %collective-permute-start.13) | collective-permute-done | bytes 131104 | tf_op jit(solution)/shard_map/ppermute | solution.py:592
  78.7 6.5 %near_projection.1 = (f32[256,4096]{1,0:T(8,128)S(1)}, bf16[1024,4096]{1,0:T(8,128)(2,1)S(1)}) custom-call(s32[2]{0:T(128)S(1)} %pad_add_fusion.me_ref.place_ref, f32[8,256]{1,0:T(8,128)S(1)} %reshape.9.gain_ref, bf16[2,1024,4096]{2,1,0:T(8,128)(2,1)} %bitcast.44, bf16[256,256]{1,0:T(8,128)(2,1)S(1)} %get-tuple-element.33.refs_0_, ...), custom_call_target="tpu_custom_call" | custom-call | flops 2147483648 | bytes 8388608 | tf_op jit(solution)/shard_map/near_projection/pallas_call | solution.py:701
  85.3 4.8 %collective-permute-done.15.refs_1_ = bf16[256,256]{1,0:T(8,128)(2,1)S(1)} collective-permute-done((bf16[256,256]{1,0:T(8,128)(2,1)S(1)}, bf16[256,256]{1,0:T(8,128)(2,1)S(1)}, u32[]{:S(2)}, u32[]{:S(2)}) %collective-permute-start.15) | collective-permute-done | bytes 131104 | tf_op jit(solution)/shard_map/ppermute | solution.py:592
  90.1 5.6 %collective-permute-done.16.refs_2_ = bf16[256,256]{1,0:T(8,128)(2,1)S(1)} collective-permute-done((bf16[256,256]{1,0:T(8,128)(2,1)S(1)}, bf16[256,256]{1,0:T(8,128)(2,1)S(1)}, u32[]{:S(2)}, u32[]{:S(2)}) %collective-permute-start.16) | collective-permute-done | bytes 131104 | tf_op jit(solution)/shard_map/ppermute | solution.py:592
  95.7 2.2 %collective-permute-done.17.refs_3_ = bf16[256,256]{1,0:T(8,128)(2,1)S(1)} collective-permute-done((bf16[256,256]{1,0:T(8,128)(2,1)S(1)}, bf16[256,256]{1,0:T(8,128)(2,1)S(1)}, u32[]{:S(2)}, u32[]{:S(2)}) %collective-permute-start.17) | collective-permute-done | bytes 131104 | tf_op jit(solution)/shard_map/ppermute | solution.py:592
  97.8 3.1 %far_projection.1 = (bf16[128,2048]{1,0:T(8,128)(2,1)S(1)}, bf16[128,2048]{1,0:T(8,128)(2,1)S(1)}, bf16[128,2048]{1,0:T(8,128)(2,1)S(1)}, bf16[128,2048]{1,0:T(8,128)(2,1)S(1)}) custom-call(s32[2]{0:T(128)S(1)} %pad_add_fusion.me_ref.place_ref, f32[8,256]{1,0:T(8,128)S(1)} %reshape.9.gain_ref, bf16[1024,4096]{1,0:T(8,128)(2,1)S(1)} %get-tuple-element.37.weight_ref, ...), custom_call_target="tpu_custom_call" | custom-call | flops 2147483648 | bytes 8388608 | tf_op jit(solution)/shard_map/far_projection/pallas_call | solution.py:701
  100.9 0.1 collective-permute-start.18
  101.0 0.5 collective-permute-start.20
  101.5 1.4 %collective-permute-done.18 = bf16[128,2048]{1,0:T(8,128)(2,1)S(1)} collective-permute-done((bf16[128,2048]{1,0:T(8,128)(2,1)S(1)}, bf16[128,2048]{1,0:T(8,128)(2,1)S(1)}, u32[]{:S(2)}, u32[]{:S(2)}) %collective-permute-start.18) | collective-permute-done | bytes 524320 | tf_op jit(solution)/shard_map/ppermute | solution.py:744
  102.9 0.1 add_convert_fusion.1
  103.1 1.6 %collective-permute-start.19 = (bf16[64,2048]{1,0:T(8,128)(2,1)S(1)}, bf16[64,2048]{1,0:T(8,128)(2,1)S(1)}, u32[]{:S(2)}, u32[]{:S(2)}) collective-permute-start(bf16[64,2048]{1,0:T(8,128)(2,1)S(1)} %slice.17), channel_id=1, source_target_pairs={{0,2},{1,3},{2,0},{3,1},{4,6},{5,7},{6,4},{7,5},{8,10},{9,11},{10,... | collective-permute-start | bytes 786440 | tf_op jit(solution)/shard_map/ppermute | solution.py:744
  104.6 0.1 add_convert_fusion
  104.8 0.6 collective-permute-start.21
  105.4 6.9 %collective-permute-done.19 = bf16[64,2048]{1,0:T(8,128)(2,1)S(1)} collective-permute-done((bf16[64,2048]{1,0:T(8,128)(2,1)S(1)}, bf16[64,2048]{1,0:T(8,128)(2,1)S(1)}, u32[]{:S(2)}, u32[]{:S(2)}) %collective-permute-start.19) | collective-permute-done | bytes 262176 | tf_op jit(solution)/shard_map/ppermute | solution.py:744
  112.4 4.7 %collective-permute-done.21 = bf16[64,2048]{1,0:T(8,128)(2,1)S(1)} collective-permute-done((bf16[64,2048]{1,0:T(8,128)(2,1)S(1)}, bf16[64,2048]{1,0:T(8,128)(2,1)S(1)}, u32[]{:S(2)}, u32[]{:S(2)}) %collective-permute-start.21) | collective-permute-done | bytes 262176 | tf_op jit(solution)/shard_map/ppermute | solution.py:744
  117.1 0.1 add_convert_fusion.2
  117.2 0.8 pad_maximum_fusion
  (44 shorter events, 0.4 us)
Async XLA Ops:
  0.0 25.6 %copy-start = (f32[4,2048]{1,0:T(4,128)S(1)}, f32[4,2048]{1,0:T(4,128)}, u32[]{:S(2)}) copy-start(f32[4,2048]{1,0:T(4,128)} %param.22) | copy-start | bytes 98308
  1.7 7.2 %collective-permute-start.7 = (bf16[272,256]{1,0:T(8,128)(2,1)S(1)}, bf16[272,256]{1,0:T(8,128)(2,1)S(1)}, u32[]{:S(2)}, u32[]{:S(2)}) collective-permute-start(bf16[272,256]{1,0:T(8,128)(2,1)S(1)} %pad_maximum_fusion.10), channel_id=1, source_target_pairs={{0,16},{4,20},{8,24},{12,28},{16,0},{20,4},{24,8},{28,12},{1,17},{... | collective-permute-start | bytes 417800 | tf_op jit(solution)/shard_map/ppermute | solution.py:592
  4.4 44.3 %copy-start.7 = (f32[4,256]{1,0:T(4,128)S(1)}, f32[4,256]{1,0:T(4,128)}, u32[]{:S(2)}) copy-start(f32[4,256]{1,0:T(4,128)} %param.24) | copy-start | bytes 12292
  4.4 44.3 %copy-start.8 = (f32[4,256]{1,0:T(4,128)S(1)}, f32[4,256]{1,0:T(4,128)}, u32[]{:S(2)}) copy-start(f32[4,256]{1,0:T(4,128)} %param.23) | copy-start | bytes 12292
  4.4 21.8 %collective-permute-start.5 = (bf16[2,256,256]{2,1,0:T(8,128)(2,1)}, bf16[2,256,256]{2,1,0:T(8,128)(2,1)S(1)}, u32[]{:S(2)}, u32[]{:S(2)}) collective-permute-start(bf16[2,256,256]{2,1,0:T(8,128)(2,1)} %pad_maximum_fusion.8), channel_id=1, source_target_pairs={{0,20},{4,16},{8,28},{12,24},{16,4},{20,0},{24,12},{28,8},{1,21},{... | collective-permute-start | bytes 786440 | tf_op jit(solution)/shard_map/ppermute | solution.py:592
  8.2 40.5 %copy-start.1 = (s32[32]{0:T(128)S(1)}, s32[32]{0:T(128)}, u32[]{:S(2)}) copy-start(s32[32]{0:T(128)} %order_ref.5) | copy-start | bytes 388
  8.2 40.5 %copy-start.3 = (s32[16]{0:T(128)S(1)}, s32[16]{0:T(128)}, u32[]{:S(2)}) copy-start(s32[16]{0:T(128)} %lengths_ref.1) | copy-start | bytes 196
  8.2 40.5 %copy-start.4 = (f32[32]{0:T(128)S(1)}, f32[32]{0:T(128)}, u32[]{:S(2)}) copy-start(f32[32]{0:T(128)} %bias_ref.1) | copy-start | bytes 388
  8.2 40.5 %copy-start.5 = (f32[32]{0:T(128)S(1)}, f32[32]{0:T(128)}, u32[]{:S(2)}) copy-start(f32[32]{0:T(128)} %log_ref.1) | copy-start | bytes 388
  8.2 25.4 %collective-permute-start = (bf16[2,256,256]{2,1,0:T(8,128)(2,1)S(1)}, bf16[2,256,256]{2,1,0:T(8,128)(2,1)S(1)}, u32[]{:S(2)}, u32[]{:S(2)}) collective-permute-start(bf16[2,256,256]{2,1,0:T(8,128)(2,1)S(1)} %pad_maximum_fusion.3), channel_id=1, source_target_pairs={{0,24},{4,28},{8,16},{12,20},{16,8},{20,12},{24,0},{28,4},{1,25},{... | collective-permute-start | bytes 786440 | tf_op jit(solution)/shard_map/ppermute | solution.py:592
  8.9 24.7 %collective-permute-start.10 = (bf16[2,272,256]{2,1,0:T(8,128)(2,1)S(1)}, bf16[2,272,256]{2,1,0:T(8,128)(2,1)S(1)}, u32[]{:S(2)}, u32[]{:S(2)}) collective-permute-start(bf16[2,272,256]{2,1,0:T(8,128)(2,1)S(1)} %pad_maximum_fusion.1.refs_0_), channel_id=1, source_target_pairs={{0,12},{4,8},{8,4},{12,0},{16,28},{20,24},{24,20},{28,16},{1,13},{... | collective-permute-start | bytes 835592 | tf_op jit(solution)/shard_map/ppermute | solution.py:592
  24.9 19.7 %collective-permute-start.9 = (bf16[2,272,256]{2,1,0:T(8,128)(2,1)S(1)}, bf16[2,272,256]{2,1,0:T(8,128)(2,1)S(1)}, u32[]{:S(2)}, u32[]{:S(2)}) collective-permute-start(bf16[2,272,256]{2,1,0:T(8,128)(2,1)S(1)} %pad_maximum_fusion.1.refs_0_), channel_id=1, source_target_pairs={{0,8},{4,12},{8,0},{12,4},{16,24},{20,28},{24,16},{28,20},{1,9},{5... | collective-permute-start | bytes 835592 | tf_op jit(solution)/shard_map/ppermute | solution.py:592
  24.9 22.2 %collective-permute-start.8 = (bf16[2,272,256]{2,1,0:T(8,128)(2,1)S(1)}, bf16[2,272,256]{2,1,0:T(8,128)(2,1)S(1)}, u32[]{:S(2)}, u32[]{:S(2)}) collective-permute-start(bf16[2,272,256]{2,1,0:T(8,128)(2,1)S(1)} %pad_maximum_fusion.1.refs_0_), channel_id=1, source_target_pairs={{0,4},{4,0},{8,12},{12,8},{16,20},{20,16},{24,28},{28,24},{1,5},{5... | collective-permute-start | bytes 835592 | tf_op jit(solution)/shard_map/ppermute | solution.py:592
  26.2 30.7 %collective-permute-start.1 = (bf16[2,256,256]{2,1,0:T(8,128)(2,1)S(1)}, bf16[2,256,256]{2,1,0:T(8,128)(2,1)S(1)}, u32[]{:S(2)}, u32[]{:S(2)}) collective-permute-start(bf16[2,256,256]{2,1,0:T(8,128)(2,1)S(1)} %pad_maximum_fusion.4), channel_id=1, source_target_pairs={{0,28},{4,24},{8,20},{12,16},{16,12},{20,8},{24,4},{28,0},{1,29},{... | collective-permute-start | bytes 786440 | tf_op jit(solution)/shard_map/ppermute | solution.py:592
  33.7 23.2 %collective-permute-start.2 = (bf16[2,256,256]{2,1,0:T(8,128)(2,1)S(1)}, bf16[2,256,256]{2,1,0:T(8,128)(2,1)S(1)}, u32[]{:S(2)}, u32[]{:S(2)}) collective-permute-start(bf16[2,256,256]{2,1,0:T(8,128)(2,1)S(1)} %pad_maximum_fusion.5), channel_id=1, source_target_pairs={{0,16},{4,20},{8,24},{12,28},{16,0},{20,4},{24,8},{28,12},{1,17},{... | collective-permute-start | bytes 786440 | tf_op jit(solution)/shard_map/ppermute | solution.py:592
  33.7 23.5 %collective-permute-start.3 = (bf16[2,256,256]{2,1,0:T(8,128)(2,1)S(1)}, bf16[2,256,256]{2,1,0:T(8,128)(2,1)S(1)}, u32[]{:S(2)}, u32[]{:S(2)}) collective-permute-start(bf16[2,256,256]{2,1,0:T(8,128)(2,1)S(1)} %pad_maximum_fusion.6), channel_id=1, source_target_pairs={{0,12},{4,8},{8,4},{12,0},{16,28},{20,24},{24,20},{28,16},{1,13},{... | collective-permute-start | bytes 786440 | tf_op jit(solution)/shard_map/ppermute | solution.py:592
  44.6 16.8 %collective-permute-start.4 = (bf16[2,256,256]{2,1,0:T(8,128)(2,1)S(1)}, bf16[2,256,256]{2,1,0:T(8,128)(2,1)S(1)}, u32[]{:S(2)}, u32[]{:S(2)}) collective-permute-start(bf16[2,256,256]{2,1,0:T(8,128)(2,1)S(1)} %pad_maximum_fusion.7), channel_id=1, source_target_pairs={{0,8},{4,12},{8,0},{12,4},{16,24},{20,28},{24,16},{28,20},{1,9},{5... | collective-permute-start | bytes 786440 | tf_op jit(solution)/shard_map/ppermute | solution.py:592
  47.1 15.0 %collective-permute-start.6 = (bf16[2,256,256]{2,1,0:T(8,128)(2,1)S(1)}, bf16[2,256,256]{2,1,0:T(8,128)(2,1)S(1)}, u32[]{:S(2)}, u32[]{:S(2)}) collective-permute-start(bf16[2,256,256]{2,1,0:T(8,128)(2,1)S(1)} %pad_maximum_fusion.9), channel_id=1, source_target_pairs={{0,4},{4,0},{8,12},{12,8},{16,20},{20,16},{24,28},{28,24},{1,5},{5... | collective-permute-start | bytes 786440 | tf_op jit(solution)/shard_map/ppermute | solution.py:592
  48.7 13.4 %copy-start.2 = (f32[32]{0:T(128)S(1)}, f32[32]{0:T(128)}, u32[]{:S(2)}) copy-start(f32[32]{0:T(128)} %skip_ref.1) | copy-start | bytes 388
  66.9 4.6 %copy-start.6 = (f32[2048]{0:T(1024)S(1)}, f32[2048]{0:T(1024)}, u32[]{:S(2)}) copy-start(f32[2048]{0:T(1024)} %param.28) | copy-start | bytes 24580
  68.0 7.3 %collective-permute-start.11 = (bf16[256,256]{1,0:T(8,128)(2,1)S(1)}, bf16[256,256]{1,0:T(8,128)(2,1)S(1)}, u32[]{:S(2)}, u32[]{:S(2)}) collective-permute-start(bf16[256,256]{1,0:T(8,128)(2,1)S(1)} %get-tuple-element.34), channel_id=1, source_target_pairs={{0,4},{4,0},{8,12},{12,8},{16,20},{20,16},{24,28},{28,24},{1,5},{5... | collective-permute-start | bytes 393224 | tf_op jit(solution)/shard_map/ppermute | solution.py:592
  68.9 8.3 %collective-permute-start.12 = (bf16[256,256]{1,0:T(8,128)(2,1)S(1)}, bf16[256,256]{1,0:T(8,128)(2,1)S(1)}, u32[]{:S(2)}, u32[]{:S(2)}) collective-permute-start(bf16[256,256]{1,0:T(8,128)(2,1)S(1)} %get-tuple-element.35), channel_id=1, source_target_pairs={{0,8},{4,12},{8,0},{12,4},{16,24},{20,28},{24,16},{28,20},{1,9},{5... | collective-permute-start | bytes 393224 | tf_op jit(solution)/shard_map/ppermute | solution.py:592
  71.4 7.3 %collective-permute-start.13 = (bf16[256,256]{1,0:T(8,128)(2,1)S(1)}, bf16[256,256]{1,0:T(8,128)(2,1)S(1)}, u32[]{:S(2)}, u32[]{:S(2)}) collective-permute-start(bf16[256,256]{1,0:T(8,128)(2,1)S(1)} %get-tuple-element.36), channel_id=1, source_target_pairs={{0,12},{4,8},{8,4},{12,0},{16,28},{20,24},{24,20},{28,16},{1,13},{... | collective-permute-start | bytes 393224 | tf_op jit(solution)/shard_map/ppermute | solution.py:592
  71.5 13.7 %collective-permute-start.14 = (bf16[256,256]{1,0:T(8,128)(2,1)S(1)}, bf16[256,256]{1,0:T(8,128)(2,1)S(1)}, u32[]{:S(2)}, u32[]{:S(2)}) collective-permute-start(bf16[256,256]{1,0:T(8,128)(2,1)S(1)} %get-tuple-element.39), channel_id=1, source_target_pairs={{0,16},{4,20},{8,24},{12,28},{16,0},{20,4},{24,8},{28,12},{1,17},{... | collective-permute-start | bytes 393224 | tf_op jit(solution)/shard_map/ppermute | solution.py:592
  72.2 17.9 %collective-permute-start.15 = (bf16[256,256]{1,0:T(8,128)(2,1)S(1)}, bf16[256,256]{1,0:T(8,128)(2,1)S(1)}, u32[]{:S(2)}, u32[]{:S(2)}) collective-permute-start(bf16[256,256]{1,0:T(8,128)(2,1)S(1)} %get-tuple-element.40), channel_id=1, source_target_pairs={{0,20},{4,16},{8,28},{12,24},{16,4},{20,0},{24,12},{28,8},{1,21},{... | collective-permute-start | bytes 393224 | tf_op jit(solution)/shard_map/ppermute | solution.py:592
  75.2 20.4 %collective-permute-start.16 = (bf16[256,256]{1,0:T(8,128)(2,1)S(1)}, bf16[256,256]{1,0:T(8,128)(2,1)S(1)}, u32[]{:S(2)}, u32[]{:S(2)}) collective-permute-start(bf16[256,256]{1,0:T(8,128)(2,1)S(1)} %get-tuple-element.41), channel_id=1, source_target_pairs={{0,24},{4,28},{8,16},{12,20},{16,8},{20,12},{24,0},{28,4},{1,25},{... | collective-permute-start | bytes 393224 | tf_op jit(solution)/shard_map/ppermute | solution.py:592
  77.2 20.7 %collective-permute-start.17 = (bf16[256,256]{1,0:T(8,128)(2,1)S(1)}, bf16[256,256]{1,0:T(8,128)(2,1)S(1)}, u32[]{:S(2)}, u32[]{:S(2)}) collective-permute-start(bf16[256,256]{1,0:T(8,128)(2,1)S(1)} %get-tuple-element.42), channel_id=1, source_target_pairs={{0,28},{4,24},{8,20},{12,16},{16,12},{20,8},{24,4},{28,0},{1,29},{... | collective-permute-start | bytes 393224 | tf_op jit(solution)/shard_map/ppermute | solution.py:592
  100.9 2.0 %collective-permute-start.18 = (bf16[128,2048]{1,0:T(8,128)(2,1)S(1)}, bf16[128,2048]{1,0:T(8,128)(2,1)S(1)}, u32[]{:S(2)}, u32[]{:S(2)}) collective-permute-start(bf16[128,2048]{1,0:T(8,128)(2,1)S(1)} %get-tuple-element.44), channel_id=1, source_target_pairs={{0,1},{1,0},{2,3},{3,2},{4,5},{5,4},{6,7},{7,6},{8,9},{9,8},{10,11... | collective-permute-start | bytes 1572872 | tf_op jit(solution)/shard_map/ppermute | solution.py:744
  101.0 3.6 %collective-permute-start.20 = (bf16[128,2048]{1,0:T(8,128)(2,1)S(1)}, bf16[128,2048]{1,0:T(8,128)(2,1)S(1)}, u32[]{:S(2)}, u32[]{:S(2)}) collective-permute-start(bf16[128,2048]{1,0:T(8,128)(2,1)S(1)} %get-tuple-element.46), channel_id=1, source_target_pairs={{0,1},{1,0},{2,3},{3,2},{4,5},{5,4},{6,7},{7,6},{8,9},{9,8},{10,11... | collective-permute-start | bytes 1572872 | tf_op jit(solution)/shard_map/ppermute | solution.py:744
  103.1 9.2 %collective-permute-start.19 = (bf16[64,2048]{1,0:T(8,128)(2,1)S(1)}, bf16[64,2048]{1,0:T(8,128)(2,1)S(1)}, u32[]{:S(2)}, u32[]{:S(2)}) collective-permute-start(bf16[64,2048]{1,0:T(8,128)(2,1)S(1)} %slice.17), channel_id=1, source_target_pairs={{0,2},{1,3},{2,0},{3,1},{4,6},{5,7},{6,4},{7,5},{8,10},{9,11},{10,... | collective-permute-start | bytes 786440 | tf_op jit(solution)/shard_map/ppermute | solution.py:744
  104.8 12.3 %collective-permute-start.21 = (bf16[64,2048]{1,0:T(8,128)(2,1)S(1)}, bf16[64,2048]{1,0:T(8,128)(2,1)S(1)}, u32[]{:S(2)}, u32[]{:S(2)}) collective-permute-start(bf16[64,2048]{1,0:T(8,128)(2,1)S(1)} %slice.19), channel_id=1, source_target_pairs={{0,2},{1,3},{2,0},{3,1},{4,6},{5,7},{6,4},{7,5},{8,10},{9,11},{10,... | collective-permute-start | bytes 786440 | tf_op jit(solution)/shard_map/ppermute | solution.py:744

commit v4 on v3

--- a/solution.py
+++ b/solution.py
@@ -414,26 +414,20 @@
     lax.fori_loop(0, chunks_step, one_chunk, 0, unroll=2)
 
 
-def scan_kernel(
-    heads, per_dev, chunks_step, turns, me_ref, order_ref, skip_ref, taps_ref, *refs
-):
+def scan_kernel(heads, per_dev, turns, place_ref, order_ref, skip_ref, taps_ref, *refs):
     piece_refs, refs = refs[: len(turns)], refs[len(turns) :]
-    mix_ref, query_ref, key_ref, tail_ref, inflow_ref, gate_ref, since_ref, out_ref = refs[:8]
-    sequence, previous, state = refs[8:]
-    me = me_ref[0]
-    step_id = pl.program_id(0)
-
-    @pl.when(step_id == 0)
-    def _():
-        previous[...] = jnp.zeros_like(previous)
-        state[...] = jnp.zeros_like(state)
-        for turn, piece_ref in zip(turns, piece_refs):
-            loader = jnp.bitwise_xor(me, turn)
-            for b in range(per_dev):
-                place = order_ref[loader * per_dev + b]
-                rows = pl.ds(pl.multiple_of(place * BLK, BLK), BLK)
-                sequence[rows, :] = piece_ref[b * BLK : (b + 1) * BLK, :]
-
+    mix_ref, query_ref, key_ref, tail_ref, inflow_ref, gate_ref, since_ref = refs[:7]
+    out_refs, (sequence, gates, laid, previous, state) = refs[7:-5], refs[-5:]
+    me, mine = place_ref[0], place_ref[1]
+    previous[...] = jnp.zeros_like(previous)
+    state[...] = jnp.zeros_like(state)
+    for turn, piece_ref in zip(turns, piece_refs):
+        loader = jnp.bitwise_xor(me, turn)
+        for b in range(per_dev):
+            place = order_ref[loader * per_dev + b]
+            rows = pl.ds(pl.multiple_of(place * BLK, BLK), BLK)
+            sequence[rows, :] = piece_ref[0, b * BLK : (b + 1) * BLK, :]
+            gates[rows, :] = piece_ref[1, b * BLK : (b + 1) * BLK, :]
     width = heads * HEAD_DIM
     lane = lax.broadcasted_iota(jnp.int32, (1, width), 1)
     skip = jnp.zeros((1, width), jnp.float32)
@@ -441,58 +435,48 @@
         skip = jnp.where(lane >= h * HEAD_DIM, skip_ref[me * heads + h], skip)
     low_half = lax.broadcasted_iota(jnp.int32, (CHUNK, LANES), 1) < HEAD_DIM
     taps = taps_ref[...]
-
-    def one_chunk(local, carry):
-        chunk = step_id * chunks_step + local
+    blocks = CHUNK // BLK
+
+    def one_chunk(chunk, carry):
         rows = pl.ds(pl.multiple_of(chunk * CHUNK, CHUNK), CHUNK)
         current = sequence[rows, :].astype(jnp.float32)
-        wide_since = jnp.concatenate([since_ref[local]] * (width // LANES), axis=1)
+        wide_since = jnp.concatenate([since_ref[chunk]] * (width // LANES), axis=1)
         values = tapped(current, previous[...], taps, wide_since).astype(jnp.bfloat16)
         previous[...] = current[CHUNK - 8 :]
         values_wide = values.astype(jnp.float32)
         entering = state[...]
         carried = jnp.dot(
-            query_ref[local], entering.astype(jnp.bfloat16), preferred_element_type=jnp.float32
-        )
-        total = carried * inflow_ref[local] + skip * values_wide
-        tail_values = (values_wide * tail_ref[local]).astype(jnp.bfloat16)
-        state[...] = gate_ref[local, :1, :] * entering + jnp.dot(
-            key_ref[local], tail_values, preferred_element_type=jnp.float32
+            query_ref[chunk], entering.astype(jnp.bfloat16), preferred_element_type=jnp.float32
+        )
+        total = carried * inflow_ref[chunk] + skip * values_wide
+        tail_values = (values_wide * tail_ref[chunk]).astype(jnp.bfloat16)
+        state[...] = gate_ref[chunk, :1, :] * entering + jnp.dot(
+            key_ref[chunk], tail_values, preferred_element_type=jnp.float32
         )
         zero = jnp.zeros((CHUNK, LANES), jnp.bfloat16)
+        intra = []
         for pair in range(heads // 2):
-            at = slice(pair * LANES, (pair + 1) * LANES)
-            both = values[:, at]
+            both = values[:, pair * LANES : (pair + 1) * LANES]
             block = jnp.concatenate(
                 [jnp.where(low_half, both, zero), jnp.where(low_half, zero, both)], axis=0
             )
-            intra = jnp.dot(
-                mix_ref[local, :, 2 * pair * CHUNK : 2 * (pair + 1) * CHUNK],
-                block,
-                preferred_element_type=jnp.float32,
-            )
-            out_ref[local, :, at] = total[:, at] + intra
-        return carry
-
-    lax.fori_loop(0, chunks_step, one_chunk, 0, unroll=2)
-
-
-def gating_kernel(per_dev, turns, place_ref, order_ref, mixed_ref, *refs):
-    piece_refs, out_refs, laid = refs[: len(turns)], refs[len(turns) : -1], refs[-1]
-    me, mine = place_ref[0], place_ref[1]
-    for turn, piece_ref in zip(turns, piece_refs):
-        loader = jnp.bitwise_xor(me, turn)
-        for b in range(per_dev):
-            place = order_ref[loader * per_dev + b]
-            gates = piece_ref[b * BLK : (b + 1) * BLK, :].astype(jnp.float32)
-            mixed = mixed_ref[pl.ds(pl.multiple_of(place * BLK, BLK), BLK), :]
-            gated = (mixed * silu(gates)).astype(jnp.bfloat16)
-            owner_turn = jnp.bitwise_xor(lax.div(place, per_dev), me)
+            weights = mix_ref[chunk, :, 2 * pair * CHUNK : 2 * (pair + 1) * CHUNK]
+            intra.append(jnp.dot(weights, block, preferred_element_type=jnp.float32))
+        mixed = total + jnp.concatenate(intra, axis=1)
+        gated = (mixed * silu(gates[rows, :].astype(jnp.float32))).astype(jnp.bfloat16)
+        for block in range(blocks):
+            place = chunk * blocks + block
             away = jnp.bitwise_xor(lax.rem(place, per_dev), mine)
             slot = 2 * (1 - lax.rem(away, 2)) + (1 - lax.div(away, 2))
-            laid[owner_turn, pl.ds(pl.multiple_of(slot * BLK, BLK), BLK), :] = gated
-    for turn, out_ref in enumerate(out_refs):
-        out_ref[...] = laid[turn]
+            start = pl.multiple_of(slot * BLK, BLK)
+            laid[lax.div(place, per_dev), pl.ds(start, BLK), :] = gated[
+                block * BLK : (block + 1) * BLK
+            ]
+        return carry
+
+    lax.fori_loop(0, mix_ref.shape[0], one_chunk, 0, unroll=2)
+    for turn, out_ref in zip(turns, out_refs):
+        out_ref[...] = laid[jnp.bitwise_xor(me, turn)]
 
 
 def normed_into(normed, gated_refs, gain_ref, me, first_turn):
@@ -537,21 +521,26 @@
     onward.wait()
 
 
-def far_kernel(parts, place_ref, gain_ref, weight_ref, near_ref, *refs):
-    gated_refs, refs = refs[: -2 * parts - 1], refs[-2 * parts - 1 :]
-    away_refs, stay_refs, normed = refs[:parts], refs[parts:-1], refs[-1]
+def project_far(normed, weight_ref, near_ref, at, away_ref, stay_ref):
+    partial = near_ref[:, at] + jnp.dot(
+        normed, weight_ref[:, at], preferred_element_type=jnp.float32
+    )
+    partial = partial.astype(jnp.bfloat16)
+    rows = partial.shape[0] // 2
+    away_ref[...] = partial[:rows]
+    stay_ref[...] = partial[rows:]
+
+
+def far_kernel(place_ref, gain_ref, weight_ref, near_ref, *refs):
+    gated_refs, (away_ref, stay_ref, normed) = refs[:-3], refs[-3:]
     normed_into(normed, gated_refs, gain_ref, place_ref[0], len(gated_refs))
-    rows, columns = away_refs[0].shape
-    tile = 1024
-    for part in range(parts):
-        for first in range(0, columns, tile):
-            at = slice(part * columns + first, part * columns + first + tile)
-            partial = near_ref[:, at] + jnp.dot(
-                normed[...], weight_ref[:, at], preferred_element_type=jnp.float32
-            )
-            partial = partial.astype(jnp.bfloat16)
-            away_refs[part][:, first : first + tile] = partial[:rows]
-            stay_refs[part][:, first : first + tile] = partial[rows:]
+    at = slice(0, away_ref.shape[1])
+    project_far(normed[...], weight_ref, near_ref, at, away_ref, stay_ref)
+
+
+def rest_kernel(place_ref, normed_ref, weight_ref, near_ref, away_ref, stay_ref):
+    at = slice(near_ref.shape[1] - away_ref.shape[1], near_ref.shape[1])
+    project_far(normed_ref[...], weight_ref, near_ref, at, away_ref, stay_ref)
 
 
 def head_split(
@@ -605,7 +594,7 @@
 
     held = jnp.stack([for_group(my_group), turned(for_group(my_group ^ 1), near)])
     group_rows = [held] + [turned(held, turn) for turn in range(1, near)]
-    turns = (0, 6, 7, 4, 3, 2, 5, 1)
+    turns = (0, 1, 2, 3, 4, 5, 6, 7)
     head_rows = [turned(for_heads(turn), turn) if turn else for_heads(turn) for turn in turns]
 
     key_taps = lax.dynamic_slice_in_dim(conv_keys, my_group * STATE, STATE, 1)
@@ -654,41 +643,25 @@
         name="mixing",
     )(place, block_order, doc_lengths, step_bias, decay_log, key_taps, query_taps, *group_rows)
 
-    mixed = pl.pallas_call(
-        functools.partial(scan_kernel, heads, per_dev, chunks_step, turns),
-        grid=(grid_steps,),
-        in_specs=[smem] * 3
-        + [whole(value_taps)]
-        + [pl.BlockSpec((None, token_count, width), lambda i: (0, 0, 0))] * ctx_count
-        + [per_step(*shape) for shape, _ in mix_shapes],
-        out_specs=per_step(CHUNK, width),
-        out_shape=jax.ShapeDtypeStruct((chunks, CHUNK, width), jnp.float32),
+    gated = pl.pallas_call(
+        functools.partial(scan_kernel, heads, per_dev, turns),
+        in_specs=[smem] * 3 + [vmem] * (1 + ctx_count + len(mix_shapes)),
+        out_specs=[vmem] * ctx_count,
+        out_shape=[jax.ShapeDtypeStruct((token_count, width), jnp.bfloat16)] * ctx_count,
         scratch_shapes=[
             pltpu.VMEM((total_tokens, width), jnp.bfloat16),
+            pltpu.VMEM((total_tokens, width), jnp.bfloat16),
+            pltpu.VMEM((ctx_count, token_count, width), jnp.bfloat16),
             pltpu.VMEM((8, width), jnp.float32),
             pltpu.VMEM((STATE, width), jnp.float32),
         ],
         compiler_params=params,
         cost_estimate=pl.CostEstimate(
-            flops=600_000_000, bytes_accessed=14_000_000, transcendentals=600_000
+            flops=600_000_000, bytes_accessed=14_000_000, transcendentals=1_200_000
         ),
         name="scan",
     )(place, block_order, skip_gain, value_taps, *head_rows, *mixing)
-
-    gated = pl.pallas_call(
-        functools.partial(gating_kernel, per_dev, turns),
-        grid=(1,),
-        in_specs=[smem, smem, pl.BlockSpec((total_tokens, width), lambda i: (0, 0))]
-        + [pl.BlockSpec((None, token_count, width), lambda i: (1, 0, 0))] * ctx_count,
-        out_specs=[pl.BlockSpec((token_count, width), lambda i: (0, 0))] * ctx_count,
-        out_shape=[jax.ShapeDtypeStruct((token_count, width), jnp.bfloat16)] * ctx_count,
-        scratch_shapes=[pltpu.VMEM((ctx_count, token_count, width), jnp.bfloat16)],
-        compiler_params=params,
-        cost_estimate=pl.CostEstimate(
-            flops=5_000_000, bytes_accessed=4_000_000, transcendentals=600_000
-        ),
-        name="gating",
-    )(place, block_order, mixed.reshape(total_tokens, width), *head_rows)
+    gated = dict(zip(turns, gated))
 
     pieces = [gated[0]] + [turned(gated[turn], turn) for turn in range(1, ctx_count)]
 
@@ -697,13 +670,13 @@
     gain = norm_gain.reshape(ctx_count, width)
     weight = out_weight.reshape(groups, group_width, columns)
 
-    def project(kernel, weight, weight_space, operands, out_shape, scratch, limit, name):
+    def project(kernel, first, weight, weight_space, operands, out_shape, scratch, limit, name):
         return pl.pallas_call(
             kernel,
             in_specs=[smem, vmem, pl.BlockSpec(memory_space=weight_space)] + [vmem] * len(operands),
             out_specs=[vmem] * len(out_shape),
             out_shape=out_shape,
-            scratch_shapes=[pltpu.VMEM((token_count, group_width), jnp.bfloat16)] + scratch,
+            scratch_shapes=scratch,
             compiler_params=pltpu.CompilerParams(vmem_limit_bytes=limit * 1024 * 1024),
             cost_estimate=pl.CostEstimate(
                 flops=2 * token_count * group_width * columns,
@@ -711,10 +684,11 @@
                 transcendentals=0,
             ),
             name=name,
-        )(place, gain, weight, *operands)
+        )(place, first, weight, *operands)
 
     near_partial, far_weight = project(
         near_kernel,
+        gain,
         weight,
         pl.ANY,
         pieces[:near],
@@ -722,30 +696,50 @@
             jax.ShapeDtypeStruct((token_count, columns), jnp.float32),
             jax.ShapeDtypeStruct((group_width, columns), jnp.bfloat16),
         ],
-        [pltpu.VMEM((group_width, columns), jnp.bfloat16), pltpu.SemaphoreType.DMA((5,))],
+        [
+            pltpu.VMEM((token_count, group_width), jnp.bfloat16),
+            pltpu.VMEM((group_width, columns), jnp.bfloat16),
+            pltpu.SemaphoreType.DMA((5,)),
+        ],
         28,
         "near_projection",
     )
-    parts = 2
     rows = token_count // 2
-    part_shape = jax.ShapeDtypeStruct((rows, columns // parts), jnp.bfloat16)
-    split = project(
-        functools.partial(far_kernel, parts),
+    normed_shape = jax.ShapeDtypeStruct((token_count, group_width), jnp.bfloat16)
+
+    def part_shape(part_columns):
+        return jax.ShapeDtypeStruct((rows, part_columns), jnp.bfloat16)
+
+    first_columns = columns // 2
+    away, stay, far_normed = project(
+        far_kernel,
+        gain,
         far_weight,
         pltpu.VMEM,
         [near_partial] + pieces[near:],
-        [part_shape] * (2 * parts),
+        [part_shape(first_columns)] * 2 + [normed_shape],
         [],
         8,
         "far_projection",
     )
+    rest_away, rest_stay = project(
+        rest_kernel,
+        far_normed,
+        far_weight,
+        pltpu.VMEM,
+        [near_partial],
+        [part_shape(columns - first_columns)] * 2,
+        [],
+        8,
+        "rest_projection",
+    )
 
     def joined(kept, sent, turn):
         came = lax.ppermute(sent, "tp", [(i, i ^ turn) for i in range(tp_count)])
         return (kept.astype(jnp.float32) + came.astype(jnp.float32)).astype(jnp.bfloat16)
 
     results = []
-    for away, stay in zip(split[:parts], split[parts:]):
+    for away, stay in ((away, stay), (rest_away, rest_stay)):
         across = joined(stay, away, 1)
         results.append(joined(across[rows // 2 :], across[: rows // 2], 2))
     return jnp.concatenate(results, axis=1)

time: 118 us -> 117 us (level)
  waiting for transfers between devices: 47.2 us -> 40.6 us
  starting transfers between devices: 41 us -> 46.2 us
    ppermute x18, starting transfers between devices: 38.3 us -> 42.6 us  [turned(): return lax.ppermute(value, 'ctx', [(i, i ^ turn) for i in range(ctx_count)])]
    ppermute x18, waiting for transfers between devices: 34.2 us -> 29.8 us  [turned(): return lax.ppermute(value, 'ctx', [(i, i ^ turn) for i in range(ctx_count)])]
    ppermute x4, waiting for transfers between devices: 13 us -> 10.8 us  [joined(): came = lax.ppermute(sent, 'tp', [(i, i ^ turn) for i in range(tp_count)])]
    pallas_call x2 -> x1, Pallas kernels: 5.9 us -> 4.9 us  [head_split(): pl.pallas_call(functools.partial(scan_kernel, heads, per_dev, turns), in_...]
    pallas_call x2 -> x3, Pallas kernels: 9.6 us -> 10.3 us  [project(): pl.pallas_call(kernel, in_specs=[smem, vmem, pl.BlockSpec(memory_space=we...]
  transfers between devices with their start and end apart: 22 -> 22, of which waited for: 14 -> 13; matrix products, arithmetic and copies ran while one was open for 3% -> 3% of each run, Pallas kernels for 12% -> 14%
where the time goes in v4:
time: 117 us; the launch traced here: 116 us
  starting transfers between devices  46.2 us (39%)
  waiting for transfers between devices  40.6 us (35%)
  Pallas kernels  23.3 us (20%)
  local copies, waits for them, and re-layouts  3.57 us (3%)
  other arithmetic  2.26 us (2%)
    ppermute x18, starting transfers between devices, turned(): return lax.ppermute(value, 'ctx', [(i, i ^ turn) for i in range(ctx_count)])  42.6 us
    ppermute x18, waiting for transfers between devices, turned(): return lax.ppermute(value, 'ctx', [(i, i ^ turn) for i in range(ctx_count)])  29.8 us
    ppermute x4, waiting for transfers between devices, joined(): came = lax.ppermute(sent, 'tp', [(i, i ^ turn) for i in range(tp_count)])  10.8 us
    pallas_call x3, Pallas kernels, project(): pl.pallas_call(kernel, in_specs=[smem, vmem, pl.BlockSpec(memory_space=we...  10.3 us
    pallas_call x1, Pallas kernels, head_split(): pl.pallas_call(functools.partial(mixing_kernel, heads, group_heads, per_d...  8.14 us
    pallas_call x1, Pallas kernels, head_split(): pl.pallas_call(functools.partial(scan_kernel, heads, per_dev, turns), in_...  4.9 us
    ppermute x4, starting transfers between devices, joined(): came = lax.ppermute(sent, 'tp', [(i, i ^ turn) for i in range(tp_count)])  3.56 us
  transfers between devices with their start and end apart: 22, of which 13 were waited for; matrix products, arithmetic and copies ran while one was open for 3% of the time, Pallas kernels for 14%

profile of v4, /device:TPU:16, one launch (start us, length us, event | category | flops | bytes accessed | tf_op | source)
XLA Modules:
  0.0 116.3 jit_solution(5957831362415780979)
XLA Ops:
  0.0 0.7 dynamic-slice_bitcast_fusion.17
  0.7 1.0 constant_dynamic-slice_fusion.2
  1.7 0.1 collective-permute-start.7
  1.9 1.8 %dynamic-slice_bitcast_fusion = (bf16[1,256,256]{2,1,0:T(8,128)(2,1)S(1)}, bf16[1,256,256]{2,1,0:T(8,128)(2,1)S(1)}, bf16[1,256,256]{2,1,0:T(8,128)(2,1)S(1)}, b...) fusion(bf16[256,2048]{1,0:T(8,128)(2,1)} %param.16, ...), kind=kLoop, calls=%fused_computation.16 | loop fusion | bytes 4194336 | tf_op jit(solution)/shard_map/stack | solution.py:591
  3.7 0.7 pad_maximum_fusion.7
  4.4 3.8 %collective-permute-start.4 = (bf16[2,256,256]{2,1,0:T(8,128)(2,1)}, bf16[2,256,256]{2,1,0:T(8,128)(2,1)S(1)}, u32[]{:S(2)}, u32[]{:S(2)}) collective-permute-start(bf16[2,256,256]{2,1,0:T(8,128)(2,1)} %pad_maximum_fusion.7), channel_id=1, source_target_pairs={{0,20},{4,16},{8,28},{12,24},{16,4},{20,0},{24,12},{28,8},{1,21},{... | collective-permute-start | bytes 786440 | tf_op jit(solution)/shard_map/ppermute | solution.py:581
  8.3 0.5 collective-permute-start.5
  9.0 15.9 %collective-permute-start.10 = (bf16[2,272,256]{2,1,0:T(8,128)(2,1)S(1)}, bf16[2,272,256]{2,1,0:T(8,128)(2,1)S(1)}, u32[]{:S(2)}, u32[]{:S(2)}) collective-permute-start(bf16[2,272,256]{2,1,0:T(8,128)(2,1)S(1)} %pad_maximum_fusion.1.refs_0_), channel_id=1, source_target_pairs={{0,12},{4,8},{8,4},{12,0},{16,28},{20,24},{24,20},{28,16},{1,13},{... | collective-permute-start | bytes 835592 | tf_op jit(solution)/shard_map/ppermute | solution.py:581
  24.9 0.5 collective-permute-start.8
  25.4 0.1 collective-permute-start.9
  25.6 0.7 collective-permute-done.4.refs_5_
  26.3 2.4 %collective-permute-start.6 = (bf16[2,256,256]{2,1,0:T(8,128)(2,1)S(1)}, bf16[2,256,256]{2,1,0:T(8,128)(2,1)S(1)}, u32[]{:S(2)}, u32[]{:S(2)}) collective-permute-start(bf16[2,256,256]{2,1,0:T(8,128)(2,1)S(1)} %pad_maximum_fusion.9), channel_id=1, source_target_pairs={{0,28},{4,24},{8,20},{12,16},{16,12},{20,8},{24,4},{28,0},{1,29},{... | collective-permute-start | bytes 786440 | tf_op jit(solution)/shard_map/ppermute | solution.py:581
  28.7 5.0 %collective-permute-done.5.refs_6_ = bf16[2,256,256]{2,1,0:T(8,128)(2,1)S(1)} collective-permute-done((bf16[2,256,256]{2,1,0:T(8,128)(2,1)S(1)}, bf16[2,256,256]{2,1,0:T(8,128)(2,1)S(1)}, u32[]{:S(2)}, u32[]{:S(2)}) %collective-permute-start.5) | collective-permute-done | bytes 262176 | tf_op jit(solution)/shard_map/ppermute | solution.py:581
  33.7 2.7 %collective-permute-start.2 = (bf16[2,256,256]{2,1,0:T(8,128)(2,1)S(1)}, bf16[2,256,256]{2,1,0:T(8,128)(2,1)S(1)}, u32[]{:S(2)}, u32[]{:S(2)}) collective-permute-start(bf16[2,256,256]{2,1,0:T(8,128)(2,1)S(1)} %pad_maximum_fusion.5), channel_id=1, source_target_pairs={{0,12},{4,8},{8,4},{12,0},{16,28},{20,24},{24,20},{28,16},{1,13},{... | collective-permute-start | bytes 786440 | tf_op jit(solution)/shard_map/ppermute | solution.py:581
  36.4 3.6 %collective-permute-done.8.refs_1_ = bf16[2,272,256]{2,1,0:T(8,128)(2,1)S(1)} collective-permute-done((bf16[2,272,256]{2,1,0:T(8,128)(2,1)S(1)}, bf16[2,272,256]{2,1,0:T(8,128)(2,1)S(1)}, u32[]{:S(2)}, u32[]{:S(2)}) %collective-permute-start.8) | collective-permute-done | bytes 278560 | tf_op jit(solution)/shard_map/ppermute | solution.py:581
  40.0 8.0 %collective-permute-start.1 = (bf16[2,256,256]{2,1,0:T(8,128)(2,1)S(1)}, bf16[2,256,256]{2,1,0:T(8,128)(2,1)S(1)}, u32[]{:S(2)}, u32[]{:S(2)}) collective-permute-start(bf16[2,256,256]{2,1,0:T(8,128)(2,1)S(1)} %pad_maximum_fusion.4), channel_id=1, source_target_pairs={{0,8},{4,12},{8,0},{12,4},{16,24},{20,28},{24,16},{28,20},{1,9},{5... | collective-permute-start | bytes 786440 | tf_op jit(solution)/shard_map/ppermute | solution.py:581
  47.9 0.5 collective-permute-start
  48.5 0.1 pad_add_fusion.me_ref.place_ref
  48.6 8.1 %mixing.1 = (bf16[16,128,512]{2,1,0:T(8,128)(2,1)S(1)}, bf16[16,128,128]{2,1,0:T(8,128)(2,1)S(1)}, bf16[16,128,128]{2,1,0:T(8,128)(2,1)S(1)}, f32[16,128,256]{2,...) custom-call(s32[2]{0:T(128)S(1)} %pad_add_fusion.me_ref.place_ref, ...), custom_call_target="tpu_custom_call" | custom-call | flops 20000000 | bytes 20000000 | tf_op jit(solution)/shard_map/mixing/pallas_call | solution.py:626
  56.8 0.5 collective-permute-done.2.refs_3_
  57.3 4.1 %collective-permute-done.1.refs_2_ = bf16[2,256,256]{2,1,0:T(8,128)(2,1)S(1)} collective-permute-done((bf16[2,256,256]{2,1,0:T(8,128)(2,1)S(1)}, bf16[2,256,256]{2,1,0:T(8,128)(2,1)S(1)}, u32[]{:S(2)}, u32[]{:S(2)}) %collective-permute-start.1) | collective-permute-done | bytes 262176 | tf_op jit(solution)/shard_map/ppermute | solution.py:581
  61.4 0.8 collective-permute-done.refs_1_
  62.2 4.9 %scan.1 = (bf16[256,256]{1,0:T(8,128)(2,1)S(1)}, bf16[256,256]{1,0:T(8,128)(2,1)S(1)}, bf16[256,256]{1,0:T(8,128)(2,1)S(1)}, bf16[256,256]{1,0:T(8,128)(2,1)S(1)...) custom-call(s32[2]{0:T(128)S(1)} %pad_add_fusion.me_ref.place_ref, ...), custom_call_target="tpu_custom_call" | custom-call | flops 600000000 | bytes 14000000 | tf_op jit(solution)/shard_map/scan/pallas_call | solution.py:646
  67.1 0.8 collective-permute-start.11
  67.9 2.5 %collective-permute-start.12 = (bf16[256,256]{1,0:T(8,128)(2,1)S(1)}, bf16[256,256]{1,0:T(8,128)(2,1)S(1)}, u32[]{:S(2)}, u32[]{:S(2)}) collective-permute-start(bf16[256,256]{1,0:T(8,128)(2,1)S(1)} %get-tuple-element.36), channel_id=1, source_target_pairs={{0,8},{4,12},{8,0},{12,4},{16,24},{20,28},{24,16},{28,20},{1,9},{5... | collective-permute-start | bytes 393224 | tf_op jit(solution)/shard_map/ppermute | solution.py:581
  70.4 0.2 collective-permute-start.13
  70.6 0.7 collective-permute-start.14
  71.3 2.9 %collective-permute-start.15 = (bf16[256,256]{1,0:T(8,128)(2,1)S(1)}, bf16[256,256]{1,0:T(8,128)(2,1)S(1)}, u32[]{:S(2)}, u32[]{:S(2)}) collective-permute-start(bf16[256,256]{1,0:T(8,128)(2,1)S(1)} %get-tuple-element.41), channel_id=1, source_target_pairs={{0,20},{4,16},{8,28},{12,24},{16,4},{20,0},{24,12},{28,8},{1,21},{... | collective-permute-start | bytes 393224 | tf_op jit(solution)/shard_map/ppermute | solution.py:581
  74.2 0.6 collective-permute-start.16
  74.9 1.3 %collective-permute-done.12.refs_2_ = bf16[256,256]{1,0:T(8,128)(2,1)S(1)} collective-permute-done((bf16[256,256]{1,0:T(8,128)(2,1)S(1)}, bf16[256,256]{1,0:T(8,128)(2,1)S(1)}, u32[]{:S(2)}, u32[]{:S(2)}) %collective-permute-start.12) | collective-permute-done | bytes 131104 | tf_op jit(solution)/shard_map/ppermute | solution.py:581
  76.2 0.3 collective-permute-start.17
  76.5 1.2 %collective-permute-done.13.refs_3_ = bf16[256,256]{1,0:T(8,128)(2,1)S(1)} collective-permute-done((bf16[256,256]{1,0:T(8,128)(2,1)S(1)}, bf16[256,256]{1,0:T(8,128)(2,1)S(1)}, u32[]{:S(2)}, u32[]{:S(2)}) %collective-permute-start.13) | collective-permute-done | bytes 131104 | tf_op jit(solution)/shard_map/ppermute | solution.py:581
  77.7 6.5 %near_projection.1 = (f32[256,4096]{1,0:T(8,128)S(1)}, bf16[1024,4096]{1,0:T(8,128)(2,1)S(1)}) custom-call(s32[2]{0:T(128)S(1)} %pad_add_fusion.me_ref.place_ref, f32[8,256]{1,0:T(8,128)S(1)} %reshape.6.gain_ref, bf16[2,1024,4096]{2,1,0:T(8,128)(2,1)} %bitcast.42, bf16[256,256]{1,0:T(8,128)(2,1)S(1)} %get-tuple-element.34.refs_0_, ...), custom_call_target="tpu_custom_call" | custom-call | flops 2147483648 | bytes 8388608 | tf_op jit(solution)/shard_map/near_projection/pallas_call | solution.py:674
  84.3 4.8 %collective-permute-done.15.refs_1_ = bf16[256,256]{1,0:T(8,128)(2,1)S(1)} collective-permute-done((bf16[256,256]{1,0:T(8,128)(2,1)S(1)}, bf16[256,256]{1,0:T(8,128)(2,1)S(1)}, u32[]{:S(2)}, u32[]{:S(2)}) %collective-permute-start.15) | collective-permute-done | bytes 131104 | tf_op jit(solution)/shard_map/ppermute | solution.py:581
  89.1 5.6 %collective-permute-done.16.refs_2_ = bf16[256,256]{1,0:T(8,128)(2,1)S(1)} collective-permute-done((bf16[256,256]{1,0:T(8,128)(2,1)S(1)}, bf16[256,256]{1,0:T(8,128)(2,1)S(1)}, u32[]{:S(2)}, u32[]{:S(2)}) %collective-permute-start.16) | collective-permute-done | bytes 131104 | tf_op jit(solution)/shard_map/ppermute | solution.py:581
  94.7 2.2 %collective-permute-done.17.refs_3_ = bf16[256,256]{1,0:T(8,128)(2,1)S(1)} collective-permute-done((bf16[256,256]{1,0:T(8,128)(2,1)S(1)}, bf16[256,256]{1,0:T(8,128)(2,1)S(1)}, u32[]{:S(2)}, u32[]{:S(2)}) %collective-permute-start.17) | collective-permute-done | bytes 131104 | tf_op jit(solution)/shard_map/ppermute | solution.py:581
  96.8 2.0 %far_projection.1 = (bf16[128,2048]{1,0:T(8,128)(2,1)S(1)}, bf16[128,2048]{1,0:T(8,128)(2,1)S(1)}, bf16[256,1024]{1,0:T(8,128)(2,1)S(1)}) custom-call(s32[2]{0:T(128)S(1)} %pad_add_fusion.me_ref.place_ref, f32[8,256]{1,0:T(8,128)S(1)} %reshape.6.gain_ref, bf16[1024,4096]{1,0:T(8,128)(2,1)S(1)} %get-tuple-element.38.weight_ref, ...), custom_call_target="tpu_custom_call" | custom-call | flops 2147483648 | bytes 8388608 | tf_op jit(solution)/shard_map/far_projection/pallas_call | solution.py:674
  98.9 0.1 collective-permute-start.18
  98.9 1.8 %rest_projection.1 = (bf16[128,2048]{1,0:T(8,128)(2,1)S(1)}, bf16[128,2048]{1,0:T(8,128)(2,1)S(1)}) custom-call(s32[2]{0:T(128)S(1)} %pad_add_fusion.me_ref.place_ref, bf16[256,1024]{1,0:T(8,128)(2,1)S(1)} %get-tuple-element.46.normed_ref, bf16[1024,4096]{1,0:T(8,128)(2,1)S(1)} %get-tuple-element.38.weight_ref, f32[256,4096]{1,0:T(8,128)S(1)} %get-tuple-element.39.near_ref), custom_call_target="tpu_custom_call" | custom-call | flops 2147483648 | bytes 8388608 | tf_op jit(solution)/shard_map/rest_projection/pallas_call | solution.py:674
  100.8 0.6 collective-permute-start.20
  101.3 0.1 add_convert_fusion.1
  101.5 1.6 %collective-permute-start.19 = (bf16[64,2048]{1,0:T(8,128)(2,1)S(1)}, bf16[64,2048]{1,0:T(8,128)(2,1)S(1)}, u32[]{:S(2)}, u32[]{:S(2)}) collective-permute-start(bf16[64,2048]{1,0:T(8,128)(2,1)S(1)} %slice.17), channel_id=1, source_target_pairs={{0,2},{1,3},{2,0},{3,1},{4,6},{5,7},{6,4},{7,5},{8,10},{9,11},{10,... | collective-permute-start | bytes 786440 | tf_op jit(solution)/shard_map/ppermute | solution.py:738
  103.0 0.1 add_convert_fusion
  103.2 1.4 %collective-permute-start.21 = (bf16[64,2048]{1,0:T(8,128)(2,1)S(1)}, bf16[64,2048]{1,0:T(8,128)(2,1)S(1)}, u32[]{:S(2)}, u32[]{:S(2)}) collective-permute-start(bf16[64,2048]{1,0:T(8,128)(2,1)S(1)} %slice.19), channel_id=1, source_target_pairs={{0,2},{1,3},{2,0},{3,1},{4,6},{5,7},{6,4},{7,5},{8,10},{9,11},{10,... | collective-permute-start | bytes 786440 | tf_op jit(solution)/shard_map/ppermute | solution.py:738
  104.6 6.1 %collective-permute-done.19 = bf16[64,2048]{1,0:T(8,128)(2,1)S(1)} collective-permute-done((bf16[64,2048]{1,0:T(8,128)(2,1)S(1)}, bf16[64,2048]{1,0:T(8,128)(2,1)S(1)}, u32[]{:S(2)}, u32[]{:S(2)}) %collective-permute-start.19) | collective-permute-done | bytes 262176 | tf_op jit(solution)/shard_map/ppermute | solution.py:738
  110.7 0.1 add_convert_fusion.3
  110.8 4.6 %collective-permute-done.21 = bf16[64,2048]{1,0:T(8,128)(2,1)S(1)} collective-permute-done((bf16[64,2048]{1,0:T(8,128)(2,1)S(1)}, bf16[64,2048]{1,0:T(8,128)(2,1)S(1)}, u32[]{:S(2)}, u32[]{:S(2)}) %collective-permute-start.21) | collective-permute-done | bytes 262176 | tf_op jit(solution)/shard_map/ppermute | solution.py:738
  115.5 0.8 pad_maximum_fusion
  (44 shorter events, 0.4 us)
Async XLA Ops:
  0.0 25.6 %copy-start = (f32[4,2048]{1,0:T(4,128)S(1)}, f32[4,2048]{1,0:T(4,128)}, u32[]{:S(2)}) copy-start(f32[4,2048]{1,0:T(4,128)} %param.22) | copy-start | bytes 98308
  1.7 7.2 %collective-permute-start.7 = (bf16[272,256]{1,0:T(8,128)(2,1)S(1)}, bf16[272,256]{1,0:T(8,128)(2,1)S(1)}, u32[]{:S(2)}, u32[]{:S(2)}) collective-permute-start(bf16[272,256]{1,0:T(8,128)(2,1)S(1)} %pad_maximum_fusion.10), channel_id=1, source_target_pairs={{0,16},{4,20},{8,24},{12,28},{16,0},{20,4},{24,8},{28,12},{1,17},{... | collective-permute-start | bytes 417800 | tf_op jit(solution)/shard_map/ppermute | solution.py:581
  1.8 46.7 %copy-start.7 = (f32[4,256]{1,0:T(4,128)S(1)}, f32[4,256]{1,0:T(4,128)}, u32[]{:S(2)}) copy-start(f32[4,256]{1,0:T(4,128)} %param.24) | copy-start | bytes 12292
  1.8 46.7 %copy-start.8 = (f32[4,256]{1,0:T(4,128)S(1)}, f32[4,256]{1,0:T(4,128)}, u32[]{:S(2)}) copy-start(f32[4,256]{1,0:T(4,128)} %param.23) | copy-start | bytes 12292
  1.9 46.7 %copy-start.1 = (s32[32]{0:T(128)S(1)}, s32[32]{0:T(128)}, u32[]{:S(2)}) copy-start(s32[32]{0:T(128)} %order_ref.3) | copy-start | bytes 388
  1.9 46.7 %copy-start.3 = (s32[16]{0:T(128)S(1)}, s32[16]{0:T(128)}, u32[]{:S(2)}) copy-start(s32[16]{0:T(128)} %lengths_ref.1) | copy-start | bytes 196
  1.9 46.7 %copy-start.4 = (f32[32]{0:T(128)S(1)}, f32[32]{0:T(128)}, u32[]{:S(2)}) copy-start(f32[32]{0:T(128)} %bias_ref.1) | copy-start | bytes 388
  1.9 46.7 %copy-start.5 = (f32[32]{0:T(128)S(1)}, f32[32]{0:T(128)}, u32[]{:S(2)}) copy-start(f32[32]{0:T(128)} %log_ref.1) | copy-start | bytes 388
  4.4 57.7 %copy-start.2 = (f32[32]{0:T(128)S(1)}, f32[32]{0:T(128)}, u32[]{:S(2)}) copy-start(f32[32]{0:T(128)} %skip_ref.1) | copy-start | bytes 388
  4.4 21.9 %collective-permute-start.4 = (bf16[2,256,256]{2,1,0:T(8,128)(2,1)}, bf16[2,256,256]{2,1,0:T(8,128)(2,1)S(1)}, u32[]{:S(2)}, u32[]{:S(2)}) collective-permute-start(bf16[2,256,256]{2,1,0:T(8,128)(2,1)} %pad_maximum_fusion.7), channel_id=1, source_target_pairs={{0,20},{4,16},{8,28},{12,24},{16,4},{20,0},{24,12},{28,8},{1,21},{... | collective-permute-start | bytes 786440 | tf_op jit(solution)/shard_map/ppermute | solution.py:581
  8.3 25.4 %collective-permute-start.5 = (bf16[2,256,256]{2,1,0:T(8,128)(2,1)S(1)}, bf16[2,256,256]{2,1,0:T(8,128)(2,1)S(1)}, u32[]{:S(2)}, u32[]{:S(2)}) collective-permute-start(bf16[2,256,256]{2,1,0:T(8,128)(2,1)S(1)} %pad_maximum_fusion.8), channel_id=1, source_target_pairs={{0,24},{4,28},{8,16},{12,20},{16,8},{20,12},{24,0},{28,4},{1,25},{... | collective-permute-start | bytes 786440 | tf_op jit(solution)/shard_map/ppermute | solution.py:581
  9.0 24.8 %collective-permute-start.10 = (bf16[2,272,256]{2,1,0:T(8,128)(2,1)S(1)}, bf16[2,272,256]{2,1,0:T(8,128)(2,1)S(1)}, u32[]{:S(2)}, u32[]{:S(2)}) collective-permute-start(bf16[2,272,256]{2,1,0:T(8,128)(2,1)S(1)} %pad_maximum_fusion.1.refs_0_), channel_id=1, source_target_pairs={{0,12},{4,8},{8,4},{12,0},{16,28},{20,24},{24,20},{28,16},{1,13},{... | collective-permute-start | bytes 835592 | tf_op jit(solution)/shard_map/ppermute | solution.py:581
  24.9 15.1 %collective-permute-start.8 = (bf16[2,272,256]{2,1,0:T(8,128)(2,1)S(1)}, bf16[2,272,256]{2,1,0:T(8,128)(2,1)S(1)}, u32[]{:S(2)}, u32[]{:S(2)}) collective-permute-start(bf16[2,272,256]{2,1,0:T(8,128)(2,1)S(1)} %pad_maximum_fusion.1.refs_0_), channel_id=1, source_target_pairs={{0,4},{4,0},{8,12},{12,8},{16,20},{20,16},{24,28},{28,24},{1,5},{5... | collective-permute-start | bytes 835592 | tf_op jit(solution)/shard_map/ppermute | solution.py:581
  25.4 22.5 %collective-permute-start.9 = (bf16[2,272,256]{2,1,0:T(8,128)(2,1)S(1)}, bf16[2,272,256]{2,1,0:T(8,128)(2,1)S(1)}, u32[]{:S(2)}, u32[]{:S(2)}) collective-permute-start(bf16[2,272,256]{2,1,0:T(8,128)(2,1)S(1)} %pad_maximum_fusion.1.refs_0_), channel_id=1, source_target_pairs={{0,8},{4,12},{8,0},{12,4},{16,24},{20,28},{24,16},{28,20},{1,9},{5... | collective-permute-start | bytes 835592 | tf_op jit(solution)/shard_map/ppermute | solution.py:581
  26.3 30.5 %collective-permute-start.6 = (bf16[2,256,256]{2,1,0:T(8,128)(2,1)S(1)}, bf16[2,256,256]{2,1,0:T(8,128)(2,1)S(1)}, u32[]{:S(2)}, u32[]{:S(2)}) collective-permute-start(bf16[2,256,256]{2,1,0:T(8,128)(2,1)S(1)} %pad_maximum_fusion.9), channel_id=1, source_target_pairs={{0,28},{4,24},{8,20},{12,16},{16,12},{20,8},{24,4},{28,0},{1,29},{... | collective-permute-start | bytes 786440 | tf_op jit(solution)/shard_map/ppermute | solution.py:581
  33.7 23.1 %collective-permute-start.3 = (bf16[2,256,256]{2,1,0:T(8,128)(2,1)S(1)}, bf16[2,256,256]{2,1,0:T(8,128)(2,1)S(1)}, u32[]{:S(2)}, u32[]{:S(2)}) collective-permute-start(bf16[2,256,256]{2,1,0:T(8,128)(2,1)S(1)} %pad_maximum_fusion.6), channel_id=1, source_target_pairs={{0,16},{4,20},{8,24},{12,28},{16,0},{20,4},{24,8},{28,12},{1,17},{... | collective-permute-start | bytes 786440 | tf_op jit(solution)/shard_map/ppermute | solution.py:581
  33.7 23.6 %collective-permute-start.2 = (bf16[2,256,256]{2,1,0:T(8,128)(2,1)S(1)}, bf16[2,256,256]{2,1,0:T(8,128)(2,1)S(1)}, u32[]{:S(2)}, u32[]{:S(2)}) collective-permute-start(bf16[2,256,256]{2,1,0:T(8,128)(2,1)S(1)} %pad_maximum_fusion.5), channel_id=1, source_target_pairs={{0,12},{4,8},{8,4},{12,0},{16,28},{20,24},{24,20},{28,16},{1,13},{... | collective-permute-start | bytes 786440 | tf_op jit(solution)/shard_map/ppermute | solution.py:581
  40.0 21.4 %collective-permute-start.1 = (bf16[2,256,256]{2,1,0:T(8,128)(2,1)S(1)}, bf16[2,256,256]{2,1,0:T(8,128)(2,1)S(1)}, u32[]{:S(2)}, u32[]{:S(2)}) collective-permute-start(bf16[2,256,256]{2,1,0:T(8,128)(2,1)S(1)} %pad_maximum_fusion.4), channel_id=1, source_target_pairs={{0,8},{4,12},{8,0},{12,4},{16,24},{20,28},{24,16},{28,20},{1,9},{5... | collective-permute-start | bytes 786440 | tf_op jit(solution)/shard_map/ppermute | solution.py:581
  47.9 14.2 %collective-permute-start = (bf16[2,256,256]{2,1,0:T(8,128)(2,1)S(1)}, bf16[2,256,256]{2,1,0:T(8,128)(2,1)S(1)}, u32[]{:S(2)}, u32[]{:S(2)}) collective-permute-start(bf16[2,256,256]{2,1,0:T(8,128)(2,1)S(1)} %pad_maximum_fusion.3), channel_id=1, source_target_pairs={{0,4},{4,0},{8,12},{12,8},{16,20},{20,16},{24,28},{28,24},{1,5},{5... | collective-permute-start | bytes 786440 | tf_op jit(solution)/shard_map/ppermute | solution.py:581
  62.2 8.5 %copy-start.6 = (f32[2048]{0:T(1024)S(1)}, f32[2048]{0:T(1024)}, u32[]{:S(2)}) copy-start(f32[2048]{0:T(1024)} %param.28) | copy-start | bytes 24580
  67.1 7.2 %collective-permute-start.11 = (bf16[256,256]{1,0:T(8,128)(2,1)S(1)}, bf16[256,256]{1,0:T(8,128)(2,1)S(1)}, u32[]{:S(2)}, u32[]{:S(2)}) collective-permute-start(bf16[256,256]{1,0:T(8,128)(2,1)S(1)} %get-tuple-element.35), channel_id=1, source_target_pairs={{0,4},{4,0},{8,12},{12,8},{16,20},{20,16},{24,28},{28,24},{1,5},{5... | collective-permute-start | bytes 393224 | tf_op jit(solution)/shard_map/ppermute | solution.py:581
  67.9 8.3 %collective-permute-start.12 = (bf16[256,256]{1,0:T(8,128)(2,1)S(1)}, bf16[256,256]{1,0:T(8,128)(2,1)S(1)}, u32[]{:S(2)}, u32[]{:S(2)}) collective-permute-start(bf16[256,256]{1,0:T(8,128)(2,1)S(1)} %get-tuple-element.36), channel_id=1, source_target_pairs={{0,8},{4,12},{8,0},{12,4},{16,24},{20,28},{24,16},{28,20},{1,9},{5... | collective-permute-start | bytes 393224 | tf_op jit(solution)/shard_map/ppermute | solution.py:581
  70.4 7.3 %collective-permute-start.13 = (bf16[256,256]{1,0:T(8,128)(2,1)S(1)}, bf16[256,256]{1,0:T(8,128)(2,1)S(1)}, u32[]{:S(2)}, u32[]{:S(2)}) collective-permute-start(bf16[256,256]{1,0:T(8,128)(2,1)S(1)} %get-tuple-element.37), channel_id=1, source_target_pairs={{0,12},{4,8},{8,4},{12,0},{16,28},{20,24},{24,20},{28,16},{1,13},{... | collective-permute-start | bytes 393224 | tf_op jit(solution)/shard_map/ppermute | solution.py:581
  70.6 13.6 %collective-permute-start.14 = (bf16[256,256]{1,0:T(8,128)(2,1)S(1)}, bf16[256,256]{1,0:T(8,128)(2,1)S(1)}, u32[]{:S(2)}, u32[]{:S(2)}) collective-permute-start(bf16[256,256]{1,0:T(8,128)(2,1)S(1)} %get-tuple-element.40), channel_id=1, source_target_pairs={{0,16},{4,20},{8,24},{12,28},{16,0},{20,4},{24,8},{28,12},{1,17},{... | collective-permute-start | bytes 393224 | tf_op jit(solution)/shard_map/ppermute | solution.py:581
  71.3 17.8 %collective-permute-start.15 = (bf16[256,256]{1,0:T(8,128)(2,1)S(1)}, bf16[256,256]{1,0:T(8,128)(2,1)S(1)}, u32[]{:S(2)}, u32[]{:S(2)}) collective-permute-start(bf16[256,256]{1,0:T(8,128)(2,1)S(1)} %get-tuple-element.41), channel_id=1, source_target_pairs={{0,20},{4,16},{8,28},{12,24},{16,4},{20,0},{24,12},{28,8},{1,21},{... | collective-permute-start | bytes 393224 | tf_op jit(solution)/shard_map/ppermute | solution.py:581
  74.2 20.4 %collective-permute-start.16 = (bf16[256,256]{1,0:T(8,128)(2,1)S(1)}, bf16[256,256]{1,0:T(8,128)(2,1)S(1)}, u32[]{:S(2)}, u32[]{:S(2)}) collective-permute-start(bf16[256,256]{1,0:T(8,128)(2,1)S(1)} %get-tuple-element.42), channel_id=1, source_target_pairs={{0,24},{4,28},{8,16},{12,20},{16,8},{20,12},{24,0},{28,4},{1,25},{... | collective-permute-start | bytes 393224 | tf_op jit(solution)/shard_map/ppermute | solution.py:581
  76.2 20.7 %collective-permute-start.17 = (bf16[256,256]{1,0:T(8,128)(2,1)S(1)}, bf16[256,256]{1,0:T(8,128)(2,1)S(1)}, u32[]{:S(2)}, u32[]{:S(2)}) collective-permute-start(bf16[256,256]{1,0:T(8,128)(2,1)S(1)} %get-tuple-element.43), channel_id=1, source_target_pairs={{0,28},{4,24},{8,20},{12,16},{16,12},{20,8},{24,4},{28,0},{1,29},{... | collective-permute-start | bytes 393224 | tf_op jit(solution)/shard_map/ppermute | solution.py:581
  98.9 2.5 %collective-permute-start.18 = (bf16[128,2048]{1,0:T(8,128)(2,1)S(1)}, bf16[128,2048]{1,0:T(8,128)(2,1)S(1)}, u32[]{:S(2)}, u32[]{:S(2)}) collective-permute-start(bf16[128,2048]{1,0:T(8,128)(2,1)S(1)} %get-tuple-element.45), channel_id=1, source_target_pairs={{0,1},{1,0},{2,3},{3,2},{4,5},{5,4},{6,7},{7,6},{8,9},{9,8},{10,11... | collective-permute-start | bytes 1572872 | tf_op jit(solution)/shard_map/ppermute | solution.py:738
  100.8 2.3 %collective-permute-start.20 = (bf16[128,2048]{1,0:T(8,128)(2,1)S(1)}, bf16[128,2048]{1,0:T(8,128)(2,1)S(1)}, u32[]{:S(2)}, u32[]{:S(2)}) collective-permute-start(bf16[128,2048]{1,0:T(8,128)(2,1)S(1)} %get-tuple-element.48), channel_id=1, source_target_pairs={{0,1},{1,0},{2,3},{3,2},{4,5},{5,4},{6,7},{7,6},{8,9},{9,8},{10,11... | collective-permute-start | bytes 1572872 | tf_op jit(solution)/shard_map/ppermute | solution.py:738
  101.5 9.2 %collective-permute-start.19 = (bf16[64,2048]{1,0:T(8,128)(2,1)S(1)}, bf16[64,2048]{1,0:T(8,128)(2,1)S(1)}, u32[]{:S(2)}, u32[]{:S(2)}) collective-permute-start(bf16[64,2048]{1,0:T(8,128)(2,1)S(1)} %slice.17), channel_id=1, source_target_pairs={{0,2},{1,3},{2,0},{3,1},{4,6},{5,7},{6,4},{7,5},{8,10},{9,11},{10,... | collective-permute-start | bytes 786440 | tf_op jit(solution)/shard_map/ppermute | solution.py:738
  103.2 12.2 %collective-permute-start.21 = (bf16[64,2048]{1,0:T(8,128)(2,1)S(1)}, bf16[64,2048]{1,0:T(8,128)(2,1)S(1)}, u32[]{:S(2)}, u32[]{:S(2)}) collective-permute-start(bf16[64,2048]{1,0:T(8,128)(2,1)S(1)} %slice.19), channel_id=1, source_target_pairs={{0,2},{1,3},{2,0},{3,1},{4,6},{5,7},{6,4},{7,5},{8,10},{9,11},{10,... | collective-permute-start | bytes 786440 | tf_op jit(solution)/shard_map/ppermute | solution.py:738

commit v5 on v4

--- a/solution.py
+++ b/solution.py
@@ -474,7 +474,7 @@
             ]
         return carry
 
-    lax.fori_loop(0, mix_ref.shape[0], one_chunk, 0, unroll=2)
+    lax.fori_loop(0, mix_ref.shape[0], one_chunk, 0, unroll=4)
     for turn, out_ref in zip(turns, out_refs):
         out_ref[...] = laid[jnp.bitwise_xor(me, turn)]
 
@@ -594,7 +594,7 @@
 
     held = jnp.stack([for_group(my_group), turned(for_group(my_group ^ 1), near)])
     group_rows = [held] + [turned(held, turn) for turn in range(1, near)]
-    turns = (0, 1, 2, 3, 4, 5, 6, 7)
+    turns = (0, 3, 4, 7, 1, 2, 5, 6)
     head_rows = [turned(for_heads(turn), turn) if turn else for_heads(turn) for turn in turns]
 
     key_taps = lax.dynamic_slice_in_dim(conv_keys, my_group * STATE, STATE, 1)

time: 117 us -> 110 us (0.940)
  starting transfers between devices: 46.2 us -> 27.6 us
  waiting for transfers between devices: 40.6 us -> 51.6 us
    ppermute x18, starting transfers between devices: 42.6 us -> 24.1 us  [turned(): return lax.ppermute(value, 'ctx', [(i, i ^ turn) for i in range(ctx_count)])]
    ppermute x18, waiting for transfers between devices: 29.8 us -> 40.9 us  [turned(): return lax.ppermute(value, 'ctx', [(i, i ^ turn) for i in range(ctx_count)])]
  transfers between devices with their start and end apart: 22 -> 22, of which waited for: 13 -> 13; matrix products, arithmetic and copies ran while one was open for 3% -> 3% of each run, Pallas kernels for 14% -> 15%
where the time goes in v5:
time: 110 us; the launch traced here: 108 us
  waiting for transfers between devices  51.6 us (47%)
  starting transfers between devices  27.6 us (25%)
  Pallas kernels  22.8 us (21%)
  local copies, waits for them, and re-layouts  3.57 us (3%)
  other arithmetic  2.26 us (2%)
    ppermute x18, waiting for transfers between devices, turned(): return lax.ppermute(value, 'ctx', [(i, i ^ turn) for i in range(ctx_count)])  40.9 us
    ppermute x18, starting transfers between devices, turned(): return lax.ppermute(value, 'ctx', [(i, i ^ turn) for i in range(ctx_count)])  24.1 us
    ppermute x4, waiting for transfers between devices, joined(): came = lax.ppermute(sent, 'tp', [(i, i ^ turn) for i in range(tp_count)])  10.8 us
    pallas_call x3, Pallas kernels, project(): pl.pallas_call(kernel, in_specs=[smem, vmem, pl.BlockSpec(memory_space=we...  10.3 us
    pallas_call x1, Pallas kernels, head_split(): pl.pallas_call(functools.partial(mixing_kernel, heads, group_heads, per_d...  8.14 us
    pallas_call x1, Pallas kernels, head_split(): pl.pallas_call(functools.partial(scan_kernel, heads, per_dev, turns), in_...  4.38 us
    ppermute x4, starting transfers between devices, joined(): came = lax.ppermute(sent, 'tp', [(i, i ^ turn) for i in range(tp_count)])  3.57 us
  transfers between devices with their start and end apart: 22, of which 13 were waited for; matrix products, arithmetic and copies ran while one was open for 3% of the time, Pallas kernels for 15%

profile of v5, /device:TPU:16, one launch (start us, length us, event | category | flops | bytes accessed | tf_op | source)
XLA Modules:
  0.0 108.3 jit_solution(15631885980053180414)
XLA Ops:
  0.0 0.7 dynamic-slice_bitcast_fusion.17
  0.7 1.0 constant_dynamic-slice_fusion.2
  1.7 0.1 collective-permute-start.7
  1.9 1.8 %dynamic-slice_bitcast_fusion = (bf16[1,256,256]{2,1,0:T(8,128)(2,1)S(1)}, bf16[1,256,256]{2,1,0:T(8,128)(2,1)S(1)}, bf16[1,256,256]{2,1,0:T(8,128)(2,1)S(1)}, b...) fusion(bf16[256,2048]{1,0:T(8,128)(2,1)} %param.16, ...), kind=kLoop, calls=%fused_computation.16 | loop fusion | bytes 4194336 | tf_op jit(solution)/shard_map/stack | solution.py:591
  3.7 0.7 pad_maximum_fusion.7
  4.4 1.8 %collective-permute-start.4 = (bf16[2,256,256]{2,1,0:T(8,128)(2,1)}, bf16[2,256,256]{2,1,0:T(8,128)(2,1)S(1)}, u32[]{:S(2)}, u32[]{:S(2)}) collective-permute-start(bf16[2,256,256]{2,1,0:T(8,128)(2,1)} %pad_maximum_fusion.7), channel_id=1, source_target_pairs={{0,8},{4,12},{8,0},{12,4},{16,24},{20,28},{24,16},{28,20},{1,9},{5... | collective-permute-start | bytes 786440 | tf_op jit(solution)/shard_map/ppermute | solution.py:581
  6.3 3.6 %collective-permute-start.5 = (bf16[2,256,256]{2,1,0:T(8,128)(2,1)S(1)}, bf16[2,256,256]{2,1,0:T(8,128)(2,1)S(1)}, u32[]{:S(2)}, u32[]{:S(2)}) collective-permute-start(bf16[2,256,256]{2,1,0:T(8,128)(2,1)S(1)} %pad_maximum_fusion.8), channel_id=1, source_target_pairs={{0,20},{4,16},{8,28},{12,24},{16,4},{20,0},{24,12},{28,8},{1,21},{... | collective-permute-start | bytes 786440 | tf_op jit(solution)/shard_map/ppermute | solution.py:581
  10.1 3.7 %collective-permute-start.10 = (bf16[2,272,256]{2,1,0:T(8,128)(2,1)S(1)}, bf16[2,272,256]{2,1,0:T(8,128)(2,1)S(1)}, u32[]{:S(2)}, u32[]{:S(2)}) collective-permute-start(bf16[2,272,256]{2,1,0:T(8,128)(2,1)S(1)} %pad_maximum_fusion.1.refs_0_), channel_id=1, source_target_pairs={{0,12},{4,8},{8,4},{12,0},{16,28},{20,24},{24,20},{28,16},{1,13},{... | collective-permute-start | bytes 835592 | tf_op jit(solution)/shard_map/ppermute | solution.py:581
  13.8 0.5 collective-permute-start.8
  14.3 0.1 collective-permute-start.9
  14.5 6.4 %collective-permute-done.4.refs_5_ = bf16[2,256,256]{2,1,0:T(8,128)(2,1)S(1)} collective-permute-done((bf16[2,256,256]{2,1,0:T(8,128)(2,1)}, bf16[2,256,256]{2,1,0:T(8,128)(2,1)S(1)}, u32[]{:S(2)}, u32[]{:S(2)}) %collective-permute-start.4) | collective-permute-done | bytes 262176 | tf_op jit(solution)/shard_map/ppermute | solution.py:581
  20.9 3.3 %collective-permute-done.5.refs_6_ = bf16[2,256,256]{2,1,0:T(8,128)(2,1)S(1)} collective-permute-done((bf16[2,256,256]{2,1,0:T(8,128)(2,1)S(1)}, bf16[2,256,256]{2,1,0:T(8,128)(2,1)S(1)}, u32[]{:S(2)}, u32[]{:S(2)}) %collective-permute-start.5) | collective-permute-done | bytes 262176 | tf_op jit(solution)/shard_map/ppermute | solution.py:581
  24.2 0.4 collective-permute-start.3
  24.6 4.3 %collective-permute-done.10.refs_3_ = bf16[2,272,256]{2,1,0:T(8,128)(2,1)S(1)} collective-permute-done((bf16[2,272,256]{2,1,0:T(8,128)(2,1)S(1)}, bf16[2,272,256]{2,1,0:T(8,128)(2,1)S(1)}, u32[]{:S(2)}, u32[]{:S(2)}) %collective-permute-start.10) | collective-permute-done | bytes 278560 | tf_op jit(solution)/shard_map/ppermute | solution.py:581
  28.9 0.5 collective-permute-start.2
  29.4 7.4 %collective-permute-done.8.refs_1_ = bf16[2,272,256]{2,1,0:T(8,128)(2,1)S(1)} collective-permute-done((bf16[2,272,256]{2,1,0:T(8,128)(2,1)S(1)}, bf16[2,272,256]{2,1,0:T(8,128)(2,1)S(1)}, u32[]{:S(2)}, u32[]{:S(2)}) %collective-permute-start.8) | collective-permute-done | bytes 278560 | tf_op jit(solution)/shard_map/ppermute | solution.py:581
  36.8 7.4 %collective-permute-done.9.refs_2_ = bf16[2,272,256]{2,1,0:T(8,128)(2,1)S(1)} collective-permute-done((bf16[2,272,256]{2,1,0:T(8,128)(2,1)S(1)}, bf16[2,272,256]{2,1,0:T(8,128)(2,1)S(1)}, u32[]{:S(2)}, u32[]{:S(2)}) %collective-permute-start.9) | collective-permute-done | bytes 278560 | tf_op jit(solution)/shard_map/ppermute | solution.py:581
  44.2 3.9 %collective-permute-start = (bf16[2,256,256]{2,1,0:T(8,128)(2,1)S(1)}, bf16[2,256,256]{2,1,0:T(8,128)(2,1)S(1)}, u32[]{:S(2)}, u32[]{:S(2)}) collective-permute-start(bf16[2,256,256]{2,1,0:T(8,128)(2,1)S(1)} %pad_maximum_fusion.3), channel_id=1, source_target_pairs={{0,12},{4,8},{8,4},{12,0},{16,28},{20,24},{24,20},{28,16},{1,13},{... | collective-permute-start | bytes 786440 | tf_op jit(solution)/shard_map/ppermute | solution.py:581
  48.2 0.1 pad_add_fusion.me_ref.place_ref
  48.3 8.1 %mixing.1 = (bf16[16,128,512]{2,1,0:T(8,128)(2,1)S(1)}, bf16[16,128,128]{2,1,0:T(8,128)(2,1)S(1)}, bf16[16,128,128]{2,1,0:T(8,128)(2,1)S(1)}, f32[16,128,256]{2,...) custom-call(s32[2]{0:T(128)S(1)} %pad_add_fusion.me_ref.place_ref, ...), custom_call_target="tpu_custom_call" | custom-call | flops 20000000 | bytes 20000000 | tf_op jit(solution)/shard_map/mixing/pallas_call | solution.py:626
  56.5 1.1 collective-permute-done.refs_1_
  57.6 4.4 %scan.1 = (bf16[256,256]{1,0:T(8,128)(2,1)S(1)}, bf16[256,256]{1,0:T(8,128)(2,1)S(1)}, bf16[256,256]{1,0:T(8,128)(2,1)S(1)}, bf16[256,256]{1,0:T(8,128)(2,1)S(1)...) custom-call(s32[2]{0:T(128)S(1)} %pad_add_fusion.me_ref.place_ref, ...), custom_call_target="tpu_custom_call" | custom-call | flops 600000000 | bytes 14000000 | tf_op jit(solution)/shard_map/scan/pallas_call | solution.py:646
  62.0 0.7 collective-permute-start.11
  62.7 2.6 %collective-permute-start.12 = (bf16[256,256]{1,0:T(8,128)(2,1)S(1)}, bf16[256,256]{1,0:T(8,128)(2,1)S(1)}, u32[]{:S(2)}, u32[]{:S(2)}) collective-permute-start(bf16[256,256]{1,0:T(8,128)(2,1)S(1)} %get-tuple-element.36), channel_id=1, source_target_pairs={{0,8},{4,12},{8,0},{12,4},{16,24},{20,28},{24,16},{28,20},{1,9},{5... | collective-permute-start | bytes 393224 | tf_op jit(solution)/shard_map/ppermute | solution.py:581
  65.3 0.2 collective-permute-start.13
  65.5 1.7 %collective-permute-start.14 = (bf16[256,256]{1,0:T(8,128)(2,1)S(1)}, bf16[256,256]{1,0:T(8,128)(2,1)S(1)}, u32[]{:S(2)}, u32[]{:S(2)}) collective-permute-start(bf16[256,256]{1,0:T(8,128)(2,1)S(1)} %get-tuple-element.40), channel_id=1, source_target_pairs={{0,16},{4,20},{8,24},{12,28},{16,0},{20,4},{24,8},{28,12},{1,17},{... | collective-permute-start | bytes 393224 | tf_op jit(solution)/shard_map/ppermute | solution.py:581
  67.3 1.9 %collective-permute-start.15 = (bf16[256,256]{1,0:T(8,128)(2,1)S(1)}, bf16[256,256]{1,0:T(8,128)(2,1)S(1)}, u32[]{:S(2)}, u32[]{:S(2)}) collective-permute-start(bf16[256,256]{1,0:T(8,128)(2,1)S(1)} %get-tuple-element.41), channel_id=1, source_target_pairs={{0,20},{4,16},{8,28},{12,24},{16,4},{20,0},{24,12},{28,8},{1,21},{... | collective-permute-start | bytes 393224 | tf_op jit(solution)/shard_map/ppermute | solution.py:581
  69.1 0.6 collective-permute-start.16
  69.8 1.6 %collective-permute-start.17 = (bf16[256,256]{1,0:T(8,128)(2,1)S(1)}, bf16[256,256]{1,0:T(8,128)(2,1)S(1)}, u32[]{:S(2)}, u32[]{:S(2)}) collective-permute-start(bf16[256,256]{1,0:T(8,128)(2,1)S(1)} %get-tuple-element.43), channel_id=1, source_target_pairs={{0,28},{4,24},{8,20},{12,16},{16,12},{20,8},{24,4},{28,0},{1,29},{... | collective-permute-start | bytes 393224 | tf_op jit(solution)/shard_map/ppermute | solution.py:581
  71.4 1.4 %collective-permute-done.13.refs_3_ = bf16[256,256]{1,0:T(8,128)(2,1)S(1)} collective-permute-done((bf16[256,256]{1,0:T(8,128)(2,1)S(1)}, bf16[256,256]{1,0:T(8,128)(2,1)S(1)}, u32[]{:S(2)}, u32[]{:S(2)}) %collective-permute-start.13) | collective-permute-done | bytes 131104 | tf_op jit(solution)/shard_map/ppermute | solution.py:581
  72.7 6.5 %near_projection.1 = (f32[256,4096]{1,0:T(8,128)S(1)}, bf16[1024,4096]{1,0:T(8,128)(2,1)S(1)}) custom-call(s32[2]{0:T(128)S(1)} %pad_add_fusion.me_ref.place_ref, f32[8,256]{1,0:T(8,128)S(1)} %reshape.6.gain_ref, bf16[2,1024,4096]{2,1,0:T(8,128)(2,1)} %bitcast.42, bf16[256,256]{1,0:T(8,128)(2,1)S(1)} %get-tuple-element.34.refs_0_, ...), custom_call_target="tpu_custom_call" | custom-call | flops 2147483648 | bytes 8388608 | tf_op jit(solution)/shard_map/near_projection/pallas_call | solution.py:674
  79.3 1.6 %collective-permute-done.14.refs_0_ = bf16[256,256]{1,0:T(8,128)(2,1)S(1)} collective-permute-done((bf16[256,256]{1,0:T(8,128)(2,1)S(1)}, bf16[256,256]{1,0:T(8,128)(2,1)S(1)}, u32[]{:S(2)}, u32[]{:S(2)}) %collective-permute-start.14) | collective-permute-done | bytes 131104 | tf_op jit(solution)/shard_map/ppermute | solution.py:581
  80.9 2.8 %collective-permute-done.15.refs_1_ = bf16[256,256]{1,0:T(8,128)(2,1)S(1)} collective-permute-done((bf16[256,256]{1,0:T(8,128)(2,1)S(1)}, bf16[256,256]{1,0:T(8,128)(2,1)S(1)}, u32[]{:S(2)}, u32[]{:S(2)}) %collective-permute-start.15) | collective-permute-done | bytes 131104 | tf_op jit(solution)/shard_map/ppermute | solution.py:581
  83.7 3.5 %collective-permute-done.16.refs_2_ = bf16[256,256]{1,0:T(8,128)(2,1)S(1)} collective-permute-done((bf16[256,256]{1,0:T(8,128)(2,1)S(1)}, bf16[256,256]{1,0:T(8,128)(2,1)S(1)}, u32[]{:S(2)}, u32[]{:S(2)}) %collective-permute-start.16) | collective-permute-done | bytes 131104 | tf_op jit(solution)/shard_map/ppermute | solution.py:581
  87.3 1.6 %collective-permute-done.17.refs_3_ = bf16[256,256]{1,0:T(8,128)(2,1)S(1)} collective-permute-done((bf16[256,256]{1,0:T(8,128)(2,1)S(1)}, bf16[256,256]{1,0:T(8,128)(2,1)S(1)}, u32[]{:S(2)}, u32[]{:S(2)}) %collective-permute-start.17) | collective-permute-done | bytes 131104 | tf_op jit(solution)/shard_map/ppermute | solution.py:581
  88.9 2.0 %far_projection.1 = (bf16[128,2048]{1,0:T(8,128)(2,1)S(1)}, bf16[128,2048]{1,0:T(8,128)(2,1)S(1)}, bf16[256,1024]{1,0:T(8,128)(2,1)S(1)}) custom-call(s32[2]{0:T(128)S(1)} %pad_add_fusion.me_ref.place_ref, f32[8,256]{1,0:T(8,128)S(1)} %reshape.6.gain_ref, bf16[1024,4096]{1,0:T(8,128)(2,1)S(1)} %get-tuple-element.38.weight_ref, ...), custom_call_target="tpu_custom_call" | custom-call | flops 2147483648 | bytes 8388608 | tf_op jit(solution)/shard_map/far_projection/pallas_call | solution.py:674
  90.9 0.1 collective-permute-start.18
  90.9 1.8 %rest_projection.1 = (bf16[128,2048]{1,0:T(8,128)(2,1)S(1)}, bf16[128,2048]{1,0:T(8,128)(2,1)S(1)}) custom-call(s32[2]{0:T(128)S(1)} %pad_add_fusion.me_ref.place_ref, bf16[256,1024]{1,0:T(8,128)(2,1)S(1)} %get-tuple-element.46.normed_ref, bf16[1024,4096]{1,0:T(8,128)(2,1)S(1)} %get-tuple-element.38.weight_ref, f32[256,4096]{1,0:T(8,128)S(1)} %get-tuple-element.39.near_ref), custom_call_target="tpu_custom_call" | custom-call | flops 2147483648 | bytes 8388608 | tf_op jit(solution)/shard_map/rest_projection/pallas_call | solution.py:674
  92.8 0.6 collective-permute-start.20
  93.3 0.1 add_convert_fusion.1
  93.5 1.6 %collective-permute-start.19 = (bf16[64,2048]{1,0:T(8,128)(2,1)S(1)}, bf16[64,2048]{1,0:T(8,128)(2,1)S(1)}, u32[]{:S(2)}, u32[]{:S(2)}) collective-permute-start(bf16[64,2048]{1,0:T(8,128)(2,1)S(1)} %slice.17), channel_id=1, source_target_pairs={{0,2},{1,3},{2,0},{3,1},{4,6},{5,7},{6,4},{7,5},{8,10},{9,11},{10,... | collective-permute-start | bytes 786440 | tf_op jit(solution)/shard_map/ppermute | solution.py:738
  95.0 0.1 add_convert_fusion
  95.2 1.4 %collective-permute-start.21 = (bf16[64,2048]{1,0:T(8,128)(2,1)S(1)}, bf16[64,2048]{1,0:T(8,128)(2,1)S(1)}, u32[]{:S(2)}, u32[]{:S(2)}) collective-permute-start(bf16[64,2048]{1,0:T(8,128)(2,1)S(1)} %slice.19), channel_id=1, source_target_pairs={{0,2},{1,3},{2,0},{3,1},{4,6},{5,7},{6,4},{7,5},{8,10},{9,11},{10,... | collective-permute-start | bytes 786440 | tf_op jit(solution)/shard_map/ppermute | solution.py:738
  96.6 6.1 %collective-permute-done.19 = bf16[64,2048]{1,0:T(8,128)(2,1)S(1)} collective-permute-done((bf16[64,2048]{1,0:T(8,128)(2,1)S(1)}, bf16[64,2048]{1,0:T(8,128)(2,1)S(1)}, u32[]{:S(2)}, u32[]{:S(2)}) %collective-permute-start.19) | collective-permute-done | bytes 262176 | tf_op jit(solution)/shard_map/ppermute | solution.py:738
  102.7 0.1 add_convert_fusion.3
  102.8 4.6 %collective-permute-done.21 = bf16[64,2048]{1,0:T(8,128)(2,1)S(1)} collective-permute-done((bf16[64,2048]{1,0:T(8,128)(2,1)S(1)}, bf16[64,2048]{1,0:T(8,128)(2,1)S(1)}, u32[]{:S(2)}, u32[]{:S(2)}) %collective-permute-start.21) | collective-permute-done | bytes 262176 | tf_op jit(solution)/shard_map/ppermute | solution.py:738
  107.4 0.1 add_convert_fusion.2
  107.5 0.8 pad_maximum_fusion
  (44 shorter events, 0.4 us)
Async XLA Ops:
  0.0 14.4 %copy-start = (f32[4,2048]{1,0:T(4,128)S(1)}, f32[4,2048]{1,0:T(4,128)}, u32[]{:S(2)}) copy-start(f32[4,2048]{1,0:T(4,128)} %param.22) | copy-start | bytes 98308
  1.7 8.3 %collective-permute-start.7 = (bf16[272,256]{1,0:T(8,128)(2,1)S(1)}, bf16[272,256]{1,0:T(8,128)(2,1)S(1)}, u32[]{:S(2)}, u32[]{:S(2)}) collective-permute-start(bf16[272,256]{1,0:T(8,128)(2,1)S(1)} %pad_maximum_fusion.10), channel_id=1, source_target_pairs={{0,16},{4,20},{8,24},{12,28},{16,0},{20,4},{24,8},{28,12},{1,17},{... | collective-permute-start | bytes 417800 | tf_op jit(solution)/shard_map/ppermute | solution.py:581
  1.8 46.4 %copy-start.7 = (f32[4,256]{1,0:T(4,128)S(1)}, f32[4,256]{1,0:T(4,128)}, u32[]{:S(2)}) copy-start(f32[4,256]{1,0:T(4,128)} %param.24) | copy-start | bytes 12292
  1.8 46.4 %copy-start.8 = (f32[4,256]{1,0:T(4,128)S(1)}, f32[4,256]{1,0:T(4,128)}, u32[]{:S(2)}) copy-start(f32[4,256]{1,0:T(4,128)} %param.23) | copy-start | bytes 12292
  1.9 46.4 %copy-start.1 = (s32[32]{0:T(128)S(1)}, s32[32]{0:T(128)}, u32[]{:S(2)}) copy-start(s32[32]{0:T(128)} %order_ref.3) | copy-start | bytes 388
  1.9 46.4 %copy-start.3 = (s32[16]{0:T(128)S(1)}, s32[16]{0:T(128)}, u32[]{:S(2)}) copy-start(s32[16]{0:T(128)} %lengths_ref.1) | copy-start | bytes 196
  1.9 46.4 %copy-start.4 = (f32[32]{0:T(128)S(1)}, f32[32]{0:T(128)}, u32[]{:S(2)}) copy-start(f32[32]{0:T(128)} %bias_ref.1) | copy-start | bytes 388
  1.9 46.4 %copy-start.5 = (f32[32]{0:T(128)S(1)}, f32[32]{0:T(128)}, u32[]{:S(2)}) copy-start(f32[32]{0:T(128)} %log_ref.1) | copy-start | bytes 388
  4.4 53.1 %copy-start.2 = (f32[32]{0:T(128)S(1)}, f32[32]{0:T(128)}, u32[]{:S(2)}) copy-start(f32[32]{0:T(128)} %skip_ref.1) | copy-start | bytes 388
  4.4 16.5 %collective-permute-start.4 = (bf16[2,256,256]{2,1,0:T(8,128)(2,1)}, bf16[2,256,256]{2,1,0:T(8,128)(2,1)S(1)}, u32[]{:S(2)}, u32[]{:S(2)}) collective-permute-start(bf16[2,256,256]{2,1,0:T(8,128)(2,1)} %pad_maximum_fusion.7), channel_id=1, source_target_pairs={{0,8},{4,12},{8,0},{12,4},{16,24},{20,28},{24,16},{28,20},{1,9},{5... | collective-permute-start | bytes 786440 | tf_op jit(solution)/shard_map/ppermute | solution.py:581
  6.3 17.9 %collective-permute-start.5 = (bf16[2,256,256]{2,1,0:T(8,128)(2,1)S(1)}, bf16[2,256,256]{2,1,0:T(8,128)(2,1)S(1)}, u32[]{:S(2)}, u32[]{:S(2)}) collective-permute-start(bf16[2,256,256]{2,1,0:T(8,128)(2,1)S(1)} %pad_maximum_fusion.8), channel_id=1, source_target_pairs={{0,20},{4,16},{8,28},{12,24},{16,4},{20,0},{24,12},{28,8},{1,21},{... | collective-permute-start | bytes 786440 | tf_op jit(solution)/shard_map/ppermute | solution.py:581
  10.1 18.8 %collective-permute-start.10 = (bf16[2,272,256]{2,1,0:T(8,128)(2,1)S(1)}, bf16[2,272,256]{2,1,0:T(8,128)(2,1)S(1)}, u32[]{:S(2)}, u32[]{:S(2)}) collective-permute-start(bf16[2,272,256]{2,1,0:T(8,128)(2,1)S(1)} %pad_maximum_fusion.1.refs_0_), channel_id=1, source_target_pairs={{0,12},{4,8},{8,4},{12,0},{16,28},{20,24},{24,20},{28,16},{1,13},{... | collective-permute-start | bytes 835592 | tf_op jit(solution)/shard_map/ppermute | solution.py:581
  13.8 23.0 %collective-permute-start.8 = (bf16[2,272,256]{2,1,0:T(8,128)(2,1)S(1)}, bf16[2,272,256]{2,1,0:T(8,128)(2,1)S(1)}, u32[]{:S(2)}, u32[]{:S(2)}) collective-permute-start(bf16[2,272,256]{2,1,0:T(8,128)(2,1)S(1)} %pad_maximum_fusion.1.refs_0_), channel_id=1, source_target_pairs={{0,4},{4,0},{8,12},{12,8},{16,20},{20,16},{24,28},{28,24},{1,5},{5... | collective-permute-start | bytes 835592 | tf_op jit(solution)/shard_map/ppermute | solution.py:581
  14.3 29.9 %collective-permute-start.9 = (bf16[2,272,256]{2,1,0:T(8,128)(2,1)S(1)}, bf16[2,272,256]{2,1,0:T(8,128)(2,1)S(1)}, u32[]{:S(2)}, u32[]{:S(2)}) collective-permute-start(bf16[2,272,256]{2,1,0:T(8,128)(2,1)S(1)} %pad_maximum_fusion.1.refs_0_), channel_id=1, source_target_pairs={{0,8},{4,12},{8,0},{12,4},{16,24},{20,28},{24,16},{28,20},{1,9},{5... | collective-permute-start | bytes 835592 | tf_op jit(solution)/shard_map/ppermute | solution.py:581
  20.9 35.5 %collective-permute-start.6 = (bf16[2,256,256]{2,1,0:T(8,128)(2,1)S(1)}, bf16[2,256,256]{2,1,0:T(8,128)(2,1)S(1)}, u32[]{:S(2)}, u32[]{:S(2)}) collective-permute-start(bf16[2,256,256]{2,1,0:T(8,128)(2,1)S(1)} %pad_maximum_fusion.9), channel_id=1, source_target_pairs={{0,24},{4,28},{8,16},{12,20},{16,8},{20,12},{24,0},{28,4},{1,25},{... | collective-permute-start | bytes 786440 | tf_op jit(solution)/shard_map/ppermute | solution.py:581
  24.2 32.2 %collective-permute-start.3 = (bf16[2,256,256]{2,1,0:T(8,128)(2,1)S(1)}, bf16[2,256,256]{2,1,0:T(8,128)(2,1)S(1)}, u32[]{:S(2)}, u32[]{:S(2)}) collective-permute-start(bf16[2,256,256]{2,1,0:T(8,128)(2,1)S(1)} %pad_maximum_fusion.6), channel_id=1, source_target_pairs={{0,4},{4,0},{8,12},{12,8},{16,20},{20,16},{24,28},{28,24},{1,5},{5... | collective-permute-start | bytes 786440 | tf_op jit(solution)/shard_map/ppermute | solution.py:581
  28.9 27.6 %collective-permute-start.2 = (bf16[2,256,256]{2,1,0:T(8,128)(2,1)S(1)}, bf16[2,256,256]{2,1,0:T(8,128)(2,1)S(1)}, u32[]{:S(2)}, u32[]{:S(2)}) collective-permute-start(bf16[2,256,256]{2,1,0:T(8,128)(2,1)S(1)} %pad_maximum_fusion.5), channel_id=1, source_target_pairs={{0,28},{4,24},{8,20},{12,16},{16,12},{20,8},{24,4},{28,0},{1,29},{... | collective-permute-start | bytes 786440 | tf_op jit(solution)/shard_map/ppermute | solution.py:581
  36.8 19.7 %collective-permute-start.1 = (bf16[2,256,256]{2,1,0:T(8,128)(2,1)S(1)}, bf16[2,256,256]{2,1,0:T(8,128)(2,1)S(1)}, u32[]{:S(2)}, u32[]{:S(2)}) collective-permute-start(bf16[2,256,256]{2,1,0:T(8,128)(2,1)S(1)} %pad_maximum_fusion.4), channel_id=1, source_target_pairs={{0,16},{4,20},{8,24},{12,28},{16,0},{20,4},{24,8},{28,12},{1,17},{... | collective-permute-start | bytes 786440 | tf_op jit(solution)/shard_map/ppermute | solution.py:581
  44.2 13.4 %collective-permute-start = (bf16[2,256,256]{2,1,0:T(8,128)(2,1)S(1)}, bf16[2,256,256]{2,1,0:T(8,128)(2,1)S(1)}, u32[]{:S(2)}, u32[]{:S(2)}) collective-permute-start(bf16[2,256,256]{2,1,0:T(8,128)(2,1)S(1)} %pad_maximum_fusion.3), channel_id=1, source_target_pairs={{0,12},{4,8},{8,4},{12,0},{16,28},{20,24},{24,20},{28,16},{1,13},{... | collective-permute-start | bytes 786440 | tf_op jit(solution)/shard_map/ppermute | solution.py:581
  57.6 7.9 %copy-start.6 = (f32[2048]{0:T(1024)S(1)}, f32[2048]{0:T(1024)}, u32[]{:S(2)}) copy-start(f32[2048]{0:T(1024)} %param.28) | copy-start | bytes 24580
  62.0 7.2 %collective-permute-start.11 = (bf16[256,256]{1,0:T(8,128)(2,1)S(1)}, bf16[256,256]{1,0:T(8,128)(2,1)S(1)}, u32[]{:S(2)}, u32[]{:S(2)}) collective-permute-start(bf16[256,256]{1,0:T(8,128)(2,1)S(1)} %get-tuple-element.35), channel_id=1, source_target_pairs={{0,4},{4,0},{8,12},{12,8},{16,20},{20,16},{24,28},{28,24},{1,5},{5... | collective-permute-start | bytes 393224 | tf_op jit(solution)/shard_map/ppermute | solution.py:581
  62.7 7.1 %collective-permute-start.12 = (bf16[256,256]{1,0:T(8,128)(2,1)S(1)}, bf16[256,256]{1,0:T(8,128)(2,1)S(1)}, u32[]{:S(2)}, u32[]{:S(2)}) collective-permute-start(bf16[256,256]{1,0:T(8,128)(2,1)S(1)} %get-tuple-element.36), channel_id=1, source_target_pairs={{0,8},{4,12},{8,0},{12,4},{16,24},{20,28},{24,16},{28,20},{1,9},{5... | collective-permute-start | bytes 393224 | tf_op jit(solution)/shard_map/ppermute | solution.py:581
  65.3 7.4 %collective-permute-start.13 = (bf16[256,256]{1,0:T(8,128)(2,1)S(1)}, bf16[256,256]{1,0:T(8,128)(2,1)S(1)}, u32[]{:S(2)}, u32[]{:S(2)}) collective-permute-start(bf16[256,256]{1,0:T(8,128)(2,1)S(1)} %get-tuple-element.37), channel_id=1, source_target_pairs={{0,12},{4,8},{8,4},{12,0},{16,28},{20,24},{24,20},{28,16},{1,13},{... | collective-permute-start | bytes 393224 | tf_op jit(solution)/shard_map/ppermute | solution.py:581
  65.5 15.4 %collective-permute-start.14 = (bf16[256,256]{1,0:T(8,128)(2,1)S(1)}, bf16[256,256]{1,0:T(8,128)(2,1)S(1)}, u32[]{:S(2)}, u32[]{:S(2)}) collective-permute-start(bf16[256,256]{1,0:T(8,128)(2,1)S(1)} %get-tuple-element.40), channel_id=1, source_target_pairs={{0,16},{4,20},{8,24},{12,28},{16,0},{20,4},{24,8},{28,12},{1,17},{... | collective-permute-start | bytes 393224 | tf_op jit(solution)/shard_map/ppermute | solution.py:581
  67.3 16.4 %collective-permute-start.15 = (bf16[256,256]{1,0:T(8,128)(2,1)S(1)}, bf16[256,256]{1,0:T(8,128)(2,1)S(1)}, u32[]{:S(2)}, u32[]{:S(2)}) collective-permute-start(bf16[256,256]{1,0:T(8,128)(2,1)S(1)} %get-tuple-element.41), channel_id=1, source_target_pairs={{0,20},{4,16},{8,28},{12,24},{16,4},{20,0},{24,12},{28,8},{1,21},{... | collective-permute-start | bytes 393224 | tf_op jit(solution)/shard_map/ppermute | solution.py:581
  69.1 18.1 %collective-permute-start.16 = (bf16[256,256]{1,0:T(8,128)(2,1)S(1)}, bf16[256,256]{1,0:T(8,128)(2,1)S(1)}, u32[]{:S(2)}, u32[]{:S(2)}) collective-permute-start(bf16[256,256]{1,0:T(8,128)(2,1)S(1)} %get-tuple-element.42), channel_id=1, source_target_pairs={{0,24},{4,28},{8,16},{12,20},{16,8},{20,12},{24,0},{28,4},{1,25},{... | collective-permute-start | bytes 393224 | tf_op jit(solution)/shard_map/ppermute | solution.py:581
  69.8 19.1 %collective-permute-start.17 = (bf16[256,256]{1,0:T(8,128)(2,1)S(1)}, bf16[256,256]{1,0:T(8,128)(2,1)S(1)}, u32[]{:S(2)}, u32[]{:S(2)}) collective-permute-start(bf16[256,256]{1,0:T(8,128)(2,1)S(1)} %get-tuple-element.43), channel_id=1, source_target_pairs={{0,28},{4,24},{8,20},{12,16},{16,12},{20,8},{24,4},{28,0},{1,29},{... | collective-permute-start | bytes 393224 | tf_op jit(solution)/shard_map/ppermute | solution.py:581
  90.9 2.5 %collective-permute-start.18 = (bf16[128,2048]{1,0:T(8,128)(2,1)S(1)}, bf16[128,2048]{1,0:T(8,128)(2,1)S(1)}, u32[]{:S(2)}, u32[]{:S(2)}) collective-permute-start(bf16[128,2048]{1,0:T(8,128)(2,1)S(1)} %get-tuple-element.45), channel_id=1, source_target_pairs={{0,1},{1,0},{2,3},{3,2},{4,5},{5,4},{6,7},{7,6},{8,9},{9,8},{10,11... | collective-permute-start | bytes 1572872 | tf_op jit(solution)/shard_map/ppermute | solution.py:738
  92.8 2.3 %collective-permute-start.20 = (bf16[128,2048]{1,0:T(8,128)(2,1)S(1)}, bf16[128,2048]{1,0:T(8,128)(2,1)S(1)}, u32[]{:S(2)}, u32[]{:S(2)}) collective-permute-start(bf16[128,2048]{1,0:T(8,128)(2,1)S(1)} %get-tuple-element.48), channel_id=1, source_target_pairs={{0,1},{1,0},{2,3},{3,2},{4,5},{5,4},{6,7},{7,6},{8,9},{9,8},{10,11... | collective-permute-start | bytes 1572872 | tf_op jit(solution)/shard_map/ppermute | solution.py:738
  93.5 9.2 %collective-permute-start.19 = (bf16[64,2048]{1,0:T(8,128)(2,1)S(1)}, bf16[64,2048]{1,0:T(8,128)(2,1)S(1)}, u32[]{:S(2)}, u32[]{:S(2)}) collective-permute-start(bf16[64,2048]{1,0:T(8,128)(2,1)S(1)} %slice.17), channel_id=1, source_target_pairs={{0,2},{1,3},{2,0},{3,1},{4,6},{5,7},{6,4},{7,5},{8,10},{9,11},{10,... | collective-permute-start | bytes 786440 | tf_op jit(solution)/shard_map/ppermute | solution.py:738
  95.2 12.2 %collective-permute-start.21 = (bf16[64,2048]{1,0:T(8,128)(2,1)S(1)}, bf16[64,2048]{1,0:T(8,128)(2,1)S(1)}, u32[]{:S(2)}, u32[]{:S(2)}) collective-permute-start(bf16[64,2048]{1,0:T(8,128)(2,1)S(1)} %slice.19), channel_id=1, source_target_pairs={{0,2},{1,3},{2,0},{3,1},{4,6},{5,7},{6,4},{7,5},{8,10},{9,11},{10,... | collective-permute-start | bytes 786440 | tf_op jit(solution)/shard_map/ppermute | solution.py:738

commit v6 on v5

--- a/solution.py
+++ b/solution.py
@@ -594,7 +594,7 @@
 
     held = jnp.stack([for_group(my_group), turned(for_group(my_group ^ 1), near)])
     group_rows = [held] + [turned(held, turn) for turn in range(1, near)]
-    turns = (0, 3, 4, 7, 1, 2, 5, 6)
+    turns = (0, 1, 4, 7, 3, 2, 5, 6)
     head_rows = [turned(for_heads(turn), turn) if turn else for_heads(turn) for turn in turns]
 
     key_taps = lax.dynamic_slice_in_dim(conv_keys, my_group * STATE, STATE, 1)

time: 110 us -> 109 us (level); the launches traced: 108 us -> 109 us
  waiting for transfers between devices: 51.6 us -> 53.9 us
  starting transfers between devices: 27.6 us -> 25.7 us
    ppermute x4, starting transfers between devices: 3.57 us -> 2.34 us  [joined(): came = lax.ppermute(sent, 'tp', [(i, i ^ turn) for i in range(tp_count)])]
    ppermute x4, waiting for transfers between devices: 10.8 us -> 12 us  [joined(): came = lax.ppermute(sent, 'tp', [(i, i ^ turn) for i in range(tp_count)])]
  transfers between devices with their start and end apart: 22 -> 22, of which waited for: 13 -> 15; matrix products, arithmetic and copies ran while one was open for 3% -> 3% of each run, Pallas kernels for 15% -> 15%
where the time goes in v6:
time: 109 us
  waiting for transfers between devices  53.9 us (49%)
  starting transfers between devices  25.7 us (24%)
  Pallas kernels  22.8 us (21%)
  local copies, waits for them, and re-layouts  3.57 us (3%)
  other arithmetic  2.26 us (2%)
    ppermute x18, waiting for transfers between devices, turned(): return lax.ppermute(value, 'ctx', [(i, i ^ turn) for i in range(ctx_count)])  41.9 us
    ppermute x18, starting transfers between devices, turned(): return lax.ppermute(value, 'ctx', [(i, i ^ turn) for i in range(ctx_count)])  23.4 us
    ppermute x4, waiting for transfers between devices, joined(): came = lax.ppermute(sent, 'tp', [(i, i ^ turn) for i in range(tp_count)])  12 us
    pallas_call x3, Pallas kernels, project(): pl.pallas_call(kernel, in_specs=[smem, vmem, pl.BlockSpec(memory_space=we...  10.3 us
    pallas_call x1, Pallas kernels, head_split(): pl.pallas_call(functools.partial(mixing_kernel, heads, group_heads, per_d...  8.14 us
    pallas_call x1, Pallas kernels, head_split(): pl.pallas_call(functools.partial(scan_kernel, heads, per_dev, turns), in_...  4.38 us
    ppermute x4, starting transfers between devices, joined(): came = lax.ppermute(sent, 'tp', [(i, i ^ turn) for i in range(tp_count)])  2.34 us
  transfers between devices with their start and end apart: 22, of which 15 were waited for; matrix products, arithmetic and copies ran while one was open for 3% of the time, Pallas kernels for 15%

profile of v6, /device:TPU:16, one launch (start us, length us, event | category | flops | bytes accessed | tf_op | source)
XLA Modules:
  0.0 108.6 jit_solution(3183768243405625281)
XLA Ops:
  0.0 0.7 dynamic-slice_bitcast_fusion.17
  0.7 1.0 constant_dynamic-slice_fusion.2
  1.7 0.1 collective-permute-start.7
  1.9 1.8 %dynamic-slice_bitcast_fusion = (bf16[1,256,256]{2,1,0:T(8,128)(2,1)S(1)}, bf16[1,256,256]{2,1,0:T(8,128)(2,1)S(1)}, bf16[1,256,256]{2,1,0:T(8,128)(2,1)S(1)}, b...) fusion(bf16[256,2048]{1,0:T(8,128)(2,1)} %param.16, ...), kind=kLoop, calls=%fused_computation.16 | loop fusion | bytes 4194336 | tf_op jit(solution)/shard_map/stack | solution.py:591
  3.7 0.7 pad_maximum_fusion.7
  4.4 1.8 %collective-permute-start.4 = (bf16[2,256,256]{2,1,0:T(8,128)(2,1)}, bf16[2,256,256]{2,1,0:T(8,128)(2,1)S(1)}, u32[]{:S(2)}, u32[]{:S(2)}) collective-permute-start(bf16[2,256,256]{2,1,0:T(8,128)(2,1)} %pad_maximum_fusion.7), channel_id=1, source_target_pairs={{0,8},{4,12},{8,0},{12,4},{16,24},{20,28},{24,16},{28,20},{1,9},{5... | collective-permute-start | bytes 786440 | tf_op jit(solution)/shard_map/ppermute | solution.py:581
  6.3 3.6 %collective-permute-start.5 = (bf16[2,256,256]{2,1,0:T(8,128)(2,1)S(1)}, bf16[2,256,256]{2,1,0:T(8,128)(2,1)S(1)}, u32[]{:S(2)}, u32[]{:S(2)}) collective-permute-start(bf16[2,256,256]{2,1,0:T(8,128)(2,1)S(1)} %pad_maximum_fusion.8), channel_id=1, source_target_pairs={{0,20},{4,16},{8,28},{12,24},{16,4},{20,0},{24,12},{28,8},{1,21},{... | collective-permute-start | bytes 786440 | tf_op jit(solution)/shard_map/ppermute | solution.py:581
  10.1 3.7 %collective-permute-start.10 = (bf16[2,272,256]{2,1,0:T(8,128)(2,1)S(1)}, bf16[2,272,256]{2,1,0:T(8,128)(2,1)S(1)}, u32[]{:S(2)}, u32[]{:S(2)}) collective-permute-start(bf16[2,272,256]{2,1,0:T(8,128)(2,1)S(1)} %pad_maximum_fusion.1.refs_0_), channel_id=1, source_target_pairs={{0,12},{4,8},{8,4},{12,0},{16,28},{20,24},{24,20},{28,16},{1,13},{... | collective-permute-start | bytes 835592 | tf_op jit(solution)/shard_map/ppermute | solution.py:581
  13.8 0.5 collective-permute-start.8
  14.3 0.1 collective-permute-start.9
  14.5 6.4 %collective-permute-done.4.refs_5_ = bf16[2,256,256]{2,1,0:T(8,128)(2,1)S(1)} collective-permute-done((bf16[2,256,256]{2,1,0:T(8,128)(2,1)}, bf16[2,256,256]{2,1,0:T(8,128)(2,1)S(1)}, u32[]{:S(2)}, u32[]{:S(2)}) %collective-permute-start.4) | collective-permute-done | bytes 262176 | tf_op jit(solution)/shard_map/ppermute | solution.py:581
  20.9 3.3 %collective-permute-done.5.refs_6_ = bf16[2,256,256]{2,1,0:T(8,128)(2,1)S(1)} collective-permute-done((bf16[2,256,256]{2,1,0:T(8,128)(2,1)S(1)}, bf16[2,256,256]{2,1,0:T(8,128)(2,1)S(1)}, u32[]{:S(2)}, u32[]{:S(2)}) %collective-permute-start.5) | collective-permute-done | bytes 262176 | tf_op jit(solution)/shard_map/ppermute | solution.py:581
  24.2 0.7 collective-permute-start.3
  24.9 4.0 %collective-permute-done.10.refs_3_ = bf16[2,272,256]{2,1,0:T(8,128)(2,1)S(1)} collective-permute-done((bf16[2,272,256]{2,1,0:T(8,128)(2,1)S(1)}, bf16[2,272,256]{2,1,0:T(8,128)(2,1)S(1)}, u32[]{:S(2)}, u32[]{:S(2)}) %collective-permute-start.10) | collective-permute-done | bytes 278560 | tf_op jit(solution)/shard_map/ppermute | solution.py:581
  28.9 0.5 collective-permute-start.2
  29.4 6.6 %collective-permute-done.8.refs_1_ = bf16[2,272,256]{2,1,0:T(8,128)(2,1)S(1)} collective-permute-done((bf16[2,272,256]{2,1,0:T(8,128)(2,1)S(1)}, bf16[2,272,256]{2,1,0:T(8,128)(2,1)S(1)}, u32[]{:S(2)}, u32[]{:S(2)}) %collective-permute-start.8) | collective-permute-done | bytes 278560 | tf_op jit(solution)/shard_map/ppermute | solution.py:581
  36.0 4.7 %collective-permute-done.9.refs_2_ = bf16[2,272,256]{2,1,0:T(8,128)(2,1)S(1)} collective-permute-done((bf16[2,272,256]{2,1,0:T(8,128)(2,1)S(1)}, bf16[2,272,256]{2,1,0:T(8,128)(2,1)S(1)}, u32[]{:S(2)}, u32[]{:S(2)}) %collective-permute-start.9) | collective-permute-done | bytes 278560 | tf_op jit(solution)/shard_map/ppermute | solution.py:581
  40.8 1.8 %collective-permute-start = (bf16[2,256,256]{2,1,0:T(8,128)(2,1)S(1)}, bf16[2,256,256]{2,1,0:T(8,128)(2,1)S(1)}, u32[]{:S(2)}, u32[]{:S(2)}) collective-permute-start(bf16[2,256,256]{2,1,0:T(8,128)(2,1)S(1)} %pad_maximum_fusion.3), channel_id=1, source_target_pairs={{0,4},{4,0},{8,12},{12,8},{16,20},{20,16},{24,28},{28,24},{1,5},{5... | collective-permute-start | bytes 786440 | tf_op jit(solution)/shard_map/ppermute | solution.py:581
  42.5 0.1 pad_add_fusion.me_ref.place_ref
  42.7 8.1 %mixing.1 = (bf16[16,128,512]{2,1,0:T(8,128)(2,1)S(1)}, bf16[16,128,128]{2,1,0:T(8,128)(2,1)S(1)}, bf16[16,128,128]{2,1,0:T(8,128)(2,1)S(1)}, f32[16,128,256]{2,...) custom-call(s32[2]{0:T(128)S(1)} %pad_add_fusion.me_ref.place_ref, ...), custom_call_target="tpu_custom_call" | custom-call | flops 20000000 | bytes 20000000 | tf_op jit(solution)/shard_map/mixing/pallas_call | solution.py:626
  50.8 2.6 %collective-permute-done.3.refs_4_ = bf16[2,256,256]{2,1,0:T(8,128)(2,1)S(1)} collective-permute-done((bf16[2,256,256]{2,1,0:T(8,128)(2,1)S(1)}, bf16[2,256,256]{2,1,0:T(8,128)(2,1)S(1)}, u32[]{:S(2)}, u32[]{:S(2)}) %collective-permute-start.3) | collective-permute-done | bytes 262176 | tf_op jit(solution)/shard_map/ppermute | solution.py:581
  53.4 2.5 %collective-permute-done.1.refs_2_ = bf16[2,256,256]{2,1,0:T(8,128)(2,1)S(1)} collective-permute-done((bf16[2,256,256]{2,1,0:T(8,128)(2,1)S(1)}, bf16[2,256,256]{2,1,0:T(8,128)(2,1)S(1)}, u32[]{:S(2)}, u32[]{:S(2)}) %collective-permute-start.1) | collective-permute-done | bytes 262176 | tf_op jit(solution)/shard_map/ppermute | solution.py:581
  56.0 4.4 %scan.1 = (bf16[256,256]{1,0:T(8,128)(2,1)S(1)}, bf16[256,256]{1,0:T(8,128)(2,1)S(1)}, bf16[256,256]{1,0:T(8,128)(2,1)S(1)}, bf16[256,256]{1,0:T(8,128)(2,1)S(1)...) custom-call(s32[2]{0:T(128)S(1)} %pad_add_fusion.me_ref.place_ref, ...), custom_call_target="tpu_custom_call" | custom-call | flops 600000000 | bytes 14000000 | tf_op jit(solution)/shard_map/scan/pallas_call | solution.py:646
  60.3 1.5 %collective-permute-start.11 = (bf16[256,256]{1,0:T(8,128)(2,1)S(1)}, bf16[256,256]{1,0:T(8,128)(2,1)S(1)}, u32[]{:S(2)}, u32[]{:S(2)}) collective-permute-start(bf16[256,256]{1,0:T(8,128)(2,1)S(1)} %get-tuple-element.35), channel_id=1, source_target_pairs={{0,4},{4,0},{8,12},{12,8},{16,20},{20,16},{24,28},{28,24},{1,5},{5... | collective-permute-start | bytes 393224 | tf_op jit(solution)/shard_map/ppermute | solution.py:581
  61.8 2.8 %collective-permute-start.12 = (bf16[256,256]{1,0:T(8,128)(2,1)S(1)}, bf16[256,256]{1,0:T(8,128)(2,1)S(1)}, u32[]{:S(2)}, u32[]{:S(2)}) collective-permute-start(bf16[256,256]{1,0:T(8,128)(2,1)S(1)} %get-tuple-element.36), channel_id=1, source_target_pairs={{0,8},{4,12},{8,0},{12,4},{16,24},{20,28},{24,16},{28,20},{1,9},{5... | collective-permute-start | bytes 393224 | tf_op jit(solution)/shard_map/ppermute | solution.py:581
  64.6 0.5 collective-permute-start.13
  65.1 2.2 %collective-permute-start.14 = (bf16[256,256]{1,0:T(8,128)(2,1)S(1)}, bf16[256,256]{1,0:T(8,128)(2,1)S(1)}, u32[]{:S(2)}, u32[]{:S(2)}) collective-permute-start(bf16[256,256]{1,0:T(8,128)(2,1)S(1)} %get-tuple-element.40), channel_id=1, source_target_pairs={{0,16},{4,20},{8,24},{12,28},{16,0},{20,4},{24,8},{28,12},{1,17},{... | collective-permute-start | bytes 393224 | tf_op jit(solution)/shard_map/ppermute | solution.py:581
  67.3 1.2 %collective-permute-start.15 = (bf16[256,256]{1,0:T(8,128)(2,1)S(1)}, bf16[256,256]{1,0:T(8,128)(2,1)S(1)}, u32[]{:S(2)}, u32[]{:S(2)}) collective-permute-start(bf16[256,256]{1,0:T(8,128)(2,1)S(1)} %get-tuple-element.41), channel_id=1, source_target_pairs={{0,20},{4,16},{8,28},{12,24},{16,4},{20,0},{24,12},{28,8},{1,21},{... | collective-permute-start | bytes 393224 | tf_op jit(solution)/shard_map/ppermute | solution.py:581
  68.4 1.0 collective-permute-start.16
  69.5 1.4 %collective-permute-start.17 = (bf16[256,256]{1,0:T(8,128)(2,1)S(1)}, bf16[256,256]{1,0:T(8,128)(2,1)S(1)}, u32[]{:S(2)}, u32[]{:S(2)}) collective-permute-start(bf16[256,256]{1,0:T(8,128)(2,1)S(1)} %get-tuple-element.43), channel_id=1, source_target_pairs={{0,28},{4,24},{8,20},{12,16},{16,12},{20,8},{24,4},{28,0},{1,29},{... | collective-permute-start | bytes 393224 | tf_op jit(solution)/shard_map/ppermute | solution.py:581
  70.9 1.3 %collective-permute-done.13.refs_3_ = bf16[256,256]{1,0:T(8,128)(2,1)S(1)} collective-permute-done((bf16[256,256]{1,0:T(8,128)(2,1)S(1)}, bf16[256,256]{1,0:T(8,128)(2,1)S(1)}, u32[]{:S(2)}, u32[]{:S(2)}) %collective-permute-start.13) | collective-permute-done | bytes 131104 | tf_op jit(solution)/shard_map/ppermute | solution.py:581
  72.2 6.5 %near_projection.1 = (f32[256,4096]{1,0:T(8,128)S(1)}, bf16[1024,4096]{1,0:T(8,128)(2,1)S(1)}) custom-call(s32[2]{0:T(128)S(1)} %pad_add_fusion.me_ref.place_ref, f32[8,256]{1,0:T(8,128)S(1)} %reshape.6.gain_ref, bf16[2,1024,4096]{2,1,0:T(8,128)(2,1)} %bitcast.42, bf16[256,256]{1,0:T(8,128)(2,1)S(1)} %get-tuple-element.34.refs_0_, ...), custom_call_target="tpu_custom_call" | custom-call | flops 2147483648 | bytes 8388608 | tf_op jit(solution)/shard_map/near_projection/pallas_call | solution.py:674
  78.7 2.1 %collective-permute-done.14.refs_0_ = bf16[256,256]{1,0:T(8,128)(2,1)S(1)} collective-permute-done((bf16[256,256]{1,0:T(8,128)(2,1)S(1)}, bf16[256,256]{1,0:T(8,128)(2,1)S(1)}, u32[]{:S(2)}, u32[]{:S(2)}) %collective-permute-start.14) | collective-permute-done | bytes 131104 | tf_op jit(solution)/shard_map/ppermute | solution.py:581
  80.8 2.8 %collective-permute-done.15.refs_1_ = bf16[256,256]{1,0:T(8,128)(2,1)S(1)} collective-permute-done((bf16[256,256]{1,0:T(8,128)(2,1)S(1)}, bf16[256,256]{1,0:T(8,128)(2,1)S(1)}, u32[]{:S(2)}, u32[]{:S(2)}) %collective-permute-start.15) | collective-permute-done | bytes 131104 | tf_op jit(solution)/shard_map/ppermute | solution.py:581
  83.7 3.5 %collective-permute-done.16.refs_2_ = bf16[256,256]{1,0:T(8,128)(2,1)S(1)} collective-permute-done((bf16[256,256]{1,0:T(8,128)(2,1)S(1)}, bf16[256,256]{1,0:T(8,128)(2,1)S(1)}, u32[]{:S(2)}, u32[]{:S(2)}) %collective-permute-start.16) | collective-permute-done | bytes 131104 | tf_op jit(solution)/shard_map/ppermute | solution.py:581
  87.2 2.0 %collective-permute-done.17.refs_3_ = bf16[256,256]{1,0:T(8,128)(2,1)S(1)} collective-permute-done((bf16[256,256]{1,0:T(8,128)(2,1)S(1)}, bf16[256,256]{1,0:T(8,128)(2,1)S(1)}, u32[]{:S(2)}, u32[]{:S(2)}) %collective-permute-start.17) | collective-permute-done | bytes 131104 | tf_op jit(solution)/shard_map/ppermute | solution.py:581
  89.2 2.0 %far_projection.1 = (bf16[128,2048]{1,0:T(8,128)(2,1)S(1)}, bf16[128,2048]{1,0:T(8,128)(2,1)S(1)}, bf16[256,1024]{1,0:T(8,128)(2,1)S(1)}) custom-call(s32[2]{0:T(128)S(1)} %pad_add_fusion.me_ref.place_ref, f32[8,256]{1,0:T(8,128)S(1)} %reshape.6.gain_ref, bf16[1024,4096]{1,0:T(8,128)(2,1)S(1)} %get-tuple-element.38.weight_ref, ...), custom_call_target="tpu_custom_call" | custom-call | flops 2147483648 | bytes 8388608 | tf_op jit(solution)/shard_map/far_projection/pallas_call | solution.py:674
  91.2 0.1 collective-permute-start.18
  91.2 1.8 %rest_projection.1 = (bf16[128,2048]{1,0:T(8,128)(2,1)S(1)}, bf16[128,2048]{1,0:T(8,128)(2,1)S(1)}) custom-call(s32[2]{0:T(128)S(1)} %pad_add_fusion.me_ref.place_ref, bf16[256,1024]{1,0:T(8,128)(2,1)S(1)} %get-tuple-element.46.normed_ref, bf16[1024,4096]{1,0:T(8,128)(2,1)S(1)} %get-tuple-element.38.weight_ref, f32[256,4096]{1,0:T(8,128)S(1)} %get-tuple-element.39.near_ref), custom_call_target="tpu_custom_call" | custom-call | flops 2147483648 | bytes 8388608 | tf_op jit(solution)/shard_map/rest_projection/pallas_call | solution.py:674
  93.1 0.6 collective-permute-start.20
  93.6 0.1 add_convert_fusion.1
  93.8 0.9 collective-permute-start.19
  94.6 0.5 collective-permute-done.20
  95.2 0.1 add_convert_fusion
  95.3 0.9 collective-permute-start.21
  96.2 6.8 %collective-permute-done.19 = bf16[64,2048]{1,0:T(8,128)(2,1)S(1)} collective-permute-done((bf16[64,2048]{1,0:T(8,128)(2,1)S(1)}, bf16[64,2048]{1,0:T(8,128)(2,1)S(1)}, u32[]{:S(2)}, u32[]{:S(2)}) %collective-permute-start.19) | collective-permute-done | bytes 262176 | tf_op jit(solution)/shard_map/ppermute | solution.py:738
  103.1 4.6 %collective-permute-done.21 = bf16[64,2048]{1,0:T(8,128)(2,1)S(1)} collective-permute-done((bf16[64,2048]{1,0:T(8,128)(2,1)S(1)}, bf16[64,2048]{1,0:T(8,128)(2,1)S(1)}, u32[]{:S(2)}, u32[]{:S(2)}) %collective-permute-start.21) | collective-permute-done | bytes 262176 | tf_op jit(solution)/shard_map/ppermute | solution.py:738
  107.8 0.8 pad_maximum_fusion
  (44 shorter events, 0.5 us)
Async XLA Ops:
  0.0 14.4 %copy-start = (f32[4,2048]{1,0:T(4,128)S(1)}, f32[4,2048]{1,0:T(4,128)}, u32[]{:S(2)}) copy-start(f32[4,2048]{1,0:T(4,128)} %param.22) | copy-start | bytes 98308
  1.7 8.3 %collective-permute-start.7 = (bf16[272,256]{1,0:T(8,128)(2,1)S(1)}, bf16[272,256]{1,0:T(8,128)(2,1)S(1)}, u32[]{:S(2)}, u32[]{:S(2)}) collective-permute-start(bf16[272,256]{1,0:T(8,128)(2,1)S(1)} %pad_maximum_fusion.10), channel_id=1, source_target_pairs={{0,16},{4,20},{8,24},{12,28},{16,0},{20,4},{24,8},{28,12},{1,17},{... | collective-permute-start | bytes 417800 | tf_op jit(solution)/shard_map/ppermute | solution.py:581
  1.8 40.8 %copy-start.7 = (f32[4,256]{1,0:T(4,128)S(1)}, f32[4,256]{1,0:T(4,128)}, u32[]{:S(2)}) copy-start(f32[4,256]{1,0:T(4,128)} %param.24) | copy-start | bytes 12292
  1.8 40.8 %copy-start.8 = (f32[4,256]{1,0:T(4,128)S(1)}, f32[4,256]{1,0:T(4,128)}, u32[]{:S(2)}) copy-start(f32[4,256]{1,0:T(4,128)} %param.23) | copy-start | bytes 12292
  1.9 40.8 %copy-start.1 = (s32[32]{0:T(128)S(1)}, s32[32]{0:T(128)}, u32[]{:S(2)}) copy-start(s32[32]{0:T(128)} %order_ref.3) | copy-start | bytes 388
  1.9 40.8 %copy-start.3 = (s32[16]{0:T(128)S(1)}, s32[16]{0:T(128)}, u32[]{:S(2)}) copy-start(s32[16]{0:T(128)} %lengths_ref.1) | copy-start | bytes 196
  1.9 40.8 %copy-start.4 = (f32[32]{0:T(128)S(1)}, f32[32]{0:T(128)}, u32[]{:S(2)}) copy-start(f32[32]{0:T(128)} %bias_ref.1) | copy-start | bytes 388
  1.9 40.8 %copy-start.5 = (f32[32]{0:T(128)S(1)}, f32[32]{0:T(128)}, u32[]{:S(2)}) copy-start(f32[32]{0:T(128)} %log_ref.1) | copy-start | bytes 388
  4.4 51.5 %copy-start.2 = (f32[32]{0:T(128)S(1)}, f32[32]{0:T(128)}, u32[]{:S(2)}) copy-start(f32[32]{0:T(128)} %skip_ref.1) | copy-start | bytes 388
  4.4 16.5 %collective-permute-start.4 = (bf16[2,256,256]{2,1,0:T(8,128)(2,1)}, bf16[2,256,256]{2,1,0:T(8,128)(2,1)S(1)}, u32[]{:S(2)}, u32[]{:S(2)}) collective-permute-start(bf16[2,256,256]{2,1,0:T(8,128)(2,1)} %pad_maximum_fusion.7), channel_id=1, source_target_pairs={{0,8},{4,12},{8,0},{12,4},{16,24},{20,28},{24,16},{28,20},{1,9},{5... | collective-permute-start | bytes 786440 | tf_op jit(solution)/shard_map/ppermute | solution.py:581
  6.3 17.9 %collective-permute-start.5 = (bf16[2,256,256]{2,1,0:T(8,128)(2,1)S(1)}, bf16[2,256,256]{2,1,0:T(8,128)(2,1)S(1)}, u32[]{:S(2)}, u32[]{:S(2)}) collective-permute-start(bf16[2,256,256]{2,1,0:T(8,128)(2,1)S(1)} %pad_maximum_fusion.8), channel_id=1, source_target_pairs={{0,20},{4,16},{8,28},{12,24},{16,4},{20,0},{24,12},{28,8},{1,21},{... | collective-permute-start | bytes 786440 | tf_op jit(solution)/shard_map/ppermute | solution.py:581
  10.1 18.8 %collective-permute-start.10 = (bf16[2,272,256]{2,1,0:T(8,128)(2,1)S(1)}, bf16[2,272,256]{2,1,0:T(8,128)(2,1)S(1)}, u32[]{:S(2)}, u32[]{:S(2)}) collective-permute-start(bf16[2,272,256]{2,1,0:T(8,128)(2,1)S(1)} %pad_maximum_fusion.1.refs_0_), channel_id=1, source_target_pairs={{0,12},{4,8},{8,4},{12,0},{16,28},{20,24},{24,20},{28,16},{1,13},{... | collective-permute-start | bytes 835592 | tf_op jit(solution)/shard_map/ppermute | solution.py:581
  13.8 22.2 %collective-permute-start.8 = (bf16[2,272,256]{2,1,0:T(8,128)(2,1)S(1)}, bf16[2,272,256]{2,1,0:T(8,128)(2,1)S(1)}, u32[]{:S(2)}, u32[]{:S(2)}) collective-permute-start(bf16[2,272,256]{2,1,0:T(8,128)(2,1)S(1)} %pad_maximum_fusion.1.refs_0_), channel_id=1, source_target_pairs={{0,4},{4,0},{8,12},{12,8},{16,20},{20,16},{24,28},{28,24},{1,5},{5... | collective-permute-start | bytes 835592 | tf_op jit(solution)/shard_map/ppermute | solution.py:581
  14.3 26.5 %collective-permute-start.9 = (bf16[2,272,256]{2,1,0:T(8,128)(2,1)S(1)}, bf16[2,272,256]{2,1,0:T(8,128)(2,1)S(1)}, u32[]{:S(2)}, u32[]{:S(2)}) collective-permute-start(bf16[2,272,256]{2,1,0:T(8,128)(2,1)S(1)} %pad_maximum_fusion.1.refs_0_), channel_id=1, source_target_pairs={{0,8},{4,12},{8,0},{12,4},{16,24},{20,28},{24,16},{28,20},{1,9},{5... | collective-permute-start | bytes 835592 | tf_op jit(solution)/shard_map/ppermute | solution.py:581
  20.9 29.9 %collective-permute-start.6 = (bf16[2,256,256]{2,1,0:T(8,128)(2,1)S(1)}, bf16[2,256,256]{2,1,0:T(8,128)(2,1)S(1)}, u32[]{:S(2)}, u32[]{:S(2)}) collective-permute-start(bf16[2,256,256]{2,1,0:T(8,128)(2,1)S(1)} %pad_maximum_fusion.9), channel_id=1, source_target_pairs={{0,24},{4,28},{8,16},{12,20},{16,8},{20,12},{24,0},{28,4},{1,25},{... | collective-permute-start | bytes 786440 | tf_op jit(solution)/shard_map/ppermute | solution.py:581
  24.2 29.2 %collective-permute-start.3 = (bf16[2,256,256]{2,1,0:T(8,128)(2,1)S(1)}, bf16[2,256,256]{2,1,0:T(8,128)(2,1)S(1)}, u32[]{:S(2)}, u32[]{:S(2)}) collective-permute-start(bf16[2,256,256]{2,1,0:T(8,128)(2,1)S(1)} %pad_maximum_fusion.6), channel_id=1, source_target_pairs={{0,12},{4,8},{8,4},{12,0},{16,28},{20,24},{24,20},{28,16},{1,13},{... | collective-permute-start | bytes 786440 | tf_op jit(solution)/shard_map/ppermute | solution.py:581
  28.9 24.5 %collective-permute-start.2 = (bf16[2,256,256]{2,1,0:T(8,128)(2,1)S(1)}, bf16[2,256,256]{2,1,0:T(8,128)(2,1)S(1)}, u32[]{:S(2)}, u32[]{:S(2)}) collective-permute-start(bf16[2,256,256]{2,1,0:T(8,128)(2,1)S(1)} %pad_maximum_fusion.5), channel_id=1, source_target_pairs={{0,28},{4,24},{8,20},{12,16},{16,12},{20,8},{24,4},{28,0},{1,29},{... | collective-permute-start | bytes 786440 | tf_op jit(solution)/shard_map/ppermute | solution.py:581
  36.0 19.9 %collective-permute-start.1 = (bf16[2,256,256]{2,1,0:T(8,128)(2,1)S(1)}, bf16[2,256,256]{2,1,0:T(8,128)(2,1)S(1)}, u32[]{:S(2)}, u32[]{:S(2)}) collective-permute-start(bf16[2,256,256]{2,1,0:T(8,128)(2,1)S(1)} %pad_maximum_fusion.4), channel_id=1, source_target_pairs={{0,16},{4,20},{8,24},{12,28},{16,0},{20,4},{24,8},{28,12},{1,17},{... | collective-permute-start | bytes 786440 | tf_op jit(solution)/shard_map/ppermute | solution.py:581
  40.8 15.2 %collective-permute-start = (bf16[2,256,256]{2,1,0:T(8,128)(2,1)S(1)}, bf16[2,256,256]{2,1,0:T(8,128)(2,1)S(1)}, u32[]{:S(2)}, u32[]{:S(2)}) collective-permute-start(bf16[2,256,256]{2,1,0:T(8,128)(2,1)S(1)} %pad_maximum_fusion.3), channel_id=1, source_target_pairs={{0,4},{4,0},{8,12},{12,8},{16,20},{20,16},{24,28},{28,24},{1,5},{5... | collective-permute-start | bytes 786440 | tf_op jit(solution)/shard_map/ppermute | solution.py:581
  55.9 9.1 %copy-start.6 = (f32[2048]{0:T(1024)S(1)}, f32[2048]{0:T(1024)}, u32[]{:S(2)}) copy-start(f32[2048]{0:T(1024)} %param.28) | copy-start | bytes 24580
  60.3 8.1 %collective-permute-start.11 = (bf16[256,256]{1,0:T(8,128)(2,1)S(1)}, bf16[256,256]{1,0:T(8,128)(2,1)S(1)}, u32[]{:S(2)}, u32[]{:S(2)}) collective-permute-start(bf16[256,256]{1,0:T(8,128)(2,1)S(1)} %get-tuple-element.35), channel_id=1, source_target_pairs={{0,4},{4,0},{8,12},{12,8},{16,20},{20,16},{24,28},{28,24},{1,5},{5... | collective-permute-start | bytes 393224 | tf_op jit(solution)/shard_map/ppermute | solution.py:581
  61.8 7.7 %collective-permute-start.12 = (bf16[256,256]{1,0:T(8,128)(2,1)S(1)}, bf16[256,256]{1,0:T(8,128)(2,1)S(1)}, u32[]{:S(2)}, u32[]{:S(2)}) collective-permute-start(bf16[256,256]{1,0:T(8,128)(2,1)S(1)} %get-tuple-element.36), channel_id=1, source_target_pairs={{0,8},{4,12},{8,0},{12,4},{16,24},{20,28},{24,16},{28,20},{1,9},{5... | collective-permute-start | bytes 393224 | tf_op jit(solution)/shard_map/ppermute | solution.py:581
  64.6 7.6 %collective-permute-start.13 = (bf16[256,256]{1,0:T(8,128)(2,1)S(1)}, bf16[256,256]{1,0:T(8,128)(2,1)S(1)}, u32[]{:S(2)}, u32[]{:S(2)}) collective-permute-start(bf16[256,256]{1,0:T(8,128)(2,1)S(1)} %get-tuple-element.37), channel_id=1, source_target_pairs={{0,12},{4,8},{8,4},{12,0},{16,28},{20,24},{24,20},{28,16},{1,13},{... | collective-permute-start | bytes 393224 | tf_op jit(solution)/shard_map/ppermute | solution.py:581
  65.1 15.8 %collective-permute-start.14 = (bf16[256,256]{1,0:T(8,128)(2,1)S(1)}, bf16[256,256]{1,0:T(8,128)(2,1)S(1)}, u32[]{:S(2)}, u32[]{:S(2)}) collective-permute-start(bf16[256,256]{1,0:T(8,128)(2,1)S(1)} %get-tuple-element.40), channel_id=1, source_target_pairs={{0,16},{4,20},{8,24},{12,28},{16,0},{20,4},{24,8},{28,12},{1,17},{... | collective-permute-start | bytes 393224 | tf_op jit(solution)/shard_map/ppermute | solution.py:581
  67.3 16.4 %collective-permute-start.15 = (bf16[256,256]{1,0:T(8,128)(2,1)S(1)}, bf16[256,256]{1,0:T(8,128)(2,1)S(1)}, u32[]{:S(2)}, u32[]{:S(2)}) collective-permute-start(bf16[256,256]{1,0:T(8,128)(2,1)S(1)} %get-tuple-element.41), channel_id=1, source_target_pairs={{0,20},{4,16},{8,28},{12,24},{16,4},{20,0},{24,12},{28,8},{1,21},{... | collective-permute-start | bytes 393224 | tf_op jit(solution)/shard_map/ppermute | solution.py:581
  68.4 18.7 %collective-permute-start.16 = (bf16[256,256]{1,0:T(8,128)(2,1)S(1)}, bf16[256,256]{1,0:T(8,128)(2,1)S(1)}, u32[]{:S(2)}, u32[]{:S(2)}) collective-permute-start(bf16[256,256]{1,0:T(8,128)(2,1)S(1)} %get-tuple-element.42), channel_id=1, source_target_pairs={{0,24},{4,28},{8,16},{12,20},{16,8},{20,12},{24,0},{28,4},{1,25},{... | collective-permute-start | bytes 393224 | tf_op jit(solution)/shard_map/ppermute | solution.py:581
  69.5 19.7 %collective-permute-start.17 = (bf16[256,256]{1,0:T(8,128)(2,1)S(1)}, bf16[256,256]{1,0:T(8,128)(2,1)S(1)}, u32[]{:S(2)}, u32[]{:S(2)}) collective-permute-start(bf16[256,256]{1,0:T(8,128)(2,1)S(1)} %get-tuple-element.43), channel_id=1, source_target_pairs={{0,28},{4,24},{8,20},{12,16},{16,12},{20,8},{24,4},{28,0},{1,29},{... | collective-permute-start | bytes 393224 | tf_op jit(solution)/shard_map/ppermute | solution.py:581
  91.2 2.5 %collective-permute-start.18 = (bf16[128,2048]{1,0:T(8,128)(2,1)S(1)}, bf16[128,2048]{1,0:T(8,128)(2,1)S(1)}, u32[]{:S(2)}, u32[]{:S(2)}) collective-permute-start(bf16[128,2048]{1,0:T(8,128)(2,1)S(1)} %get-tuple-element.45), channel_id=1, source_target_pairs={{0,1},{1,0},{2,3},{3,2},{4,5},{5,4},{6,7},{7,6},{8,9},{9,8},{10,11... | collective-permute-start | bytes 1572872 | tf_op jit(solution)/shard_map/ppermute | solution.py:738
  93.1 2.1 %collective-permute-start.20 = (bf16[128,2048]{1,0:T(8,128)(2,1)S(1)}, bf16[128,2048]{1,0:T(8,128)(2,1)S(1)}, u32[]{:S(2)}, u32[]{:S(2)}) collective-permute-start(bf16[128,2048]{1,0:T(8,128)(2,1)S(1)} %get-tuple-element.48), channel_id=1, source_target_pairs={{0,1},{1,0},{2,3},{3,2},{4,5},{5,4},{6,7},{7,6},{8,9},{9,8},{10,11... | collective-permute-start | bytes 1572872 | tf_op jit(solution)/shard_map/ppermute | solution.py:738
  93.8 9.2 %collective-permute-start.19 = (bf16[64,2048]{1,0:T(8,128)(2,1)S(1)}, bf16[64,2048]{1,0:T(8,128)(2,1)S(1)}, u32[]{:S(2)}, u32[]{:S(2)}) collective-permute-start(bf16[64,2048]{1,0:T(8,128)(2,1)S(1)} %slice.17), channel_id=1, source_target_pairs={{0,2},{1,3},{2,0},{3,1},{4,6},{5,7},{6,4},{7,5},{8,10},{9,11},{10,... | collective-permute-start | bytes 786440 | tf_op jit(solution)/shard_map/ppermute | solution.py:738
  95.3 12.4 %collective-permute-start.21 = (bf16[64,2048]{1,0:T(8,128)(2,1)S(1)}, bf16[64,2048]{1,0:T(8,128)(2,1)S(1)}, u32[]{:S(2)}, u32[]{:S(2)}) collective-permute-start(bf16[64,2048]{1,0:T(8,128)(2,1)S(1)} %slice.19), channel_id=1, source_target_pairs={{0,2},{1,3},{2,0},{3,1},{4,6},{5,7},{6,4},{7,5},{8,10},{9,11},{10,... | collective-permute-start | bytes 786440 | tf_op jit(solution)/shard_map/ppermute | solution.py:738

commit v7 on v6

--- a/solution.py
+++ b/solution.py
@@ -479,20 +479,11 @@
         out_ref[...] = laid[jnp.bitwise_xor(me, turn)]
 
 
-def normed_into(normed, gated_refs, gain_ref, me, first_turn):
-    count = len(gated_refs)
-    rows, width = gated_refs[0].shape
-    wide = [ref[...].astype(jnp.float32) for ref in gated_refs]
-    squares = wide[0] * wide[0]
-    for piece in wide[1:]:
+def squares_of(pieces):
+    squares = pieces[0] * pieces[0]
+    for piece in pieces[1:]:
         squares = squares + piece * piece
-    mean = jnp.sum(squares, axis=1, keepdims=True) * (1.0 / (count * width))
-    inverse_rms = lax.rsqrt(mean + 1e-05)
-    for turn, piece in enumerate(wide):
-        source = jnp.bitwise_xor(me, first_turn + turn)
-        at = pl.multiple_of(lax.rem(source, count) * width, width)
-        gain = gain_ref[pl.ds(source, 1), :]
-        normed[:, pl.ds(at, width)] = (piece * inverse_rms * gain).astype(jnp.bfloat16)
+    return jnp.sum(squares, axis=1, keepdims=True)
 
 
 def weight_tiles(weight_ref, group, buffer, sems, count):
@@ -505,24 +496,43 @@
 
 
 def near_kernel(place_ref, gain_ref, weight_ref, *refs):
-    gated_refs, (partial_ref, next_ref, normed, buffer, sems) = refs[:-5], refs[-5:]
-    count = sems.shape[0] - 1
-    group = lax.div(place_ref[0], len(gated_refs))
+    gated_refs, refs = refs[:-6], refs[-6:]
+    partial_ref, squares_ref, next_ref, gained, buffer, sems = refs
+    me = place_ref[0]
+    near = len(gated_refs) + 1
+    width = gated_refs[0].shape[1]
+    depth = near * width
+    count = sems.shape[0] - 2
+    group = lax.div(me, near)
+    last = pl.multiple_of(lax.rem(jnp.bitwise_xor(me, near - 1), near) * width, width)
     tiles, copies = weight_tiles(weight_ref, group, buffer, sems, count)
-    onward = pltpu.make_async_copy(weight_ref.at[1 - group], next_ref, sems.at[count])
-    for copy in copies + [onward]:
+    onward = [
+        pltpu.make_async_copy(weight_ref.at[1 - group], next_ref.at[:depth], sems.at[count]),
+        pltpu.make_async_copy(
+            weight_ref.at[group, pl.ds(last, width)], next_ref.at[depth:], sems.at[count + 1]
+        ),
+    ]
+    for copy in copies + onward:
         copy.start()
-    normed_into(normed, gated_refs, gain_ref, place_ref[0], 0)
+    wide = [ref[...].astype(jnp.float32) for ref in gated_refs]
+    squares_ref[...] = jnp.broadcast_to(squares_of(wide), squares_ref.shape)
+    for turn, piece in enumerate(wide):
+        source = jnp.bitwise_xor(me, turn)
+        at = pl.multiple_of(lax.rem(source, near) * width, width)
+        gained[:, pl.ds(at, width)] = (piece * gain_ref[pl.ds(source, 1), :]).astype(jnp.bfloat16)
+    gained[:, pl.ds(last, width)] = jnp.zeros((gained.shape[0], width), jnp.bfloat16)
     for at, copy in zip(tiles, copies):
         copy.wait()
         partial_ref[:, at] = jnp.dot(
-            normed[...], buffer[:, at], preferred_element_type=jnp.float32
-        )
-    onward.wait()
-
-
-def project_far(normed, weight_ref, near_ref, at, away_ref, stay_ref):
-    partial = near_ref[:, at] + jnp.dot(
+            gained[...], buffer[:, at], preferred_element_type=jnp.float32
+        )
+    for copy in onward:
+        copy.wait()
+
+
+def project_far(normed, scale, weight_ref, near_ref, at, away_ref, stay_ref):
+    wide_scale = jnp.concatenate([scale] * (away_ref.shape[1] // LANES), axis=1)
+    partial = near_ref[:, at] * wide_scale + jnp.dot(
         normed, weight_ref[:, at], preferred_element_type=jnp.float32
     )
     partial = partial.astype(jnp.bfloat16)
@@ -531,16 +541,31 @@
     stay_ref[...] = partial[rows:]
 
 
-def far_kernel(place_ref, gain_ref, weight_ref, near_ref, *refs):
-    gated_refs, (away_ref, stay_ref, normed) = refs[:-3], refs[-3:]
-    normed_into(normed, gated_refs, gain_ref, place_ref[0], len(gated_refs))
+def far_kernel(place_ref, gain_ref, weight_ref, near_ref, squares_ref, *refs):
+    gated_refs, (away_ref, stay_ref, normed, scale_ref) = refs[:-4], refs[-4:]
+    me = place_ref[0]
+    near = len(gated_refs) - 1
+    rows, width = gated_refs[0].shape
+    share = 1.0 / (near * width)
+    wide = [ref[...].astype(jnp.float32) for ref in gated_refs]
+    far_scale = lax.rsqrt(squares_of(wide[:near]) * share + 1e-05)
+    for turn, piece in enumerate(wide[:near]):
+        source = jnp.bitwise_xor(me, near + turn)
+        at = pl.multiple_of(lax.rem(source, near) * width, width)
+        gain = gain_ref[pl.ds(source, 1), :]
+        normed[:, pl.ds(at, width)] = (piece * far_scale * gain).astype(jnp.bfloat16)
+    near_scale = lax.rsqrt((squares_ref[:, :1] + squares_of(wide[near:])) * share + 1e-05)
+    gain = gain_ref[pl.ds(jnp.bitwise_xor(me, near - 1), 1), :]
+    normed[:, near * width :] = (wide[near] * near_scale * gain).astype(jnp.bfloat16)
+    scale = jnp.broadcast_to(near_scale, scale_ref.shape)
+    scale_ref[...] = scale
     at = slice(0, away_ref.shape[1])
-    project_far(normed[...], weight_ref, near_ref, at, away_ref, stay_ref)
-
-
-def rest_kernel(place_ref, normed_ref, weight_ref, near_ref, away_ref, stay_ref):
+    project_far(normed[...], scale, weight_ref, near_ref, at, away_ref, stay_ref)
+
+
+def rest_kernel(place_ref, normed_ref, weight_ref, near_ref, scale_ref, away_ref, stay_ref):
     at = slice(near_ref.shape[1] - away_ref.shape[1], near_ref.shape[1])
-    project_far(normed_ref[...], weight_ref, near_ref, at, away_ref, stay_ref)
+    project_far(normed_ref[...], scale_ref[...], weight_ref, near_ref, at, away_ref, stay_ref)
 
 
 def head_split(
@@ -686,38 +711,41 @@
             name=name,
         )(place, first, weight, *operands)
 
-    near_partial, far_weight = project(
+    far_width = group_width + width
+    row_shape = jax.ShapeDtypeStruct((token_count, LANES), jnp.float32)
+    near_partial, near_squares, far_weight = project(
         near_kernel,
         gain,
         weight,
         pl.ANY,
-        pieces[:near],
+        pieces[: near - 1],
         [
             jax.ShapeDtypeStruct((token_count, columns), jnp.float32),
-            jax.ShapeDtypeStruct((group_width, columns), jnp.bfloat16),
+            row_shape,
+            jax.ShapeDtypeStruct((far_width, columns), jnp.bfloat16),
         ],
         [
             pltpu.VMEM((token_count, group_width), jnp.bfloat16),
             pltpu.VMEM((group_width, columns), jnp.bfloat16),
-            pltpu.SemaphoreType.DMA((5,)),
+            pltpu.SemaphoreType.DMA((6,)),
         ],
         28,
         "near_projection",
     )
     rows = token_count // 2
-    normed_shape = jax.ShapeDtypeStruct((token_count, group_width), jnp.bfloat16)
+    normed_shape = jax.ShapeDtypeStruct((token_count, far_width), jnp.bfloat16)
 
     def part_shape(part_columns):
         return jax.ShapeDtypeStruct((rows, part_columns), jnp.bfloat16)
 
     first_columns = columns // 2
-    away, stay, far_normed = project(
+    away, stay, far_normed, near_scale = project(
         far_kernel,
         gain,
         far_weight,
         pltpu.VMEM,
-        [near_partial] + pieces[near:],
-        [part_shape(first_columns)] * 2 + [normed_shape],
+        [near_partial, near_squares] + pieces[near:] + pieces[near - 1 : near],
+        [part_shape(first_columns)] * 2 + [normed_shape, row_shape],
         [],
         8,
         "far_projection",
@@ -727,7 +755,7 @@
         far_normed,
         far_weight,
         pltpu.VMEM,
-        [near_partial],
+        [near_partial, near_scale],
         [part_shape(columns - first_columns)] * 2,
         [],
         8,

time: 109 us -> 109 us (level); the launches traced: 109 us -> 107 us
  waiting for transfers between devices: 53.9 us -> 48.5 us
  starting transfers between devices: 25.7 us -> 28.4 us
  Pallas kernels: 22.8 us -> 24.1 us
    ppermute x18, waiting for transfers between devices: 41.9 us -> 37.4 us  [turned(): return lax.ppermute(value, 'ctx', [(i, i ^ turn) for i in range(ctx_count)])]
    ppermute x18, starting transfers between devices: 23.4 us -> 25.2 us  [turned(): return lax.ppermute(value, 'ctx', [(i, i ^ turn) for i in range(ctx_count)])]
    pallas_call x3, Pallas kernels: 10.3 us -> 11.6 us  [project(): pl.pallas_call(kernel, in_specs=[smem, vmem, pl.BlockSpec(memory_space=we...]
  transfers between devices with their start and end apart: 22 -> 22, of which waited for: 15 -> 13; matrix products, arithmetic and copies ran while one was open for 3% -> 3% of each run, Pallas kernels for 15% -> 16%
where the time goes in v7:
time: 109 us; the launch traced here: 107 us
  waiting for transfers between devices  48.5 us (44%)
  starting transfers between devices  28.4 us (26%)
  Pallas kernels  24.1 us (22%)
  local copies, waits for them, and re-layouts  3.57 us (3%)
  other arithmetic  2.27 us (2%)
    ppermute x18, waiting for transfers between devices, turned(): return lax.ppermute(value, 'ctx', [(i, i ^ turn) for i in range(ctx_count)])  37.4 us
    ppermute x18, starting transfers between devices, turned(): return lax.ppermute(value, 'ctx', [(i, i ^ turn) for i in range(ctx_count)])  25.2 us
    pallas_call x3, Pallas kernels, project(): pl.pallas_call(kernel, in_specs=[smem, vmem, pl.BlockSpec(memory_space=we...  11.6 us
    ppermute x4, waiting for transfers between devices, joined(): came = lax.ppermute(sent, 'tp', [(i, i ^ turn) for i in range(tp_count)])  11.2 us
    pallas_call x1, Pallas kernels, head_split(): pl.pallas_call(functools.partial(mixing_kernel, heads, group_heads, per_d...  8.14 us
    pallas_call x1, Pallas kernels, head_split(): pl.pallas_call(functools.partial(scan_kernel, heads, per_dev, turns), in_...  4.38 us
    ppermute x4, starting transfers between devices, joined(): came = lax.ppermute(sent, 'tp', [(i, i ^ turn) for i in range(tp_count)])  3.15 us
  transfers between devices with their start and end apart: 22, of which 13 were waited for; matrix products, arithmetic and copies ran while one was open for 3% of the time, Pallas kernels for 16%

profile of v7, /device:TPU:16, one launch (start us, length us, event | category | flops | bytes accessed | tf_op | source)
XLA Modules:
  0.0 107.2 jit_solution(1012194639527665535)
XLA Ops:
  0.0 0.7 dynamic-slice_bitcast_fusion.17
  0.7 1.0 constant_dynamic-slice_fusion.2
  1.7 0.1 collective-permute-start.7
  1.9 1.8 %dynamic-slice_bitcast_fusion = (bf16[1,256,256]{2,1,0:T(8,128)(2,1)S(1)}, bf16[1,256,256]{2,1,0:T(8,128)(2,1)S(1)}, bf16[1,256,256]{2,1,0:T(8,128)(2,1)S(1)}, b...) fusion(bf16[256,2048]{1,0:T(8,128)(2,1)} %param.16, ...), kind=kLoop, calls=%fused_computation.16 | loop fusion | bytes 4194336 | tf_op jit(solution)/shard_map/stack | solution.py:616
  3.7 0.7 pad_maximum_fusion.7
  4.4 1.8 %collective-permute-start.4 = (bf16[2,256,256]{2,1,0:T(8,128)(2,1)}, bf16[2,256,256]{2,1,0:T(8,128)(2,1)S(1)}, u32[]{:S(2)}, u32[]{:S(2)}) collective-permute-start(bf16[2,256,256]{2,1,0:T(8,128)(2,1)} %pad_maximum_fusion.7), channel_id=1, source_target_pairs={{0,8},{4,12},{8,0},{12,4},{16,24},{20,28},{24,16},{28,20},{1,9},{5... | collective-permute-start | bytes 786440 | tf_op jit(solution)/shard_map/ppermute | solution.py:606
  6.3 3.6 %collective-permute-start.5 = (bf16[2,256,256]{2,1,0:T(8,128)(2,1)S(1)}, bf16[2,256,256]{2,1,0:T(8,128)(2,1)S(1)}, u32[]{:S(2)}, u32[]{:S(2)}) collective-permute-start(bf16[2,256,256]{2,1,0:T(8,128)(2,1)S(1)} %pad_maximum_fusion.8), channel_id=1, source_target_pairs={{0,20},{4,16},{8,28},{12,24},{16,4},{20,0},{24,12},{28,8},{1,21},{... | collective-permute-start | bytes 786440 | tf_op jit(solution)/shard_map/ppermute | solution.py:606
  10.1 3.7 %collective-permute-start.10 = (bf16[2,272,256]{2,1,0:T(8,128)(2,1)S(1)}, bf16[2,272,256]{2,1,0:T(8,128)(2,1)S(1)}, u32[]{:S(2)}, u32[]{:S(2)}) collective-permute-start(bf16[2,272,256]{2,1,0:T(8,128)(2,1)S(1)} %pad_maximum_fusion.1.refs_0_), channel_id=1, source_target_pairs={{0,12},{4,8},{8,4},{12,0},{16,28},{20,24},{24,20},{28,16},{1,13},{... | collective-permute-start | bytes 835592 | tf_op jit(solution)/shard_map/ppermute | solution.py:606
  13.8 0.5 collective-permute-start.8
  14.3 0.1 collective-permute-start.9
  14.5 6.4 %collective-permute-done.4.refs_5_ = bf16[2,256,256]{2,1,0:T(8,128)(2,1)S(1)} collective-permute-done((bf16[2,256,256]{2,1,0:T(8,128)(2,1)}, bf16[2,256,256]{2,1,0:T(8,128)(2,1)S(1)}, u32[]{:S(2)}, u32[]{:S(2)}) %collective-permute-start.4) | collective-permute-done | bytes 262176 | tf_op jit(solution)/shard_map/ppermute | solution.py:606
  20.9 3.3 %collective-permute-done.5.refs_6_ = bf16[2,256,256]{2,1,0:T(8,128)(2,1)S(1)} collective-permute-done((bf16[2,256,256]{2,1,0:T(8,128)(2,1)S(1)}, bf16[2,256,256]{2,1,0:T(8,128)(2,1)S(1)}, u32[]{:S(2)}, u32[]{:S(2)}) %collective-permute-start.5) | collective-permute-done | bytes 262176 | tf_op jit(solution)/shard_map/ppermute | solution.py:606
  24.2 0.7 collective-permute-start.3
  24.9 4.0 %collective-permute-done.10.refs_3_ = bf16[2,272,256]{2,1,0:T(8,128)(2,1)S(1)} collective-permute-done((bf16[2,272,256]{2,1,0:T(8,128)(2,1)S(1)}, bf16[2,272,256]{2,1,0:T(8,128)(2,1)S(1)}, u32[]{:S(2)}, u32[]{:S(2)}) %collective-permute-start.10) | collective-permute-done | bytes 278560 | tf_op jit(solution)/shard_map/ppermute | solution.py:606
  28.9 0.5 collective-permute-start.2
  29.4 6.6 %collective-permute-done.8.refs_1_ = bf16[2,272,256]{2,1,0:T(8,128)(2,1)S(1)} collective-permute-done((bf16[2,272,256]{2,1,0:T(8,128)(2,1)S(1)}, bf16[2,272,256]{2,1,0:T(8,128)(2,1)S(1)}, u32[]{:S(2)}, u32[]{:S(2)}) %collective-permute-start.8) | collective-permute-done | bytes 278560 | tf_op jit(solution)/shard_map/ppermute | solution.py:606
  36.0 4.7 %collective-permute-done.9.refs_2_ = bf16[2,272,256]{2,1,0:T(8,128)(2,1)S(1)} collective-permute-done((bf16[2,272,256]{2,1,0:T(8,128)(2,1)S(1)}, bf16[2,272,256]{2,1,0:T(8,128)(2,1)S(1)}, u32[]{:S(2)}, u32[]{:S(2)}) %collective-permute-start.9) | collective-permute-done | bytes 278560 | tf_op jit(solution)/shard_map/ppermute | solution.py:606
  40.8 1.8 %collective-permute-start = (bf16[2,256,256]{2,1,0:T(8,128)(2,1)S(1)}, bf16[2,256,256]{2,1,0:T(8,128)(2,1)S(1)}, u32[]{:S(2)}, u32[]{:S(2)}) collective-permute-start(bf16[2,256,256]{2,1,0:T(8,128)(2,1)S(1)} %pad_maximum_fusion.3), channel_id=1, source_target_pairs={{0,4},{4,0},{8,12},{12,8},{16,20},{20,16},{24,28},{28,24},{1,5},{5... | collective-permute-start | bytes 786440 | tf_op jit(solution)/shard_map/ppermute | solution.py:606
  42.5 0.1 pad_add_fusion.me_ref.place_ref
  42.7 8.1 %mixing.1 = (bf16[16,128,512]{2,1,0:T(8,128)(2,1)S(1)}, bf16[16,128,128]{2,1,0:T(8,128)(2,1)S(1)}, bf16[16,128,128]{2,1,0:T(8,128)(2,1)S(1)}, f32[16,128,256]{2,...) custom-call(s32[2]{0:T(128)S(1)} %pad_add_fusion.me_ref.place_ref, ...), custom_call_target="tpu_custom_call" | custom-call | flops 20000000 | bytes 20000000 | tf_op jit(solution)/shard_map/mixing/pallas_call | solution.py:651
  50.8 2.6 %collective-permute-done.3.refs_4_ = bf16[2,256,256]{2,1,0:T(8,128)(2,1)S(1)} collective-permute-done((bf16[2,256,256]{2,1,0:T(8,128)(2,1)S(1)}, bf16[2,256,256]{2,1,0:T(8,128)(2,1)S(1)}, u32[]{:S(2)}, u32[]{:S(2)}) %collective-permute-start.3) | collective-permute-done | bytes 262176 | tf_op jit(solution)/shard_map/ppermute | solution.py:606
  53.4 2.5 %collective-permute-done.1.refs_2_ = bf16[2,256,256]{2,1,0:T(8,128)(2,1)S(1)} collective-permute-done((bf16[2,256,256]{2,1,0:T(8,128)(2,1)S(1)}, bf16[2,256,256]{2,1,0:T(8,128)(2,1)S(1)}, u32[]{:S(2)}, u32[]{:S(2)}) %collective-permute-start.1) | collective-permute-done | bytes 262176 | tf_op jit(solution)/shard_map/ppermute | solution.py:606
  56.0 4.4 %scan.1 = (bf16[256,256]{1,0:T(8,128)(2,1)S(1)}, bf16[256,256]{1,0:T(8,128)(2,1)S(1)}, bf16[256,256]{1,0:T(8,128)(2,1)S(1)}, bf16[256,256]{1,0:T(8,128)(2,1)S(1)...) custom-call(s32[2]{0:T(128)S(1)} %pad_add_fusion.me_ref.place_ref, ...), custom_call_target="tpu_custom_call" | custom-call | flops 600000000 | bytes 14000000 | tf_op jit(solution)/shard_map/scan/pallas_call | solution.py:671
  60.3 1.5 %collective-permute-start.11 = (bf16[256,256]{1,0:T(8,128)(2,1)S(1)}, bf16[256,256]{1,0:T(8,128)(2,1)S(1)}, u32[]{:S(2)}, u32[]{:S(2)}) collective-permute-start(bf16[256,256]{1,0:T(8,128)(2,1)S(1)} %get-tuple-element.37), channel_id=1, source_target_pairs={{0,4},{4,0},{8,12},{12,8},{16,20},{20,16},{24,28},{28,24},{1,5},{5... | collective-permute-start | bytes 393224 | tf_op jit(solution)/shard_map/ppermute | solution.py:606
  61.8 2.8 %collective-permute-start.12 = (bf16[256,256]{1,0:T(8,128)(2,1)S(1)}, bf16[256,256]{1,0:T(8,128)(2,1)S(1)}, u32[]{:S(2)}, u32[]{:S(2)}) collective-permute-start(bf16[256,256]{1,0:T(8,128)(2,1)S(1)} %get-tuple-element.38), channel_id=1, source_target_pairs={{0,8},{4,12},{8,0},{12,4},{16,24},{20,28},{24,16},{28,20},{1,9},{5... | collective-permute-start | bytes 393224 | tf_op jit(solution)/shard_map/ppermute | solution.py:606
  64.6 0.5 collective-permute-start.13
  65.1 2.9 %collective-permute-start.14 = (bf16[256,256]{1,0:T(8,128)(2,1)S(1)}, bf16[256,256]{1,0:T(8,128)(2,1)S(1)}, u32[]{:S(2)}, u32[]{:S(2)}) collective-permute-start(bf16[256,256]{1,0:T(8,128)(2,1)S(1)} %get-tuple-element.43), channel_id=1, source_target_pairs={{0,20},{4,16},{8,28},{12,24},{16,4},{20,0},{24,12},{28,8},{1,21},{... | collective-permute-start | bytes 393224 | tf_op jit(solution)/shard_map/ppermute | solution.py:606
  68.0 0.8 collective-permute-start.15
  68.7 1.7 %collective-permute-start.16 = (bf16[256,256]{1,0:T(8,128)(2,1)S(1)}, bf16[256,256]{1,0:T(8,128)(2,1)S(1)}, u32[]{:S(2)}, u32[]{:S(2)}) collective-permute-start(bf16[256,256]{1,0:T(8,128)(2,1)S(1)} %get-tuple-element.45), channel_id=1, source_target_pairs={{0,28},{4,24},{8,20},{12,16},{16,12},{20,8},{24,4},{28,0},{1,29},{... | collective-permute-start | bytes 393224 | tf_op jit(solution)/shard_map/ppermute | solution.py:606
  70.5 2.3 %collective-permute-start.17 = (bf16[256,256]{1,0:T(8,128)(2,1)S(1)}, bf16[256,256]{1,0:T(8,128)(2,1)S(1)}, u32[]{:S(2)}, u32[]{:S(2)}) collective-permute-start(bf16[256,256]{1,0:T(8,128)(2,1)S(1)} %get-tuple-element.46), channel_id=1, source_target_pairs={{0,12},{4,8},{8,4},{12,0},{16,28},{20,24},{24,20},{28,16},{1,13},{... | collective-permute-start | bytes 393224 | tf_op jit(solution)/shard_map/ppermute | solution.py:606
  72.8 7.2 %near_projection.1 = (f32[256,4096]{1,0:T(8,128)S(1)}, f32[256,128]{1,0:T(8,128)S(1)}, bf16[1280,4096]{1,0:T(8,128)(2,1)S(1)}) custom-call(s32[2]{0:T(128)S(1)} %pad_add_fusion.me_ref.place_ref, f32[8,256]{1,0:T(8,128)S(1)} %reshape.6.gain_ref, bf16[2,1024,4096]{2,1,0:T(8,128)(2,1)} %bitcast.42, bf16[256,256]{1,0:T(8,128)(2,1)S(1)} %get-tuple-element.36.refs_0_, ...), custom_call_target="tpu_custom_call" | custom-call | flops 2147483648 | bytes 8388608 | tf_op jit(solution)/shard_map/near_projection/pallas_call | solution.py:699
  80.0 1.2 %collective-permute-done.14.refs_1_ = bf16[256,256]{1,0:T(8,128)(2,1)S(1)} collective-permute-done((bf16[256,256]{1,0:T(8,128)(2,1)S(1)}, bf16[256,256]{1,0:T(8,128)(2,1)S(1)}, u32[]{:S(2)}, u32[]{:S(2)}) %collective-permute-start.14) | collective-permute-done | bytes 131104 | tf_op jit(solution)/shard_map/ppermute | solution.py:606
  81.2 3.9 %collective-permute-done.15.refs_2_ = bf16[256,256]{1,0:T(8,128)(2,1)S(1)} collective-permute-done((bf16[256,256]{1,0:T(8,128)(2,1)S(1)}, bf16[256,256]{1,0:T(8,128)(2,1)S(1)}, u32[]{:S(2)}, u32[]{:S(2)}) %collective-permute-start.15) | collective-permute-done | bytes 131104 | tf_op jit(solution)/shard_map/ppermute | solution.py:606
  85.1 2.1 %collective-permute-done.16.refs_3_ = bf16[256,256]{1,0:T(8,128)(2,1)S(1)} collective-permute-done((bf16[256,256]{1,0:T(8,128)(2,1)S(1)}, bf16[256,256]{1,0:T(8,128)(2,1)S(1)}, u32[]{:S(2)}, u32[]{:S(2)}) %collective-permute-start.16) | collective-permute-done | bytes 131104 | tf_op jit(solution)/shard_map/ppermute | solution.py:606
  87.2 2.3 %far_projection.1 = (bf16[128,2048]{1,0:T(8,128)(2,1)S(1)}, bf16[128,2048]{1,0:T(8,128)(2,1)S(1)}, bf16[256,1280]{1,0:T(8,128)(2,1)S(1)}, f32[256,128]{1,0:T(8,128)S(1)}) custom-call(s32[2]{0:T(128)S(1)} %pad_add_fusion.me_ref.place_ref, f32[8,256]{1,0:T(8,128)S(1)} %reshape.6.gain_ref, bf16[1280,4096]{1,0:T(8,128)(2,1)S(1)} %get-tuple-element.39.weight_ref, ...), custom_call_target="tpu_custom_call" | custom-call | flops 2147483648 | bytes 8388608 | tf_op jit(solution)/shard_map/far_projection/pallas_call | solution.py:699
  89.5 0.1 collective-permute-start.18
  89.6 2.1 %rest_projection.1 = (bf16[128,2048]{1,0:T(8,128)(2,1)S(1)}, bf16[128,2048]{1,0:T(8,128)(2,1)S(1)}) custom-call(s32[2]{0:T(128)S(1)} %pad_add_fusion.me_ref.place_ref, bf16[256,1280]{1,0:T(8,128)(2,1)S(1)} %get-tuple-element.49.normed_ref, bf16[1280,4096]{1,0:T(8,128)(2,1)S(1)} %get-tuple-element.39.weight_ref, f32[256,4096]{1,0:T(8,128)S(1)} %get-tuple-element.40.near_ref, ...), custom_call_target="tpu_custom_call" | custom-call | flops 2147483648 | bytes 8388608 | tf_op jit(solution)/shard_map/rest_projection/pallas_call | solution.py:699
  91.6 0.6 collective-permute-start.20
  92.2 0.1 add_convert_fusion.1
  92.4 1.3 %collective-permute-start.19 = (bf16[64,2048]{1,0:T(8,128)(2,1)S(1)}, bf16[64,2048]{1,0:T(8,128)(2,1)S(1)}, u32[]{:S(2)}, u32[]{:S(2)}) collective-permute-start(bf16[64,2048]{1,0:T(8,128)(2,1)S(1)} %slice.17), channel_id=1, source_target_pairs={{0,2},{1,3},{2,0},{3,1},{4,6},{5,7},{6,4},{7,5},{8,10},{9,11},{10,... | collective-permute-start | bytes 786440 | tf_op jit(solution)/shard_map/ppermute | solution.py:766
  93.6 0.1 collective-permute-done.20
  93.7 0.1 add_convert_fusion
  93.9 1.3 %collective-permute-start.21 = (bf16[64,2048]{1,0:T(8,128)(2,1)S(1)}, bf16[64,2048]{1,0:T(8,128)(2,1)S(1)}, u32[]{:S(2)}, u32[]{:S(2)}) collective-permute-start(bf16[64,2048]{1,0:T(8,128)(2,1)S(1)} %slice.19), channel_id=1, source_target_pairs={{0,2},{1,3},{2,0},{3,1},{4,6},{5,7},{6,4},{7,5},{8,10},{9,11},{10,... | collective-permute-start | bytes 786440 | tf_op jit(solution)/shard_map/ppermute | solution.py:766
  95.2 6.4 %collective-permute-done.19 = bf16[64,2048]{1,0:T(8,128)(2,1)S(1)} collective-permute-done((bf16[64,2048]{1,0:T(8,128)(2,1)S(1)}, bf16[64,2048]{1,0:T(8,128)(2,1)S(1)}, u32[]{:S(2)}, u32[]{:S(2)}) %collective-permute-start.19) | collective-permute-done | bytes 262176 | tf_op jit(solution)/shard_map/ppermute | solution.py:766
  101.6 0.1 add_convert_fusion.3
  101.7 4.6 %collective-permute-done.21 = bf16[64,2048]{1,0:T(8,128)(2,1)S(1)} collective-permute-done((bf16[64,2048]{1,0:T(8,128)(2,1)S(1)}, bf16[64,2048]{1,0:T(8,128)(2,1)S(1)}, u32[]{:S(2)}, u32[]{:S(2)}) %collective-permute-start.21) | collective-permute-done | bytes 262176 | tf_op jit(solution)/shard_map/ppermute | solution.py:766
  106.3 0.1 add_convert_fusion.2
  106.4 0.8 pad_maximum_fusion
  (44 shorter events, 0.4 us)
Async XLA Ops:
  0.0 14.4 %copy-start = (f32[4,2048]{1,0:T(4,128)S(1)}, f32[4,2048]{1,0:T(4,128)}, u32[]{:S(2)}) copy-start(f32[4,2048]{1,0:T(4,128)} %param.22) | copy-start | bytes 98308
  1.7 8.3 %collective-permute-start.7 = (bf16[272,256]{1,0:T(8,128)(2,1)S(1)}, bf16[272,256]{1,0:T(8,128)(2,1)S(1)}, u32[]{:S(2)}, u32[]{:S(2)}) collective-permute-start(bf16[272,256]{1,0:T(8,128)(2,1)S(1)} %pad_maximum_fusion.10), channel_id=1, source_target_pairs={{0,16},{4,20},{8,24},{12,28},{16,0},{20,4},{24,8},{28,12},{1,17},{... | collective-permute-start | bytes 417800 | tf_op jit(solution)/shard_map/ppermute | solution.py:606
  1.8 40.8 %copy-start.7 = (f32[4,256]{1,0:T(4,128)S(1)}, f32[4,256]{1,0:T(4,128)}, u32[]{:S(2)}) copy-start(f32[4,256]{1,0:T(4,128)} %param.24) | copy-start | bytes 12292
  1.8 40.8 %copy-start.8 = (f32[4,256]{1,0:T(4,128)S(1)}, f32[4,256]{1,0:T(4,128)}, u32[]{:S(2)}) copy-start(f32[4,256]{1,0:T(4,128)} %param.23) | copy-start | bytes 12292
  1.9 40.8 %copy-start.1 = (s32[32]{0:T(128)S(1)}, s32[32]{0:T(128)}, u32[]{:S(2)}) copy-start(s32[32]{0:T(128)} %order_ref.3) | copy-start | bytes 388
  1.9 40.8 %copy-start.3 = (s32[16]{0:T(128)S(1)}, s32[16]{0:T(128)}, u32[]{:S(2)}) copy-start(s32[16]{0:T(128)} %lengths_ref.1) | copy-start | bytes 196
  1.9 40.8 %copy-start.4 = (f32[32]{0:T(128)S(1)}, f32[32]{0:T(128)}, u32[]{:S(2)}) copy-start(f32[32]{0:T(128)} %bias_ref.1) | copy-start | bytes 388
  1.9 40.8 %copy-start.5 = (f32[32]{0:T(128)S(1)}, f32[32]{0:T(128)}, u32[]{:S(2)}) copy-start(f32[32]{0:T(128)} %log_ref.1) | copy-start | bytes 388
  4.4 51.5 %copy-start.2 = (f32[32]{0:T(128)S(1)}, f32[32]{0:T(128)}, u32[]{:S(2)}) copy-start(f32[32]{0:T(128)} %skip_ref.1) | copy-start | bytes 388
  4.4 16.5 %collective-permute-start.4 = (bf16[2,256,256]{2,1,0:T(8,128)(2,1)}, bf16[2,256,256]{2,1,0:T(8,128)(2,1)S(1)}, u32[]{:S(2)}, u32[]{:S(2)}) collective-permute-start(bf16[2,256,256]{2,1,0:T(8,128)(2,1)} %pad_maximum_fusion.7), channel_id=1, source_target_pairs={{0,8},{4,12},{8,0},{12,4},{16,24},{20,28},{24,16},{28,20},{1,9},{5... | collective-permute-start | bytes 786440 | tf_op jit(solution)/shard_map/ppermute | solution.py:606
  6.3 17.9 %collective-permute-start.5 = (bf16[2,256,256]{2,1,0:T(8,128)(2,1)S(1)}, bf16[2,256,256]{2,1,0:T(8,128)(2,1)S(1)}, u32[]{:S(2)}, u32[]{:S(2)}) collective-permute-start(bf16[2,256,256]{2,1,0:T(8,128)(2,1)S(1)} %pad_maximum_fusion.8), channel_id=1, source_target_pairs={{0,20},{4,16},{8,28},{12,24},{16,4},{20,0},{24,12},{28,8},{1,21},{... | collective-permute-start | bytes 786440 | tf_op jit(solution)/shard_map/ppermute | solution.py:606
  10.1 18.8 %collective-permute-start.10 = (bf16[2,272,256]{2,1,0:T(8,128)(2,1)S(1)}, bf16[2,272,256]{2,1,0:T(8,128)(2,1)S(1)}, u32[]{:S(2)}, u32[]{:S(2)}) collective-permute-start(bf16[2,272,256]{2,1,0:T(8,128)(2,1)S(1)} %pad_maximum_fusion.1.refs_0_), channel_id=1, source_target_pairs={{0,12},{4,8},{8,4},{12,0},{16,28},{20,24},{24,20},{28,16},{1,13},{... | collective-permute-start | bytes 835592 | tf_op jit(solution)/shard_map/ppermute | solution.py:606
  13.8 22.2 %collective-permute-start.8 = (bf16[2,272,256]{2,1,0:T(8,128)(2,1)S(1)}, bf16[2,272,256]{2,1,0:T(8,128)(2,1)S(1)}, u32[]{:S(2)}, u32[]{:S(2)}) collective-permute-start(bf16[2,272,256]{2,1,0:T(8,128)(2,1)S(1)} %pad_maximum_fusion.1.refs_0_), channel_id=1, source_target_pairs={{0,4},{4,0},{8,12},{12,8},{16,20},{20,16},{24,28},{28,24},{1,5},{5... | collective-permute-start | bytes 835592 | tf_op jit(solution)/shard_map/ppermute | solution.py:606
  14.3 26.5 %collective-permute-start.9 = (bf16[2,272,256]{2,1,0:T(8,128)(2,1)S(1)}, bf16[2,272,256]{2,1,0:T(8,128)(2,1)S(1)}, u32[]{:S(2)}, u32[]{:S(2)}) collective-permute-start(bf16[2,272,256]{2,1,0:T(8,128)(2,1)S(1)} %pad_maximum_fusion.1.refs_0_), channel_id=1, source_target_pairs={{0,8},{4,12},{8,0},{12,4},{16,24},{20,28},{24,16},{28,20},{1,9},{5... | collective-permute-start | bytes 835592 | tf_op jit(solution)/shard_map/ppermute | solution.py:606
  20.9 29.9 %collective-permute-start.6 = (bf16[2,256,256]{2,1,0:T(8,128)(2,1)S(1)}, bf16[2,256,256]{2,1,0:T(8,128)(2,1)S(1)}, u32[]{:S(2)}, u32[]{:S(2)}) collective-permute-start(bf16[2,256,256]{2,1,0:T(8,128)(2,1)S(1)} %pad_maximum_fusion.9), channel_id=1, source_target_pairs={{0,24},{4,28},{8,16},{12,20},{16,8},{20,12},{24,0},{28,4},{1,25},{... | collective-permute-start | bytes 786440 | tf_op jit(solution)/shard_map/ppermute | solution.py:606
  24.2 29.2 %collective-permute-start.3 = (bf16[2,256,256]{2,1,0:T(8,128)(2,1)S(1)}, bf16[2,256,256]{2,1,0:T(8,128)(2,1)S(1)}, u32[]{:S(2)}, u32[]{:S(2)}) collective-permute-start(bf16[2,256,256]{2,1,0:T(8,128)(2,1)S(1)} %pad_maximum_fusion.6), channel_id=1, source_target_pairs={{0,12},{4,8},{8,4},{12,0},{16,28},{20,24},{24,20},{28,16},{1,13},{... | collective-permute-start | bytes 786440 | tf_op jit(solution)/shard_map/ppermute | solution.py:606
  28.9 24.5 %collective-permute-start.2 = (bf16[2,256,256]{2,1,0:T(8,128)(2,1)S(1)}, bf16[2,256,256]{2,1,0:T(8,128)(2,1)S(1)}, u32[]{:S(2)}, u32[]{:S(2)}) collective-permute-start(bf16[2,256,256]{2,1,0:T(8,128)(2,1)S(1)} %pad_maximum_fusion.5), channel_id=1, source_target_pairs={{0,28},{4,24},{8,20},{12,16},{16,12},{20,8},{24,4},{28,0},{1,29},{... | collective-permute-start | bytes 786440 | tf_op jit(solution)/shard_map/ppermute | solution.py:606
  36.0 19.9 %collective-permute-start.1 = (bf16[2,256,256]{2,1,0:T(8,128)(2,1)S(1)}, bf16[2,256,256]{2,1,0:T(8,128)(2,1)S(1)}, u32[]{:S(2)}, u32[]{:S(2)}) collective-permute-start(bf16[2,256,256]{2,1,0:T(8,128)(2,1)S(1)} %pad_maximum_fusion.4), channel_id=1, source_target_pairs={{0,16},{4,20},{8,24},{12,28},{16,0},{20,4},{24,8},{28,12},{1,17},{... | collective-permute-start | bytes 786440 | tf_op jit(solution)/shard_map/ppermute | solution.py:606
  40.8 15.2 %collective-permute-start = (bf16[2,256,256]{2,1,0:T(8,128)(2,1)S(1)}, bf16[2,256,256]{2,1,0:T(8,128)(2,1)S(1)}, u32[]{:S(2)}, u32[]{:S(2)}) collective-permute-start(bf16[2,256,256]{2,1,0:T(8,128)(2,1)S(1)} %pad_maximum_fusion.3), channel_id=1, source_target_pairs={{0,4},{4,0},{8,12},{12,8},{16,20},{20,16},{24,28},{28,24},{1,5},{5... | collective-permute-start | bytes 786440 | tf_op jit(solution)/shard_map/ppermute | solution.py:606
  55.9 8.6 %copy-start.6 = (f32[2048]{0:T(1024)S(1)}, f32[2048]{0:T(1024)}, u32[]{:S(2)}) copy-start(f32[2048]{0:T(1024)} %param.28) | copy-start | bytes 24580
  60.3 8.4 %collective-permute-start.11 = (bf16[256,256]{1,0:T(8,128)(2,1)S(1)}, bf16[256,256]{1,0:T(8,128)(2,1)S(1)}, u32[]{:S(2)}, u32[]{:S(2)}) collective-permute-start(bf16[256,256]{1,0:T(8,128)(2,1)S(1)} %get-tuple-element.37), channel_id=1, source_target_pairs={{0,4},{4,0},{8,12},{12,8},{16,20},{20,16},{24,28},{28,24},{1,5},{5... | collective-permute-start | bytes 393224 | tf_op jit(solution)/shard_map/ppermute | solution.py:606
  61.8 8.6 %collective-permute-start.12 = (bf16[256,256]{1,0:T(8,128)(2,1)S(1)}, bf16[256,256]{1,0:T(8,128)(2,1)S(1)}, u32[]{:S(2)}, u32[]{:S(2)}) collective-permute-start(bf16[256,256]{1,0:T(8,128)(2,1)S(1)} %get-tuple-element.38), channel_id=1, source_target_pairs={{0,8},{4,12},{8,0},{12,4},{16,24},{20,28},{24,16},{28,20},{1,9},{5... | collective-permute-start | bytes 393224 | tf_op jit(solution)/shard_map/ppermute | solution.py:606
  64.6 15.4 %collective-permute-start.13 = (bf16[256,256]{1,0:T(8,128)(2,1)S(1)}, bf16[256,256]{1,0:T(8,128)(2,1)S(1)}, u32[]{:S(2)}, u32[]{:S(2)}) collective-permute-start(bf16[256,256]{1,0:T(8,128)(2,1)S(1)} %get-tuple-element.42), channel_id=1, source_target_pairs={{0,16},{4,20},{8,24},{12,28},{16,0},{20,4},{24,8},{28,12},{1,17},{... | collective-permute-start | bytes 393224 | tf_op jit(solution)/shard_map/ppermute | solution.py:606
  65.1 16.1 %collective-permute-start.14 = (bf16[256,256]{1,0:T(8,128)(2,1)S(1)}, bf16[256,256]{1,0:T(8,128)(2,1)S(1)}, u32[]{:S(2)}, u32[]{:S(2)}) collective-permute-start(bf16[256,256]{1,0:T(8,128)(2,1)S(1)} %get-tuple-element.43), channel_id=1, source_target_pairs={{0,20},{4,16},{8,28},{12,24},{16,4},{20,0},{24,12},{28,8},{1,21},{... | collective-permute-start | bytes 393224 | tf_op jit(solution)/shard_map/ppermute | solution.py:606
  68.0 17.1 %collective-permute-start.15 = (bf16[256,256]{1,0:T(8,128)(2,1)S(1)}, bf16[256,256]{1,0:T(8,128)(2,1)S(1)}, u32[]{:S(2)}, u32[]{:S(2)}) collective-permute-start(bf16[256,256]{1,0:T(8,128)(2,1)S(1)} %get-tuple-element.44), channel_id=1, source_target_pairs={{0,24},{4,28},{8,16},{12,20},{16,8},{20,12},{24,0},{28,4},{1,25},{... | collective-permute-start | bytes 393224 | tf_op jit(solution)/shard_map/ppermute | solution.py:606
  68.7 18.4 %collective-permute-start.16 = (bf16[256,256]{1,0:T(8,128)(2,1)S(1)}, bf16[256,256]{1,0:T(8,128)(2,1)S(1)}, u32[]{:S(2)}, u32[]{:S(2)}) collective-permute-start(bf16[256,256]{1,0:T(8,128)(2,1)S(1)} %get-tuple-element.45), channel_id=1, source_target_pairs={{0,28},{4,24},{8,20},{12,16},{16,12},{20,8},{24,4},{28,0},{1,29},{... | collective-permute-start | bytes 393224 | tf_op jit(solution)/shard_map/ppermute | solution.py:606
  70.5 16.7 %collective-permute-start.17 = (bf16[256,256]{1,0:T(8,128)(2,1)S(1)}, bf16[256,256]{1,0:T(8,128)(2,1)S(1)}, u32[]{:S(2)}, u32[]{:S(2)}) collective-permute-start(bf16[256,256]{1,0:T(8,128)(2,1)S(1)} %get-tuple-element.46), channel_id=1, source_target_pairs={{0,12},{4,8},{8,4},{12,0},{16,28},{20,24},{24,20},{28,16},{1,13},{... | collective-permute-start | bytes 393224 | tf_op jit(solution)/shard_map/ppermute | solution.py:606
  89.5 2.7 %collective-permute-start.18 = (bf16[128,2048]{1,0:T(8,128)(2,1)S(1)}, bf16[128,2048]{1,0:T(8,128)(2,1)S(1)}, u32[]{:S(2)}, u32[]{:S(2)}) collective-permute-start(bf16[128,2048]{1,0:T(8,128)(2,1)S(1)} %get-tuple-element.48), channel_id=1, source_target_pairs={{0,1},{1,0},{2,3},{3,2},{4,5},{5,4},{6,7},{7,6},{8,9},{9,8},{10,11... | collective-permute-start | bytes 1572872 | tf_op jit(solution)/shard_map/ppermute | solution.py:766
  91.6 2.1 %collective-permute-start.20 = (bf16[128,2048]{1,0:T(8,128)(2,1)S(1)}, bf16[128,2048]{1,0:T(8,128)(2,1)S(1)}, u32[]{:S(2)}, u32[]{:S(2)}) collective-permute-start(bf16[128,2048]{1,0:T(8,128)(2,1)S(1)} %get-tuple-element.52), channel_id=1, source_target_pairs={{0,1},{1,0},{2,3},{3,2},{4,5},{5,4},{6,7},{7,6},{8,9},{9,8},{10,11... | collective-permute-start | bytes 1572872 | tf_op jit(solution)/shard_map/ppermute | solution.py:766
  92.4 9.2 %collective-permute-start.19 = (bf16[64,2048]{1,0:T(8,128)(2,1)S(1)}, bf16[64,2048]{1,0:T(8,128)(2,1)S(1)}, u32[]{:S(2)}, u32[]{:S(2)}) collective-permute-start(bf16[64,2048]{1,0:T(8,128)(2,1)S(1)} %slice.17), channel_id=1, source_target_pairs={{0,2},{1,3},{2,0},{3,1},{4,6},{5,7},{6,4},{7,5},{8,10},{9,11},{10,... | collective-permute-start | bytes 786440 | tf_op jit(solution)/shard_map/ppermute | solution.py:766
  93.9 12.4 %collective-permute-start.21 = (bf16[64,2048]{1,0:T(8,128)(2,1)S(1)}, bf16[64,2048]{1,0:T(8,128)(2,1)S(1)}, u32[]{:S(2)}, u32[]{:S(2)}) collective-permute-start(bf16[64,2048]{1,0:T(8,128)(2,1)S(1)} %slice.19), channel_id=1, source_target_pairs={{0,2},{1,3},{2,0},{3,1},{4,6},{5,7},{6,4},{7,5},{8,10},{9,11},{10,... | collective-permute-start | bytes 786440 | tf_op jit(solution)/shard_map/ppermute | solution.py:766
